TPU v7x, 256 devices: a whole 4x4x8 slice. The times are simulated.
256 devices in a mesh: seq: 16 (over y, x), filt: 8 (over z), dp: 2 (over core).
Axes of the slice: x: 4, y: 4, z: 8, core: 2. Of those that a mesh axis runs over, the one named last changes fastest.
Arguments:
- inputs: bfloat16 [2, 4096, 2048], P('dp', 'seq'), may hold values from -6 to 6
- filters: float32 [4096, 16], P(None, 'filt'), may hold values from -0.09375 to 0.09375
- weights: bfloat16 [16, 2048, 1024], P('filt'), may hold values from -0.03125 to 0.03125
- cotangent: bfloat16 [2, 4096, 1024], P('dp', ('seq', 'filt')), may hold values from -0.0625 to 0.0625
Outputs:
- outputs: bfloat16 [2, 4096, 1024], P('dp', ('seq', 'filt'))
- weight_grad: bfloat16 [2048, 16, 1024], P(('seq', 'dp'), 'filt')
All inputs are finite; a program needn't handle non-finite values.
Results may differ from a plain program's by a relative error of at most 0.024.
Values may be sent and summed in bfloat16 or wider, within the bound.
No kernel may reach another device: no remote copies, remote signals or barrier semaphores. Data moves between devices by JAX's collectives and lax.ppermute only.
A program may use at most 128 MiB of HBM per device.

v0:
```python
import jax
import jax.numpy as jnp
from jax import lax
from jax.sharding import PartitionSpec as P


def build_toeplitz(padded, offset, out_rows, in_rows):
    span_len = out_rows + in_rows
    length = padded.shape[0] // 3
    filter_count = padded.shape[1]
    segment = lax.dynamic_slice_in_dim(padded, length + offset - in_rows + 1, span_len - 1, 0)
    backward = jnp.concatenate([segment[::-1], jnp.zeros((1, filter_count), padded.dtype)], axis=0)
    rolled = jnp.roll(backward, -(out_rows - 1), axis=0)
    tiled_rows = jnp.tile(jnp.transpose(rolled), (1, out_rows))[:, : out_rows * (span_len - 1)]
    return tiled_rows.reshape(filter_count, out_rows, span_len - 1)[:, :, :in_rows]


def shards(inputs, filters, weights, cotangent):
    own_rows = inputs[0]
    block_rows = own_rows.shape[0]
    feature_width = own_rows.shape[1]
    length = filters.shape[0]
    filter_count = filters.shape[1]
    blank_lags = jnp.zeros((length, filter_count), jnp.bfloat16)
    padded = jnp.concatenate([blank_lags, filters.astype(jnp.bfloat16), blank_lags], axis=0)
    own_start = lax.axis_index("seq") * block_rows
    zeros_init = jnp.zeros((block_rows, filter_count, feature_width), jnp.float32)
    piece = lax.all_gather(own_rows, "seq", axis=0, tiled=True)
    row_start = jnp.int32(0)
    piece_rows = piece.shape[0]

    def compute(current):
        toeplitz = build_toeplitz(padded, own_start, block_rows, piece_rows)
        return jnp.einsum("kab,bd->akd", toeplitz, piece, preferred_element_type=jnp.float32)

    useful = jnp.logical_and(row_start + piece_rows > 0, row_start < own_start + block_rows)
    running = lax.cond(useful, compute, lambda current: current, zeros_init)
    features = running.astype(jnp.bfloat16)
    summed = lax.psum_scatter(
        jnp.einsum("tkd,kdo->to", features, weights, preferred_element_type=jnp.float32).astype(
            jnp.bfloat16
        ),
        "filt",
        scatter_dimension=0,
        tiled=True,
    )
    outputs = summed[None]
    full_grad = lax.all_gather(cotangent[0], "filt", axis=0, tiled=True)
    weight_grad = lax.psum_scatter(
        jnp.einsum("tkd,to->dko", features, full_grad, preferred_element_type=jnp.float32).astype(
            jnp.bfloat16
        ),
        ("seq", "dp"),
        scatter_dimension=0,
        tiled=True,
    )
    return (outputs, weight_grad)


def solution(mesh):
    in_specs = (
        P("dp", "seq", None),
        P(None, "filt"),
        P("filt", None, None),
        P("dp", ("seq", "filt"), None),
    )
    out_specs = (P("dp", ("seq", "filt"), None), P(("seq", "dp"), "filt", None))
    return jax.shard_map(shards, mesh=mesh, in_specs=in_specs, out_specs=out_specs, check_vma=False)
```

profile of v0, /device:TPU:32, one launch (start us, length us, event | category | flops | bytes accessed | tf_op | source)
XLA Modules:
  0.0 339.1 jit_solution(13084965166544312407)
XLA Ops:
  7.2 0.0 all-gather.4.cloned.1.call-start
  7.2 0.7 all-gather.4.cloned.1.call-update
  7.9 0.0 reduce-scatter.5.cloned.1.call-start
  7.9 0.8 convert_element_type.25
  8.7 28.3 %all-gather.1 = bf16[1,256,1024]{2,1,0:T(8,128)(2,1)S(1)} all-gather(bf16[1,32,1024]{2,1,0:T(8,128)(2,1)} %param.9), channel_id=3, replica_groups=mesh['seq'=16,'filt'=8,'dp'=2] {'filt'}, dimensions={1}, use_global_device_ids=true | all-gather | bytes 589824 | tf_op jit(solution)/shard_map/all_gather | solution.py:48
  37.1 92.3 %all-gather.4.cloned.1.call-done = bf16[1,4096,2048]{2,1,0:T(8,128)(2,1)} async-done(((bf16[1,256,2048]{2,1,0:T(8,128)(2,1)}), bf16[1,4096,2048]{2,1,0:T(8,128)(2,1)}) %all-gather.4.cloned.1.call-update) | async-done | bytes 16777232 | tf_op jit(solution)/shard_map/all_gather | solution.py:28
  129.4 58.0 %conditional.1 = (bf16[256,2,2048]{2,0,1:T(8,128)(2,1)S(1)}) conditional(s32[]{:T(128)} %convert_element_type.24, () %tuple.16, (s32[]{:T(128)}, bf16[12288,2]{0,1:T(2,128)(2,1)S(1)}, bf16[4096,2048]{1,0:T(8,128)(2,1)}) %tuple.29), branch_computations={%region_0.0_spmd, %region_1.2_spmd} | conditional | flops 8591017984 | bytes 63367208 | solution.py:37
  129.4 0.1 constant_dynamic-slice_fusion
  129.5 0.1 constant_dynamic-slice_fusion.1
  129.6 3.1 reverse.2
  132.7 0.1 slice.28
  132.8 0.1 pad_slice_fusion
  132.8 0.2 reverse.1
  133.1 0.1 slice.27
  133.1 0.1 maximum_bitcast_fusion
  133.2 2.4 broadcast_bitcast_fusion
  135.6 8.9 %copy.11 = bf16[1,2,256,4352]{3,1,2,0:T(2,128)(2,1)} copy(bf16[1,2,256,4352]{3,2,1,0:T(8,128)(2,1)} %broadcast_bitcast_fusion) | data formatting | bytes 8912896 | tf_op jit(solution)/shard_map/cond
  144.5 5.4 %slice.18 = bf16[2,1113856]{1,0:T(2,128)(2,1)} slice(bf16[2,1114112]{1,0:T(2,128)(2,1)} %bitcast.31), slice={[0:2], [0:1113856]} | slice | bytes 8910848 | tf_op jit(solution)/shard_map/cond/branch_1_fun/slice | solution.py:14
  149.9 11.8 %reshape.16 = bf16[2227712]{0:T(1024)(128)(2,1)} reshape(bf16[2,1113856]{1,0:T(2,128)(2,1)} %slice.18) | data formatting | bytes 8910848 | tf_op jit(solution)/shard_map/cond
  161.7 12.1 %reshape.10 = bf16[2,256,4351]{2,1,0:T(8,128)(2,1)} reshape(bf16[2227712]{0:T(1024)(128)(2,1)} %reshape.16) | data formatting | bytes 8910848 | tf_op jit(solution)/shard_map/cond/branch_1_fun/reshape | solution.py:15
  173.9 13.6 %fusion.8 = bf16[256,2,2048]{2,0,1:T(8,128)(2,1)S(1)} fusion(bf16[4096,2048]{1,0:T(8,128)(2,1)} %get-tuple-element.12, bf16[2,256,4351]{2,1,0:T(8,128)(2,1)} %reshape.10), kind=kOutput, calls=%fused_computation.4 | convolution fusion | flops 8590983168 | bytes 23068672 | tf_op jit(solution)/shard_map/cond/branch_1_fun/kab,bd->akd/dot_general | solution.py:34
  187.4 5.6 %convert_bitcast_fusion = bf16[2048,2,1024]{2,0,1:T(8,128)(2,1)} fusion(bf16[256,2,2048]{2,0,1:T(8,128)(2,1)S(1)} %get-tuple-element.19, bf16[1,256,1024]{2,1,0:T(8,128)(2,1)S(1)} %all-gather.1), kind=kOutput, calls=%fused_computation.10 | convolution fusion | flops 2151677952 | bytes 11010048 | tf_op jit(solution)/shard_map/tkd,to->dko/dot_general | solution.py:50
  193.1 0.0 reduce-scatter.5.cloned.1.call-update
  193.1 0.0 reduce-scatter.3.cloned.1.call-start
  193.1 6.5 %fusion.13 = bf16[256,1024]{1,0:T(8,128)(2,1)} fusion(bf16[256,2,2048]{2,0,1:T(8,128)(2,1)S(1)} %get-tuple-element.19, bf16[2,2048,1024]{2,1,0:T(8,128)(2,1)} %param.8), kind=kOutput, calls=%fused_computation.12 | convolution fusion | flops 2147745792 | bytes 11010048 | tf_op jit(solution)/shard_map/tkd,kdo->to/dot_general | solution.py:40
  199.7 0.0 reduce-scatter.3.cloned.1.call-update
  199.7 93.6 %reduce-scatter.5.cloned.1.call-done = bf16[64,2,1024]{2,0,1:T(8,128)(2,1)} async-done(((bf16[2048,2,1024]{2,0,1:T(8,128)(2,1)}), bf16[64,2,1024]{2,0,1:T(8,128)(2,1)}) %reduce-scatter.5.cloned.1.call-update) | async-done | bytes 262160 | tf_op jit(solution)/shard_map/reduce_scatter | solution.py:49
  293.3 1.9 copy.9
  295.2 37.4 %reduce-scatter.3.cloned.1.call-done = bf16[32,1024]{1,0:T(8,128)(2,1)} async-done(((bf16[256,1024]{1,0:T(8,128)(2,1)}), bf16[32,1024]{1,0:T(8,128)(2,1)}) %reduce-scatter.3.cloned.1.call-update) | async-done | bytes 65552 | tf_op jit(solution)/shard_map/reduce_scatter | solution.py:39
  (2 shorter events, 0.0 us)
Async XLA Ops:
  7.2 122.3 %all-gather.4.cloned.1.call-start = ((), (), s32[]{:S(2)}) async-start(), calls=%async_computation.4 | async-start | bytes 17825792 | tf_op jit(solution)/shard_map/all_gather | solution.py:28
  7.9 285.4 %reduce-scatter.5.cloned.1.call-start = ((), (), s32[]{:S(2)}) async-start(), calls=%async_computation.3 | async-start | bytes 8650752 | tf_op jit(solution)/shard_map/reduce_scatter | solution.py:49
  193.1 139.5 %reduce-scatter.3.cloned.1.call-start = ((), (), s32[]{:S(2)}) async-start(), calls=%async_computation.2 | async-start | bytes 589824 | tf_op jit(solution)/shard_map/reduce_scatter | solution.py:39
Sparse Core Ops, SparseCore 0:
  10.4 118.9 all-gather.3
  193.2 100.0 reduce-scatter.4
  296.5 36.0 reduce-scatter.2
where the time goes:
time: 341 us; the launch traced here: 339 us
  waiting for transfers between devices  224 us (66%)
  local copies, waits for them, and re-layouts  46.3 us (14%)
  blocking collectives  28.3 us (8%)
  matrix products  25.8 us (8%)
  between operations  13.8 us (4%)
    reduce_scatter x1, waiting for transfers between devices, shards(): lax.psum_scatter(jnp.einsum('tkd,to->dko', features, full_grad, preferred...  93.6 us
    all_gather x1, waiting for transfers between devices, shards(): piece = lax.all_gather(own_rows, 'seq', axis=0, tiled=True)  92.3 us
    reduce_scatter x1, waiting for transfers between devices, shards(): lax.psum_scatter(jnp.einsum('tkd,kdo->to', features, weights, preferred_e...  37.4 us
    all_gather x1, blocking collectives, shards(): full_grad = lax.all_gather(cotangent[0], 'filt', axis=0, tiled=True)  28.3 us
    cond x7, local copies, waits for them, and re-layouts  26.5 us
    dot_general x1, matrix products, compute(): jnp.einsum('kab,bd->akd', toeplitz, piece, preferred_element_type=jnp.flo...  13.6 us
    reshape x1, local copies, waits for them, and re-layouts, build_toeplitz(): tiled_rows.reshape(filter_count, out_rows, span_len - 1)[:, :, :in_rows]  12.1 us
  transfers between devices with their start and end apart: 3, of which 3 were waited for; matrix products, arithmetic and copies ran while one was open for 3% of the time, Pallas kernels for 0%

commit v1 on v0

v1 whole, which is shorter than its diff:
```python
import functools

import jax
import jax.numpy as jnp
from jax import lax
from jax.experimental import pallas as pl
from jax.experimental.pallas import tpu as pltpu
from jax.sharding import PartitionSpec as P

BF = jnp.bfloat16
F32 = jnp.float32
VMEM_LIMIT = 56 * 1024 * 1024


def params():
    return pltpu.CompilerParams(vmem_limit_bytes=VMEM_LIMIT)


def prep_kernel(n_chunk, x_ref, w_ref, y_ref):
    step = pl.program_id(0)
    per, rows, tokens = y_ref.shape
    width = x_ref.shape[1] // n_chunk
    count, _, cols = w_ref.shape
    sub = cols // per
    x = x_ref[...]
    for k in range(count):
        u = jnp.dot(x, w_ref[k], preferred_element_type=F32).T.astype(BF)
        for c in range(per):
            y_ref[c, width + k * sub : width + (k + 1) * sub, :] = u[c * sub : (c + 1) * sub]
    span = width * per
    xs = x_ref[:, pl.ds(pl.multiple_of(step * span, span), span)]
    xt = xs.T
    for c in range(per):
        y_ref[c, :width, :] = xt[c * width : (c + 1) * width]


def prep(x, w, n_chunk):
    tokens, width = x.shape
    count, _, out_width = w.shape
    steps = 4
    per = n_chunk // steps
    rows = width // n_chunk + count * (out_width // n_chunk)

    return pl.pallas_call(
        functools.partial(prep_kernel, n_chunk),
        grid=(steps,),
        out_shape=jax.ShapeDtypeStruct((n_chunk, rows, tokens), BF),
        in_specs=[
            pl.BlockSpec((tokens, width), lambda s: (0, 0)),
            pl.BlockSpec((count, width, out_width // steps), lambda s: (0, 0, s)),
        ],
        out_specs=pl.BlockSpec((per, rows, tokens), lambda s: (s, 0, 0)),
        compiler_params=params(),
    )(x, w)


def table_kernel(f_ref, z_ref):
    count, length, block = z_ref.shape
    n = length // block
    for k in range(count):
        for c in range(n):
            lag = block * (n - 1 - c)
            g = jnp.broadcast_to(f_ref[k : k + 1, lag : lag + 2 * block], (block, 2 * block))
            m = pltpu.roll(g, 0, 1, stride=1, stride_axis=0)[:, block:]
            z_ref[k, c * block : (c + 1) * block, :] = m.astype(BF)


def table(filters, block):
    length, count = filters.shape
    f = filters.T.astype(BF).astype(F32)
    f = jnp.pad(f, ((0, 0), (block, 0)))
    return pl.pallas_call(
        table_kernel,
        out_shape=jax.ShapeDtypeStruct((count, length, block), BF),
        compiler_params=params(),
    )(f)


def out_conv_kernel(parts, width, y_ref, z_ref, p_ref, u_ref):
    n, rows, block = y_ref.shape
    count = z_ref.shape[0]
    length = n * block
    sub = (rows - width) // count
    shifts = block // sub
    for k in range(count):
        for s in range(shifts):
            d = shifts - 1 - s
            if d:
                u_ref[k, s * sub : (s + 1) * sub, : d * block] = jnp.zeros((sub, d * block), BF)
            for j in range(n - d):
                u_ref[k, s * sub : (s + 1) * sub, (j + d) * block : (j + d + 1) * block] = y_ref[
                    j, width + k * sub : width + (k + 1) * sub, :
                ]
    piece = block // parts
    half = piece // 2
    for m in range(n // shifts):
        depth = (m + 1) * shifts * block
        acc = jnp.dot(u_ref[0, :, :depth], z_ref[0, length - depth :, :], preferred_element_type=F32)
        for k in range(1, count):
            acc += jnp.dot(u_ref[k, :, :depth], z_ref[k, length - depth :, :], preferred_element_type=F32)
        t = acc.T
        for s in range(shifts):
            i = m * shifts + s
            for j in range(parts):
                low = t[j * piece : j * piece + half, s * sub : (s + 1) * sub]
                high = t[j * piece + half : (j + 1) * piece, s * sub : (s + 1) * sub]
                p_ref[i * parts + j] = jnp.concatenate([low, high], axis=1).astype(BF)


def out_conv(y, z, parts, width):

    n, rows, block = y.shape
    count = z.shape[0]
    sub = (rows - width) // count
    return pl.pallas_call(
        functools.partial(out_conv_kernel, parts, width),
        out_shape=jax.ShapeDtypeStruct((n * parts, block // parts // 2, 2 * sub), BF),
        scratch_shapes=[pltpu.VMEM((count, block, n * block), BF)],
        compiler_params=params(),
    )(y, z)


def feature_kernel(width, y_ref, z_ref, f_ref, x_ref):
    n, rows, block = y_ref.shape
    count = z_ref.shape[0]
    length = n * block
    shifts = block // width
    for s in range(shifts):
        d = shifts - 1 - s
        if d:
            x_ref[s * width : (s + 1) * width, : d * block] = jnp.zeros((width, d * block), BF)
        for j in range(n - d):
            x_ref[s * width : (s + 1) * width, (j + d) * block : (j + d + 1) * block] = y_ref[j, :width, :]
    for m in range(n // shifts):
        depth = (m + 1) * shifts * block
        for k in range(count):
            acc = jnp.dot(x_ref[:, :depth], z_ref[k, length - depth :, :], preferred_element_type=F32).astype(BF)
            for s in range(shifts):
                i = m * shifts + s
                f_ref[k * width : (k + 1) * width, i * block : (i + 1) * block] = acc[s * width : (s + 1) * width]


def feature_conv(y, z, width):

    n, rows, block = y.shape
    count = z.shape[0]
    return pl.pallas_call(
        functools.partial(feature_kernel, width),
        out_shape=jax.ShapeDtypeStruct((count * width, n * block), BF),
        scratch_shapes=[pltpu.VMEM((block, n * block), BF)],
        compiler_params=params(),
    )(y, z)


def shards(n_seq, n_filt, inputs, filters, weights, cotangent):
    x = inputs[0]
    tokens, width = x.shape
    count, _, out_width = weights.shape
    own = width // n_seq
    sub = out_width // n_seq

    spread = jnp.broadcast_to(cotangent[0][None], (n_filt,) + cotangent.shape[1:])
    block_grad = lax.all_to_all(spread, "filt", 0, 0, tiled=True).reshape(tokens, out_width)
    full_grad = lax.all_gather(block_grad, "seq", axis=0, tiled=True)

    z = table(filters, tokens)
    y = prep(x, weights, n_seq)
    y = lax.all_to_all(y, "seq", 0, 0, tiled=True)

    p = out_conv(y, z, n_filt, own)
    p = lax.all_to_all(p, ("seq", "filt"), 0, 0, tiled=True)
    p = p.reshape(n_seq, n_filt, tokens // n_filt // 2, 2, sub).astype(F32).sum(axis=1)
    outputs = p.transpose(2, 1, 0, 3).reshape(1, tokens // n_filt, out_width).astype(BF)

    f = feature_conv(y, z, own)
    grad = jnp.dot(f, full_grad, preferred_element_type=F32).reshape(count, 2, own // 2, out_width)
    me = lax.axis_index("dp")
    mine = lax.dynamic_index_in_dim(grad, me, 1, keepdims=False)
    other = lax.dynamic_index_in_dim(grad, 1 - me, 1, keepdims=False)
    other = lax.ppermute(other, "dp", [(0, 1), (1, 0)])
    weight_grad = (mine + other).astype(BF).transpose(1, 0, 2)
    return outputs, weight_grad


def solution(mesh):

    in_specs = (
        P("dp", "seq", None),
        P(None, "filt"),
        P("filt", None, None),
        P("dp", ("seq", "filt"), None),
    )
    out_specs = (P("dp", ("seq", "filt"), None), P(("seq", "dp"), "filt", None))
    body = functools.partial(shards, mesh.shape["seq"], mesh.shape["filt"])
    return jax.shard_map(body, mesh=mesh, in_specs=in_specs, out_specs=out_specs, check_vma=False)
```

time: 341 us -> 152 us (0.45)
  waiting for transfers between devices: 224 us -> 54.5 us
  local copies, waits for them, and re-layouts: 46.3 us -> 3.94 us
  Pallas kernels: 0 us -> 26.9 us
  matrix products: 25.8 us -> 6.34 us
  starting transfers between devices: 0.12 us -> 15.7 us
  blocking collectives: 28.3 us -> 24.5 us
    reduce_scatter x2 -> x0, waiting for transfers between devices: 131 us -> none  [the longest x1 93.6 us: shards(): lax.psum_scatter(jnp.einsum('tkd,to->dko', features, full_grad, preferred...]
    all_gather x1, waiting for transfers between devices: 92.3 us -> 22.7 us  [shards(): full_grad = lax.all_gather(block_grad, 'seq', axis=0, tiled=True)]
    all_to_all x0 -> x2, waiting for transfers between devices: none -> 31.8 us  [the longest x1 31.8 us: shards(): y = lax.all_to_all(y, 'seq', 0, 0, tiled=True)]
    all_gather x1 -> x0, blocking collectives: 28.3 us -> none  [shards(): full_grad = lax.all_gather(cotangent[0], 'filt', axis=0, tiled=True)]
    pallas_call x0 -> x4, Pallas kernels: none -> 26.9 us  [the longest x1 9.28 us: feature_conv(): pl.pallas_call(functools.partial(feature_kernel, width), out_shape=jax.Sh...]
    cond x7 -> x0, local copies, waits for them, and re-layouts: 26.5 us -> none
    all_to_all x0 -> x1, blocking collectives: none -> 24.5 us  [shards(): lax.all_to_all(spread, 'filt', 0, 0, tiled=True).reshape(tokens, out_width)]
    dot_general x3 -> x1, matrix products: 25.8 us -> 6.34 us  [shards(): jnp.dot(f, full_grad, preferred_element_type=F32)]
  transfers between devices with their start and end apart: 3 -> 4, of which waited for: 3 -> 2; matrix products, arithmetic and copies ran while one was open for 3% -> 7% of each run, Pallas kernels for 0% -> 18%
where the time goes in v1:
time: 152 us; the launch traced here: 150 us
  waiting for transfers between devices  54.5 us (36%)
  Pallas kernels  26.9 us (18%)
  blocking collectives  24.5 us (16%)
  starting transfers between devices  15.7 us (10%)
  between operations  14.1 us (9%)
  matrix products  6.34 us (4%)
  local copies, waits for them, and re-layouts  3.94 us (3%)
  other arithmetic  3.61 us (2%)
    all_to_all x1, waiting for transfers between devices, shards(): y = lax.all_to_all(y, 'seq', 0, 0, tiled=True)  31.8 us
    all_to_all x1, blocking collectives, shards(): lax.all_to_all(spread, 'filt', 0, 0, tiled=True).reshape(tokens, out_width)  24.5 us
    all_gather x1, waiting for transfers between devices, shards(): full_grad = lax.all_gather(block_grad, 'seq', axis=0, tiled=True)  22.7 us
    pallas_call x1, Pallas kernels, feature_conv(): pl.pallas_call(functools.partial(feature_kernel, width), out_shape=jax.Sh...  9.28 us
    all_to_all x1, starting transfers between devices, shards(): p = lax.all_to_all(p, ('seq', 'filt'), 0, 0, tiled=True)  8.39 us
    all_to_all x1, starting transfers between devices, shards(): y = lax.all_to_all(y, 'seq', 0, 0, tiled=True)  7.17 us
    pallas_call x1, Pallas kernels, prep(): pl.pallas_call(functools.partial(prep_kernel, n_chunk), grid=(steps,), ou...  7.11 us
    pallas_call x1, Pallas kernels, out_conv(): pl.pallas_call(functools.partial(out_conv_kernel, parts, width), out_shap...  6.68 us
  transfers between devices with their start and end apart: 4, of which 2 were waited for; matrix products, arithmetic and copies ran while one was open for 7% of the time, Pallas kernels for 18%

profile of v1, /device:TPU:32, one launch (start us, length us, event | category | flops | bytes accessed | tf_op | source)
XLA Modules:
  0.0 149.7 jit_solution(628009807043330044)
XLA Ops:
  7.2 0.0 all-gather.2.cloned.1.call-start
  7.2 0.9 broadcast_in_dim.8
  8.1 24.5 %all_to_all.15 = bf16[8,32,1024]{2,1,0:T(8,128)(2,1)} all-to-all(bf16[8,32,1024]{2,1,0:T(8,128)(2,1)S(1)} %broadcast_in_dim.8), channel_id=1, replica_groups=mesh['seq'=16,'filt'=8,'dp'=2] {'filt'}, dimensions={0} | all-to-all | bytes 1048576 | tf_op jit(solution)/shard_map/all_to_all | solution.py:163
  32.6 0.0 all-gather.2.cloned.1.call-update
  32.6 7.1 %shard_map.59 = bf16[16,256,256]{2,1,0:T(8,128)(2,1)} custom-call(bf16[256,2048]{1,0:T(8,128)(2,1)} %bitcast.24, bf16[2,2048,1024]{2,1,0:T(8,128)(2,1)} %w_ref.1), custom_call_target="tpu_custom_call" | custom-call | tf_op jit(solution)/shard_map/pallas_call | solution.py:44
  39.8 0.0 copy-start.1
  39.8 7.2 %all-to-all-start = ((bf16[16,256,256]{2,1,0:T(8,128)(2,1)}), bf16[16,256,256]{2,1,0:T(8,128)(2,1)S(1)}, u32[]{:S(2)}, u32[]{:S(2)}) async-start(bf16[16,256,256]{2,1,0:T(8,128)(2,1)} %shard_map.59), calls=%async_computation | async-start | bytes 4194304 | tf_op jit(solution)/shard_map/all_to_all | solution.py:168
  46.9 0.0 copy-done.1
  47.0 0.6 pad_convert_fusion.f_ref
  47.6 3.9 %shard_map.60.z_ref = bf16[2,4096,256]{2,1,0:T(8,128)(2,1)} custom-call(f32[2,4352]{1,0:T(2,128)} %pad_convert_fusion.f_ref), custom_call_target="tpu_custom_call" | custom-call | tf_op jit(solution)/shard_map/pallas_call | solution.py:72
  51.5 31.8 %all-to-all-done.y_ref = bf16[16,256,256]{2,1,0:T(8,128)(2,1)S(1)} async-done(((bf16[16,256,256]{2,1,0:T(8,128)(2,1)}), bf16[16,256,256]{2,1,0:T(8,128)(2,1)S(1)}, u32[]{:S(2)}, u32[]{:S(2)}) %all-to-all-start) | async-done | bytes 2097184 | tf_op jit(solution)/shard_map/all_to_all | solution.py:168
  83.3 0.0 copy-start
  83.3 1.3 copy-done
  84.6 6.7 %shard_map.61 = bf16[128,16,128]{2,1,0:T(8,128)(2,1)} custom-call(bf16[16,256,256]{2,1,0:T(8,128)(2,1)} %copy-done, bf16[2,4096,256]{2,1,0:T(8,128)(2,1)} %shard_map.60.z_ref), custom_call_target="tpu_custom_call" | custom-call | tf_op jit(solution)/shard_map/pallas_call | solution.py:115
  91.3 8.4 %all-to-all-start.1 = ((bf16[128,16,128]{2,1,0:T(8,128)(2,1)}), bf16[128,16,128]{2,1,0:T(8,128)(2,1)S(1)}, u32[]{:S(2)}, u32[]{:S(2)}) async-start(bf16[128,16,128]{2,1,0:T(8,128)(2,1)} %shard_map.61), calls=%async_computation.1 | async-start | bytes 1048576 | tf_op jit(solution)/shard_map/all_to_all | solution.py:171
  99.7 9.3 %shard_map.62 = bf16[256,4096]{1,0:T(8,128)(2,1)} custom-call(bf16[16,256,256]{2,1,0:T(8,128)(2,1)} %copy-done, bf16[2,4096,256]{2,1,0:T(8,128)(2,1)} %shard_map.60.z_ref), custom_call_target="tpu_custom_call" | custom-call | tf_op jit(solution)/shard_map/pallas_call | solution.py:147
  109.0 22.7 %all-gather.2.cloned.1.call-done = bf16[4096,1024]{1,0:T(8,128)(2,1)} async-done(((bf16[256,1024]{1,0:T(8,128)(2,1)}), bf16[4096,1024]{1,0:T(8,128)(2,1)}) %all-gather.2.cloned.1.call-update) | async-done | bytes 8388624 | tf_op jit(solution)/shard_map/all_gather | solution.py:164
  131.6 6.3 %fusion.2 = f32[256,1024]{1,0:T(8,128)S(1)} fusion(bf16[256,4096]{1,0:T(8,128)(2,1)} %shard_map.62, bf16[4096,1024]{1,0:T(8,128)(2,1)} %all-gather.2.cloned.1.call-done), kind=kOutput, calls=%fused_computation.8 | convolution fusion | flops 2147483648 | bytes 11534336 | tf_op jit(solution)/shard_map/dot_general | solution.py:176
  138.0 0.1 constant_dynamic-slice_fusion.1
  138.1 0.4 copy.17
  138.5 0.1 collective-permute-start
  138.6 0.0 all-to-all-done.1
  138.6 0.4 convert_element_type.38
  139.0 1.7 %reduce = bf16[16,16,2,64]{3,2,1,0:T(2,128)(2,1)S(1)} reduce(bf16[16,8,16,2,64]{4,3,2,1,0:T(2,128)(2,1)S(1)} %convert_element_type.38, bf16[]{:T(256)} %constant.15.clone.1), dimensions={1}, to_apply=%region_0.1.clone | reduce | flops 229376 | bytes 589826 | tf_op jit(solution)/shard_map/reduce_sum | solution.py:172
  140.8 0.1 copy.10
  140.8 0.8 convert_element_type.42
  141.6 0.0 collective-permute-done
  141.6 1.2 fusion.1
  (1 shorter events, 0.0 us)
Async XLA Ops:
  7.2 124.5 %all-gather.2.cloned.1.call-start = ((), (), s32[]{:S(2)}) async-start(), calls=%async_computation.3 | async-start | bytes 8912896 | tf_op jit(solution)/shard_map/all_gather | solution.py:164
  39.8 7.2 %copy-start.1 = (f32[4096,2]{0,1:T(2,128)S(1)}, f32[4096,2]{0,1:T(2,128)}, u32[]{:S(2)}) copy-start(f32[4096,2]{0,1:T(2,128)} %param.5) | copy-start | bytes 98308
  39.8 43.5 %all-to-all-start = ((bf16[16,256,256]{2,1,0:T(8,128)(2,1)}), bf16[16,256,256]{2,1,0:T(8,128)(2,1)S(1)}, u32[]{:S(2)}, u32[]{:S(2)}) async-start(bf16[16,256,256]{2,1,0:T(8,128)(2,1)} %shard_map.59), calls=%async_computation | async-start | bytes 4194304 | tf_op jit(solution)/shard_map/all_to_all | solution.py:168
  83.3 1.3 copy-start
  91.3 47.3 %all-to-all-start.1 = ((bf16[128,16,128]{2,1,0:T(8,128)(2,1)}), bf16[128,16,128]{2,1,0:T(8,128)(2,1)S(1)}, u32[]{:S(2)}, u32[]{:S(2)}) async-start(bf16[128,16,128]{2,1,0:T(8,128)(2,1)} %shard_map.61), calls=%async_computation.1 | async-start | bytes 1048576 | tf_op jit(solution)/shard_map/all_to_all | solution.py:171
  138.5 3.1 %collective-permute-start = (f32[2,64,1024]{2,0,1:T(2,128)S(1)}, f32[2,64,1024]{2,0,1:T(2,128)S(1)}, u32[]{:S(2)}, u32[]{:S(2)}) collective-permute-start(f32[2,64,1024]{2,0,1:T(2,128)S(1)} %bitcast.26), channel_id=1, source_target_pairs={{0,1},{1,0},{2,3},{3,2},{4,5},{5,4},{6,7},{7,6},{8,9},{9,8},{10,11... | collective-permute-start | bytes 1572872 | tf_op jit(solution)/shard_map/ppermute | solution.py:180
Sparse Core Ops, SparseCore 0:
  32.8 98.8 all-gather.1

commit v2 on v1

v2 whole, which is shorter than its diff:
```python
import functools

import jax
import jax.numpy as jnp
from jax import lax
from jax.experimental import pallas as pl
from jax.experimental.pallas import tpu as pltpu
from jax.sharding import PartitionSpec as P

BF = jnp.bfloat16
F32 = jnp.float32
VMEM_LIMIT = 56 * 1024 * 1024
SIDE = 4


def params():
    return pltpu.CompilerParams(vmem_limit_bytes=VMEM_LIMIT)


def cost(flops, data):
    return pl.CostEstimate(flops=flops, bytes_accessed=data, transcendentals=0)


def turn_kernel(x_ref, y_ref):
    per, width, tokens = y_ref.shape
    xt = x_ref[...].T
    for c in range(per):
        y_ref[c] = xt[c * width : (c + 1) * width]


def turn(x, n_chunk):
    tokens, width = x.shape
    steps = 2
    own = width // n_chunk
    return pl.pallas_call(
        turn_kernel,
        grid=(steps,),
        out_shape=jax.ShapeDtypeStruct((n_chunk, own, tokens), BF),
        in_specs=[pl.BlockSpec((tokens, width // steps), lambda s: (0, s))],
        out_specs=pl.BlockSpec((n_chunk // steps, own, tokens), lambda s: (s, 0, 0)),
        compiler_params=params(),
        cost_estimate=cost(0, 4 * tokens * width),
    )(x)


def project_kernel(x_ref, w_ref, y_ref):
    per, rows, tokens = y_ref.shape
    count, _, cols = w_ref.shape
    sub = cols // per
    x = x_ref[...]
    for k in range(count):
        u = jnp.dot(x, w_ref[k], preferred_element_type=F32).T.astype(BF)
        for c in range(per):
            y_ref[c, k * sub : (k + 1) * sub, :] = u[c * sub : (c + 1) * sub]


def project(x, w, n_chunk):
    tokens, width = x.shape
    count, _, out_width = w.shape
    steps = 4
    rows = count * (out_width // n_chunk)
    return pl.pallas_call(
        project_kernel,
        grid=(steps,),
        out_shape=jax.ShapeDtypeStruct((n_chunk, rows, tokens), BF),
        in_specs=[
            pl.BlockSpec((tokens, width), lambda s: (0, 0)),
            pl.BlockSpec((count, width, out_width // steps), lambda s: (0, 0, s)),
        ],
        out_specs=pl.BlockSpec((n_chunk // steps, rows, tokens), lambda s: (s, 0, 0)),
        compiler_params=params(),
        cost_estimate=cost(2 * tokens * width * count * out_width, 2 * count * width * out_width),
    )(x, w)


def out_table_kernel(block, f_ref, z_ref):
    count, length, _ = z_ref.shape
    n = length // block
    for k in range(count):
        base = jnp.broadcast_to(f_ref[k : k + 1, :], (8, f_ref.shape[1]))
        base = pltpu.roll(base, 0, 1, stride=1, stride_axis=0)
        for g in range(block // 16):
            low = pltpu.roll(base, 16 * g, 1) if g else base
            high = pltpu.roll(base, 16 * g + 8, 1)
            rows = jnp.concatenate([low, high], axis=0).astype(BF)
            for c in range(n):
                z_ref[k, c * block + 16 * g : c * block + 16 * g + 16, :] = rows[:, (n - c) * block : (n - c + 1) * block]


def feature_table_kernel(block, f_ref, z_ref):
    length, cols = z_ref.shape
    count = f_ref.shape[0]
    half = cols // count
    n = length // block
    piece = 32
    lane = lax.broadcasted_iota(jnp.int32, (16, half), 1)
    first = lax.rem(lane, 2 * piece) < piece
    for k in range(count):
        base = jnp.broadcast_to(f_ref[k : k + 1, :], (8, f_ref.shape[1]))
        base = pltpu.roll(base, 0, 1, stride=1, stride_axis=0)
        rolled = {}

        def at(g):
            if g not in rolled:
                rolled[g] = pltpu.roll(base, 8 * g, 1) if g else base
            return rolled[g]

        for g in range(block // 16):
            a = jnp.concatenate([at(2 * g), at(2 * g + 1)], axis=0)
            b = jnp.concatenate([at(2 * g + 4), at(2 * g + 5)], axis=0)
            for c in range(n):
                start = (n - c) * block
                both = jnp.where(first, a[:, start : start + half], b[:, start + half : start + 2 * half])
                z_ref[c * block + 16 * g : c * block + 16 * g + 16, k * half : (k + 1) * half] = both.astype(BF)


def out_table(f, length, block):
    count = f.shape[0]
    return pl.pallas_call(
        functools.partial(out_table_kernel, block),
        out_shape=jax.ShapeDtypeStruct((count, length, block), BF),
        compiler_params=params(),
        cost_estimate=cost(0, 2 * count * length * block),
    )(f)


def feature_table(f, length, block):
    count = f.shape[0]
    return pl.pallas_call(
        functools.partial(feature_table_kernel, block),
        out_shape=jax.ShapeDtypeStruct((length, count * block // 2), BF),
        compiler_params=params(),
        cost_estimate=cost(0, count * length * block),
    )(f)


def out_conv_kernel(parts, y_ref, z_ref, p_ref, u_ref):
    n, rows, block = y_ref.shape
    count = z_ref.shape[0]
    sub = rows // count
    length = n * block
    shifts = block // sub
    for k in range(count):
        for s in range(shifts):
            d = shifts - 1 - s
            if d:
                u_ref[k, s * sub : (s + 1) * sub, : d * block] = jnp.zeros((sub, d * block), BF)
            for j in range(n - d):
                u_ref[k, s * sub : (s + 1) * sub, (j + d) * block : (j + d + 1) * block] = y_ref[
                    j, k * sub : (k + 1) * sub, :
                ]
    piece = block // parts
    half = piece // 2
    for m in range(n // shifts):
        depth = (m + 1) * shifts * block
        acc = jnp.dot(u_ref[0, :, :depth], z_ref[0, length - depth :, :], preferred_element_type=F32)
        for k in range(1, count):
            acc += jnp.dot(u_ref[k, :, :depth], z_ref[k, length - depth :, :], preferred_element_type=F32)
        t = acc.T
        for s in range(shifts):
            i = m * shifts + s
            for j in range(parts):
                low = t[j * piece : j * piece + half, s * sub : (s + 1) * sub]
                high = t[j * piece + half : (j + 1) * piece, s * sub : (s + 1) * sub]
                p_ref[i * parts + j] = jnp.concatenate([low, high], axis=1).astype(BF)


def out_conv(y, z, parts):
    n, rows, block = y.shape
    count = z.shape[0]
    sub = rows // count
    return pl.pallas_call(
        functools.partial(out_conv_kernel, parts),
        out_shape=jax.ShapeDtypeStruct((n * parts, block // parts // 2, 2 * sub), BF),
        scratch_shapes=[pltpu.VMEM((count, block, n * block), BF)],
        compiler_params=params(),
        cost_estimate=cost(2 * count * sub * (n * block) ** 2, 2 * count * n * block * block),
    )(y, z)


def feature_kernel(y_ref, z_ref, f_ref, x_ref):
    n, width, block = y_ref.shape
    length, cols = z_ref.shape
    half = block // 2
    count = cols // half
    shifts = block // width
    for s in range(shifts):
        d = shifts - 1 - s
        if d:
            x_ref[s * width : (s + 1) * width, : d * block] = jnp.zeros((width, d * block), BF)
        for j in range(n - d):
            x_ref[s * width : (s + 1) * width, (j + d) * block : (j + d + 1) * block] = y_ref[j]
    for m in range(n // shifts):
        depth = (m + 1) * shifts * block
        acc = jnp.dot(x_ref[:, :depth], z_ref[length - depth :, :], preferred_element_type=F32).astype(BF)
        for k in range(count):
            for s in range(shifts):
                i = m * shifts + s
                f_ref[k * width : (k + 1) * width, i * half : (i + 1) * half] = acc[
                    s * width : (s + 1) * width, k * half : (k + 1) * half
                ]


def feature_conv(y, z):
    n, width, block = y.shape
    length, cols = z.shape
    count = cols // (block // 2)
    return pl.pallas_call(
        feature_kernel,
        out_shape=jax.ShapeDtypeStruct((count * width, length // 2), BF),
        scratch_shapes=[pltpu.VMEM((block, length), BF)],
        compiler_params=params(),
        cost_estimate=cost(count * width * length * length, 2 * length * cols),
    )(y, z)


def grad_kernel(place_ref, f_ref, *refs):
    pieces, out_ref, grad_ref, sem = refs[:-3], refs[-3], refs[-2], refs[-1]
    half_rows = grad_ref.shape[0] // (SIDE * SIDE)
    half_cols = grad_ref.shape[1] // 2
    y, x = place_ref[0], place_ref[1]
    copies = []
    for side, group in enumerate((pieces[:5], pieces[5:])):
        for far in range(SIDE):
            for near in range(SIDE):
                if far == 0:
                    ref, index = group[0], near
                elif far == 1:
                    ref, index = group[1], near
                elif far == SIDE - 1:
                    ref, index = group[2], near
                elif near < SIDE // 2:
                    ref, index = group[3], near
                else:
                    ref, index = group[4], near - SIDE // 2
                dy, dx = (far, near) if side == 0 else (near, far)
                block = lax.rem(y + dy, SIDE) * SIDE + lax.rem(x + dx, SIDE)
                rows = pl.ds(pl.multiple_of(block * half_rows, half_rows), half_rows)
                copies.append(
                    pltpu.make_async_copy(
                        ref.at[index], grad_ref.at[rows, side * half_cols : (side + 1) * half_cols], sem.at[len(copies)]
                    )
                )
    for copy in copies:
        copy.start()
    for copy in copies:
        copy.wait()
    count = out_ref.shape[0]
    rows = f_ref.shape[0] // count
    for k in range(count):
        out_ref[k] = jnp.dot(f_ref[k * rows : (k + 1) * rows, :], grad_ref[...], preferred_element_type=F32).astype(BF)


def grad(f, pieces, place, count, out_width):
    rows, length = f.shape
    return pl.pallas_call(
        grad_kernel,
        out_shape=jax.ShapeDtypeStruct((count, rows // count, out_width), BF),
        in_specs=[pl.BlockSpec(memory_space=pltpu.SMEM), pl.BlockSpec(memory_space=pltpu.VMEM)]
        + [pl.BlockSpec(memory_space=pl.ANY)] * len(pieces),
        scratch_shapes=[pltpu.VMEM((length, out_width), BF), pltpu.SemaphoreType.DMA((2 * SIDE * SIDE,))],
        compiler_params=params(),
        cost_estimate=cost(2 * rows * length * out_width, 2 * length * out_width),
    )(place, f, *pieces)


def shift(axis, step):
    pairs = []
    for y in range(SIDE):
        for x in range(SIDE):
            to = ((y + step) % SIDE, x) if axis == "y" else (y, (x + step) % SIDE)
            pairs.append((y * SIDE + x, to[0] * SIDE + to[1]))
    return pairs


def move(a, axis, step):
    return lax.ppermute(a, "seq", shift(axis, step))


def plane_gather(a, near, far):
    ring = jnp.stack([a, move(a, near, -1), move(a, near, 2), move(a, near, 1)])
    after, before = move(ring, far, -1), move(ring, far, 1)
    h = SIDE // 2
    return [ring, after, before, move(before[:h], far, 1), move(after[h:], far, -1)]


def shards(n_seq, n_filt, inputs, filters, weights, cotangent):
    x = inputs[0]
    tokens, width = x.shape
    count, _, out_width = weights.shape
    length = filters.shape[0]
    sub = out_width // n_seq
    own = width // n_seq
    piece = tokens // n_filt
    at_seq, at_filt, at_dp = lax.axis_index("seq"), lax.axis_index("filt"), lax.axis_index("dp")
    parity = at_filt % 2

    c = cotangent[0]
    quads = [c] + [
        lax.ppermute(c, "filt", [((i + step) % n_filt, i) for i in range(n_filt)]) for step in (2, 4, 6)
    ]
    stack = jnp.stack(quads + quads)
    half = lax.dynamic_slice_in_dim(stack, (n_filt // 2 - at_filt // 2) % (n_filt // 2), n_filt // 2, 0)
    half = jnp.stack([half[0], half[2], half[1], half[3]]).reshape(tokens // 2, out_width)

    xs = lax.all_to_all(turn(x, n_seq), "seq", 0, 0, tiled=True)
    us = lax.all_to_all(project(x, weights, n_seq), "seq", 0, 0, tiled=True)

    pieces = plane_gather(half[:, : out_width // 2], "x", "y") + plane_gather(half[:, out_width // 2 :], "y", "x")

    fb = filters.T.astype(BF)
    other = lax.ppermute(fb, "filt", [(i, i ^ 1) for i in range(n_filt)])
    pad = ((0, 0), (tokens, tokens))
    pair = jnp.pad(jnp.concatenate([fb, other]).astype(F32), pad)
    pair = lax.dynamic_slice_in_dim(pair, piece * parity, length + tokens, 1)
    z_out = out_table(jnp.pad(fb.astype(F32), ((0, 0), (tokens, 0))), length, tokens)
    z_feature = feature_table(pair, length, tokens)

    f = feature_conv(xs, z_feature)
    p = out_conv(us, z_out, n_filt)
    p = lax.all_to_all(p, ("seq", "filt"), 0, 0, tiled=True)
    p = p.reshape(n_seq, n_filt, piece // 2, 2, sub).astype(F32).sum(axis=1)
    outputs = p.transpose(2, 1, 0, 3).reshape(1, piece, out_width).astype(BF)

    place = jnp.stack([at_seq // SIDE, at_seq % SIDE]).astype(jnp.int32)
    g = grad(f, pieces, place, 2 * count, out_width).reshape(2 * count, 2, own // 2, out_width)
    mine = lax.dynamic_index_in_dim(g, at_dp, 1, keepdims=False)
    rest = lax.dynamic_index_in_dim(g, 1 - at_dp, 1, keepdims=False)
    total = mine.astype(F32) + lax.ppermute(rest, "dp", [(0, 1), (1, 0)]).astype(F32)
    back = lax.ppermute(total[count:].astype(BF), "filt", [(i, i ^ 1) for i in range(n_filt)])
    weight_grad = (total[:count] + back.astype(F32)).astype(BF).transpose(1, 0, 2)
    return outputs, weight_grad


def solution(mesh):
    in_specs = (
        P("dp", "seq", None),
        P(None, "filt"),
        P("filt", None, None),
        P("dp", ("seq", "filt"), None),
    )
    out_specs = (P("dp", ("seq", "filt"), None), P(("seq", "dp"), "filt", None))
    body = functools.partial(shards, mesh.shape["seq"], mesh.shape["filt"])
    return jax.shard_map(body, mesh=mesh, in_specs=in_specs, out_specs=out_specs, check_vma=False)
```

time: 152 us -> 136 us (0.89)
  starting transfers between devices: 15.7 us -> 57.6 us
  waiting for transfers between devices: 54.5 us -> 23.3 us
  blocking collectives: 24.5 us -> 0 us
  Pallas kernels: 26.9 us -> 40.5 us
  between operations: 14.1 us -> 1.02 us
  matrix products: 6.34 us -> 0 us
  local copies, waits for them, and re-layouts: 3.94 us -> 6.91 us
  other arithmetic: 3.61 us -> 5.41 us
    ppermute x1 -> x20, starting transfers between devices: 0.09 us -> 34.9 us  [the longest x14 23.6 us: move(): return lax.ppermute(a, 'seq', shift(axis, step))]
    all_to_all x1 -> x2, waiting for transfers between devices: 31.8 us -> 0.01 us  [the longest x1 0.01 us: shards(): us = lax.all_to_all(project(x, weights, n_seq), 'seq', 0, 0, tiled=True)]
    all_to_all x1 -> x0, blocking collectives: 24.5 us -> none  [shards(): lax.all_to_all(spread, 'filt', 0, 0, tiled=True).reshape(tokens, out_width)]
    all_gather x1 -> x0, waiting for transfers between devices: 22.7 us -> none  [shards(): full_grad = lax.all_gather(block_grad, 'seq', axis=0, tiled=True)]
    ppermute x1 -> x20, waiting for transfers between devices: 0.01 us -> 21.1 us  [the longest x1 16.2 us: shards(): lax.ppermute(total[count:].astype(BF), 'filt', [(i, i ^ 1) for i in range...]
    pallas_call x4 -> x7, Pallas kernels: 26.9 us -> 40.5 us  [the longest x1 9.05 us: feature_conv(): pl.pallas_call(feature_kernel, out_shape=jax.ShapeDtypeStruct((count * wi...]
    dot_general x1 -> x0, matrix products: 6.34 us -> none  [shards(): jnp.dot(f, full_grad, preferred_element_type=F32)]
    all_to_all x1, starting transfers between devices: 8.39 us -> 11.9 us  [shards(): p = lax.all_to_all(p, ('seq', 'filt'), 0, 0, tiled=True)]
  transfers between devices with their start and end apart: 4 -> 23, of which waited for: 2 -> 3; matrix products, arithmetic and copies ran while one was open for 7% -> 6% of each run, Pallas kernels for 18% -> 30%
where the time goes in v2:
time: 136 us; the launch traced here: 135 us
  starting transfers between devices  57.6 us (42%)
  Pallas kernels  40.5 us (30%)
  waiting for transfers between devices  23.3 us (17%)
  local copies, waits for them, and re-layouts  6.91 us (5%)
  other arithmetic  5.41 us (4%)
    ppermute x14, starting transfers between devices, move(): return lax.ppermute(a, 'seq', shift(axis, step))  23.6 us
    ppermute x1, waiting for transfers between devices, shards(): lax.ppermute(total[count:].astype(BF), 'filt', [(i, i ^ 1) for i in range...  16.2 us
    all_to_all x1, starting transfers between devices, shards(): p = lax.all_to_all(p, ('seq', 'filt'), 0, 0, tiled=True)  11.9 us
    ppermute x3, starting transfers between devices, shards(): lax.ppermute(c, 'filt', [((i + step) % n_filt, i) for i in range(n_filt)])  9.29 us
    pallas_call x1, Pallas kernels, feature_conv(): pl.pallas_call(feature_kernel, out_shape=jax.ShapeDtypeStruct((count * wi...  9.05 us
    pallas_call x1, Pallas kernels, grad(): pl.pallas_call(grad_kernel, out_shape=jax.ShapeDtypeStruct((count, rows /...  7.52 us
    all_to_all x1, starting transfers between devices, shards(): xs = lax.all_to_all(turn(x, n_seq), 'seq', 0, 0, tiled=True)  7.03 us
    pallas_call x1, Pallas kernels, project(): pl.pallas_call(project_kernel, grid=(steps,), out_shape=jax.ShapeDtypeStr...  6.88 us
  transfers between devices with their start and end apart: 23, of which 3 were waited for; matrix products, arithmetic and copies ran while one was open for 6% of the time, Pallas kernels for 30%

profile of v2, /device:TPU:32, one launch (start us, length us, event | category | flops | bytes accessed | tf_op | source)
XLA Modules:
  0.0 134.6 jit_solution(2199275436660377728)
XLA Ops:
  0.6 5.5 %collective-permute-start.1 = (bf16[32,1024]{1,0:T(8,128)(2,1)}, bf16[32,1024]{1,0:T(8,128)(2,1)S(1)}, u32[]{:S(2)}, u32[]{:S(2)}) collective-permute-start(bf16[32,1024]{1,0:T(8,128)(2,1)} %bitcast.46), channel_id=1, source_target_pairs={{4,0},{6,2},{8,4},{10,6},{12,8},{14,10},{0,12},{2,14},{5,1},{7,3},... | collective-permute-start | bytes 196616 | tf_op jit(solution)/shard_map/ppermute | solution.py:300
  6.1 1.4 %collective-permute-start.2 = (bf16[32,1024]{1,0:T(8,128)(2,1)}, bf16[32,1024]{1,0:T(8,128)(2,1)S(1)}, u32[]{:S(2)}, u32[]{:S(2)}) collective-permute-start(bf16[32,1024]{1,0:T(8,128)(2,1)} %bitcast.47), channel_id=1, source_target_pairs={{8,0},{10,2},{12,4},{14,6},{0,8},{2,10},{4,12},{6,14},{9,1},{11,3}... | collective-permute-start | bytes 196616 | tf_op jit(solution)/shard_map/ppermute | solution.py:300
  7.6 2.4 %collective-permute-start.3 = (bf16[32,1024]{1,0:T(8,128)(2,1)}, bf16[32,1024]{1,0:T(8,128)(2,1)S(1)}, u32[]{:S(2)}, u32[]{:S(2)}) collective-permute-start(bf16[32,1024]{1,0:T(8,128)(2,1)} %bitcast.48), channel_id=1, source_target_pairs={{12,0},{14,2},{0,4},{2,6},{4,8},{6,10},{8,12},{10,14},{13,1},{15,3... | collective-permute-start | bytes 196616 | tf_op jit(solution)/shard_map/ppermute | solution.py:300
  9.9 2.2 %shard_map.62 = bf16[16,128,256]{2,1,0:T(8,128)(2,1)} custom-call(bf16[256,2048]{1,0:T(8,128)(2,1)} %bitcast.40), custom_call_target="tpu_custom_call" | custom-call | bytes 2097152 | tf_op jit(solution)/shard_map/pallas_call | solution.py:35
  12.2 7.0 %all-to-all-start.2 = ((bf16[16,128,256]{2,1,0:T(8,128)(2,1)}), bf16[16,128,256]{2,1,0:T(8,128)(2,1)S(1)}, u32[]{:S(2)}, u32[]{:S(2)}) async-start(bf16[16,128,256]{2,1,0:T(8,128)(2,1)} %shard_map.62), calls=%async_computation.2 | async-start | bytes 2097152 | tf_op jit(solution)/shard_map/all_to_all | solution.py:306
  19.3 0.6 pad_convert_fusion.f_ref
  20.2 2.0 %collective-permute-start.6 = (bf16[128,512]{1,0:T(8,128)(2,1)S(1)}, bf16[128,512]{1,0:T(8,128)(2,1)S(1)}, u32[]{:S(2)}, u32[]{:S(2)}) collective-permute-start(bf16[128,512]{1,0:T(8,128)(2,1)S(1)} %get-tuple-element.11), channel_id=1, source_target_pairs={{0,16},{16,32},{32,48},{48,0},{64,80},{80,96},{96,112},{112,64},{1... | collective-permute-start | bytes 393224 | tf_op jit(solution)/shard_map/ppermute | solution.py:277
  22.2 2.7 %collective-permute-start.5 = (bf16[128,512]{1,0:T(8,128)(2,1)S(1)}, bf16[128,512]{1,0:T(8,128)(2,1)S(1)}, u32[]{:S(2)}, u32[]{:S(2)}) collective-permute-start(bf16[128,512]{1,0:T(8,128)(2,1)S(1)} %get-tuple-element.11), channel_id=1, source_target_pairs={{0,32},{16,48},{32,0},{48,16},{64,96},{80,112},{96,64},{112,80},{1... | collective-permute-start | bytes 393224 | tf_op jit(solution)/shard_map/ppermute | solution.py:277
  24.8 1.5 %collective-permute-start.4 = (bf16[128,512]{1,0:T(8,128)(2,1)S(1)}, bf16[128,512]{1,0:T(8,128)(2,1)S(1)}, u32[]{:S(2)}, u32[]{:S(2)}) collective-permute-start(bf16[128,512]{1,0:T(8,128)(2,1)S(1)} %get-tuple-element.11), channel_id=1, source_target_pairs={{0,48},{16,0},{32,16},{48,32},{64,112},{80,64},{96,80},{112,96},{1... | collective-permute-start | bytes 393224 | tf_op jit(solution)/shard_map/ppermute | solution.py:277
  26.3 6.9 %shard_map.59 = bf16[16,128,256]{2,1,0:T(8,128)(2,1)} custom-call(bf16[256,2048]{1,0:T(8,128)(2,1)} %bitcast.41, bf16[2,2048,1024]{2,1,0:T(8,128)(2,1)} %w_ref.1), custom_call_target="tpu_custom_call" | custom-call | flops 2147483648 | bytes 8388608 | tf_op jit(solution)/shard_map/pallas_call | solution.py:62
  33.2 1.5 %collective-permute-start.13 = (bf16[128,512]{1,0:T(8,128)(2,1)S(1)}, bf16[128,512]{1,0:T(8,128)(2,1)S(1)}, u32[]{:S(2)}, u32[]{:S(2)}) collective-permute-start(bf16[128,512]{1,0:T(8,128)(2,1)S(1)} %get-tuple-element.10), channel_id=1, source_target_pairs={{0,64},{16,80},{32,96},{48,112},{64,128},{80,144},{96,160},{112,17... | collective-permute-start | bytes 393224 | tf_op jit(solution)/shard_map/ppermute | solution.py:277
  34.7 2.7 %collective-permute-start.12 = (bf16[128,512]{1,0:T(8,128)(2,1)S(1)}, bf16[128,512]{1,0:T(8,128)(2,1)S(1)}, u32[]{:S(2)}, u32[]{:S(2)}) collective-permute-start(bf16[128,512]{1,0:T(8,128)(2,1)S(1)} %get-tuple-element.10), channel_id=1, source_target_pairs={{0,128},{16,144},{32,160},{48,176},{64,192},{80,208},{96,224},{112... | collective-permute-start | bytes 393224 | tf_op jit(solution)/shard_map/ppermute | solution.py:277
  37.3 2.7 %collective-permute-start.11 = (bf16[128,512]{1,0:T(8,128)(2,1)S(1)}, bf16[128,512]{1,0:T(8,128)(2,1)S(1)}, u32[]{:S(2)}, u32[]{:S(2)}) collective-permute-start(bf16[128,512]{1,0:T(8,128)(2,1)S(1)} %get-tuple-element.10), channel_id=1, source_target_pairs={{0,192},{16,208},{32,224},{48,240},{64,0},{80,16},{96,32},{112,48}... | collective-permute-start | bytes 393224 | tf_op jit(solution)/shard_map/ppermute | solution.py:277
  40.0 0.6 pad_add_fusion.place_ref
  40.6 3.5 %shard_map.60.z_ref = bf16[2,4096,256]{2,1,0:T(8,128)(2,1)} custom-call(f32[2,4352]{1,0:T(2,128)} %pad_convert_fusion.f_ref), custom_call_target="tpu_custom_call" | custom-call | bytes 4194304 | tf_op jit(solution)/shard_map/pallas_call | solution.py:119
  44.1 1.0 collective-permute-start
  45.2 0.9 collective-permute-start.7
  46.1 1.2 collective-permute-start.8
  47.4 1.0 collective-permute-start.14
  48.4 1.1 collective-permute-start.15
  49.5 0.8 fusion.7.f_ref
  50.3 4.9 %shard_map.63.z_ref = bf16[4096,512]{1,0:T(8,128)(2,1)} custom-call(f32[4,4352]{1,0:T(4,128)} %fusion.7.f_ref), custom_call_target="tpu_custom_call" | custom-call | bytes 4194304 | tf_op jit(solution)/shard_map/pallas_call | solution.py:129
  55.1 4.9 %collective-permute-done.8.refs_2_ = bf16[4,128,512]{2,1,0:T(8,128)(2,1)S(1)} collective-permute-done((bf16[4,128,512]{2,1,0:T(8,128)(2,1)S(1)}, bf16[4,128,512]{2,1,0:T(8,128)(2,1)S(1)}, u32[]{:S(2)}, u32[]{:S(2)}) %collective-permute-start.8) | collective-permute-done | bytes 524320 | tf_op jit(solution)/shard_map/ppermute | solution.py:277
  60.0 0.1 collective-permute-start.9
  60.1 0.9 slice.51
  61.0 3.1 %collective-permute-start.10 = (bf16[2,128,512]{2,1,0:T(8,128)(2,1)}, bf16[2,128,512]{2,1,0:T(8,128)(2,1)}, u32[]{:S(2)}, u32[]{:S(2)}) collective-permute-start(bf16[2,128,512]{2,1,0:T(8,128)(2,1)} %slice.51), channel_id=1, source_target_pairs={{0,192},{16,208},{32,224},{48,240},{64,0},{80,16},{96,32},{112,48}... | collective-permute-start | bytes 786440 | tf_op jit(solution)/shard_map/ppermute | solution.py:277
  64.1 0.8 slice.53
  64.9 0.7 slice.54
  65.7 0.1 copy-done.7
  65.8 3.2 %collective-permute-start.17 = (bf16[2,128,512]{2,1,0:T(8,128)(2,1)}, bf16[2,128,512]{2,1,0:T(8,128)(2,1)}, u32[]{:S(2)}, u32[]{:S(2)}) collective-permute-start(bf16[2,128,512]{2,1,0:T(8,128)(2,1)} %slice.54), channel_id=1, source_target_pairs={{0,48},{16,0},{32,16},{48,32},{64,112},{80,64},{96,80},{112,96},{1... | collective-permute-start | bytes 786440 | tf_op jit(solution)/shard_map/ppermute | solution.py:277
  69.1 3.7 %all-to-all-start = ((bf16[16,128,256]{2,1,0:T(8,128)(2,1)}), bf16[16,128,256]{2,1,0:T(8,128)(2,1)S(1)}, u32[]{:S(2)}, u32[]{:S(2)}) async-start(bf16[16,128,256]{2,1,0:T(8,128)(2,1)} %shard_map.59), calls=%async_computation | async-start | bytes 2097152 | tf_op jit(solution)/shard_map/all_to_all | solution.py:307
  72.7 9.0 %shard_map.64.f_ref = bf16[512,2048]{1,0:T(8,128)(2,1)} custom-call(bf16[16,128,256]{2,1,0:T(8,128)(2,1)} %copy-done, bf16[4096,512]{1,0:T(8,128)(2,1)} %shard_map.63.z_ref), custom_call_target="tpu_custom_call" | custom-call | flops 8589934592 | bytes 4194304 | tf_op jit(solution)/shard_map/pallas_call | solution.py:208
  81.8 7.5 %shard_map.65 = bf16[4,128,1024]{2,1,0:T(8,128)(2,1)} custom-call(s32[2]{0:T(128)} %pad_add_fusion.place_ref, bf16[512,2048]{1,0:T(8,128)(2,1)} %shard_map.64.f_ref, bf16[4,128,512]{2,1,0:T(8,128)(2,1)} %copy-done.2, bf16[4,128,512]{2,1,0:T(8,128)(2,1)} %copy-done.5, bf16[4,128,512]{2,1,0:T(8,128)(2,1)} %copy-done.6, ...), custom_call_target="tpu_custom_call" | custom-call | flops 2147483648 | bytes 4194304 | tf_op jit(solution)/shard_map/pallas_call | solution.py:256
  89.3 1.3 constant_dynamic-slice_fusion.3
  90.6 0.4 copy.18
  91.0 0.1 collective-permute-start.18
  91.2 1.0 copy-done.1
  92.2 6.4 %shard_map.61 = bf16[128,16,128]{2,1,0:T(8,128)(2,1)} custom-call(bf16[16,128,256]{2,1,0:T(8,128)(2,1)} %copy-done.1, bf16[2,4096,256]{2,1,0:T(8,128)(2,1)} %shard_map.60.z_ref), custom_call_target="tpu_custom_call" | custom-call | flops 4294967296 | bytes 4194304 | tf_op jit(solution)/shard_map/pallas_call | solution.py:172
  98.6 11.9 %all-to-all-start.1 = ((bf16[128,16,128]{2,1,0:T(8,128)(2,1)}), bf16[128,16,128]{2,1,0:T(8,128)(2,1)S(1)}, u32[]{:S(2)}, u32[]{:S(2)}) async-start(bf16[128,16,128]{2,1,0:T(8,128)(2,1)} %shard_map.61), calls=%async_computation.1 | async-start | bytes 1048576 | tf_op jit(solution)/shard_map/all_to_all | solution.py:321
  110.5 0.5 convert_add_fusion
  111.1 0.3 slice.65
  111.3 1.0 collective-permute-start.19
  112.3 16.2 %collective-permute-done.19 = bf16[2,64,1024]{2,0,1:T(2,128)(2,1)S(1)} collective-permute-done((bf16[2,64,1024]{2,0,1:T(2,128)(2,1)S(1)}, bf16[2,64,1024]{2,0,1:T(2,128)(2,1)S(1)}, u32[]{:S(2)}, u32[]{:S(2)}) %collective-permute-start.19) | collective-permute-done | bytes 262176 | tf_op jit(solution)/shard_map/ppermute | solution.py:330
  128.5 1.0 fusion.1
  129.5 2.1 %all-to-all-done.1 = bf16[128,16,128]{2,1,0:T(8,128)(2,1)S(1)} async-done(((bf16[128,16,128]{2,1,0:T(8,128)(2,1)}), bf16[128,16,128]{2,1,0:T(8,128)(2,1)S(1)}, u32[]{:S(2)}, u32[]{:S(2)}) %all-to-all-start.1) | async-done | bytes 524320 | tf_op jit(solution)/shard_map/all_to_all | solution.py:321
  131.7 0.4 convert_element_type.53
  132.1 1.7 %reduce = bf16[16,16,2,64]{3,2,1,0:T(2,128)(2,1)S(1)} reduce(bf16[16,8,16,2,64]{4,3,2,1,0:T(2,128)(2,1)S(1)} %convert_element_type.53, bf16[]{:T(256)} %constant.64.clone.1), dimensions={1}, to_apply=%region_0.1.clone | reduce | flops 229376 | bytes 589826 | tf_op jit(solution)/shard_map/reduce_sum | solution.py:322
  133.9 0.8 convert_element_type.57
  (55 shorter events, 0.5 us)
Async XLA Ops:
  0.6 19.3 %copy-start.4 = (bf16[1,32,1024]{2,1,0:T(8,128)(2,1)S(1)}, bf16[1,32,1024]{2,1,0:T(8,128)(2,1)}, u32[]{:S(2)}) copy-start(bf16[1,32,1024]{2,1,0:T(8,128)(2,1)} %param.7) | copy-start | bytes 196612
  0.6 18.6 %copy-start.9 = (f32[4096,2]{0,1:T(2,128)S(1)}, f32[4096,2]{0,1:T(2,128)}, u32[]{:S(2)}) copy-start(f32[4096,2]{0,1:T(2,128)} %param.5) | copy-start | bytes 98308
  0.6 19.3 %collective-permute-start.1 = (bf16[32,1024]{1,0:T(8,128)(2,1)}, bf16[32,1024]{1,0:T(8,128)(2,1)S(1)}, u32[]{:S(2)}, u32[]{:S(2)}) collective-permute-start(bf16[32,1024]{1,0:T(8,128)(2,1)} %bitcast.46), channel_id=1, source_target_pairs={{4,0},{6,2},{8,4},{10,6},{12,8},{14,10},{0,12},{2,14},{5,1},{7,3},... | collective-permute-start | bytes 196616 | tf_op jit(solution)/shard_map/ppermute | solution.py:300
  6.1 13.8 %collective-permute-start.2 = (bf16[32,1024]{1,0:T(8,128)(2,1)}, bf16[32,1024]{1,0:T(8,128)(2,1)S(1)}, u32[]{:S(2)}, u32[]{:S(2)}) collective-permute-start(bf16[32,1024]{1,0:T(8,128)(2,1)} %bitcast.47), channel_id=1, source_target_pairs={{8,0},{10,2},{12,4},{14,6},{0,8},{2,10},{4,12},{6,14},{9,1},{11,3}... | collective-permute-start | bytes 196616 | tf_op jit(solution)/shard_map/ppermute | solution.py:300
  7.6 12.4 %collective-permute-start.3 = (bf16[32,1024]{1,0:T(8,128)(2,1)}, bf16[32,1024]{1,0:T(8,128)(2,1)S(1)}, u32[]{:S(2)}, u32[]{:S(2)}) collective-permute-start(bf16[32,1024]{1,0:T(8,128)(2,1)} %bitcast.48), channel_id=1, source_target_pairs={{12,0},{14,2},{0,4},{2,6},{4,8},{6,10},{8,12},{10,14},{13,1},{15,3... | collective-permute-start | bytes 196616 | tf_op jit(solution)/shard_map/ppermute | solution.py:300
  12.2 56.8 %all-to-all-start.2 = ((bf16[16,128,256]{2,1,0:T(8,128)(2,1)}), bf16[16,128,256]{2,1,0:T(8,128)(2,1)S(1)}, u32[]{:S(2)}, u32[]{:S(2)}) async-start(bf16[16,128,256]{2,1,0:T(8,128)(2,1)} %shard_map.62), calls=%async_computation.2 | async-start | bytes 2097152 | tf_op jit(solution)/shard_map/all_to_all | solution.py:306
  20.2 17.1 %collective-permute-start.6 = (bf16[128,512]{1,0:T(8,128)(2,1)S(1)}, bf16[128,512]{1,0:T(8,128)(2,1)S(1)}, u32[]{:S(2)}, u32[]{:S(2)}) collective-permute-start(bf16[128,512]{1,0:T(8,128)(2,1)S(1)} %get-tuple-element.11), channel_id=1, source_target_pairs={{0,16},{16,32},{32,48},{48,0},{64,80},{80,96},{96,112},{112,64},{1... | collective-permute-start | bytes 393224 | tf_op jit(solution)/shard_map/ppermute | solution.py:277
  22.2 21.9 %collective-permute-start.5 = (bf16[128,512]{1,0:T(8,128)(2,1)S(1)}, bf16[128,512]{1,0:T(8,128)(2,1)S(1)}, u32[]{:S(2)}, u32[]{:S(2)}) collective-permute-start(bf16[128,512]{1,0:T(8,128)(2,1)S(1)} %get-tuple-element.11), channel_id=1, source_target_pairs={{0,32},{16,48},{32,0},{48,16},{64,96},{80,112},{96,64},{112,80},{1... | collective-permute-start | bytes 393224 | tf_op jit(solution)/shard_map/ppermute | solution.py:277
  24.8 20.3 %collective-permute-start.4 = (bf16[128,512]{1,0:T(8,128)(2,1)S(1)}, bf16[128,512]{1,0:T(8,128)(2,1)S(1)}, u32[]{:S(2)}, u32[]{:S(2)}) collective-permute-start(bf16[128,512]{1,0:T(8,128)(2,1)S(1)} %get-tuple-element.11), channel_id=1, source_target_pairs={{0,48},{16,0},{32,16},{48,32},{64,112},{80,64},{96,80},{112,96},{1... | collective-permute-start | bytes 393224 | tf_op jit(solution)/shard_map/ppermute | solution.py:277
  33.2 13.0 %collective-permute-start.13 = (bf16[128,512]{1,0:T(8,128)(2,1)S(1)}, bf16[128,512]{1,0:T(8,128)(2,1)S(1)}, u32[]{:S(2)}, u32[]{:S(2)}) collective-permute-start(bf16[128,512]{1,0:T(8,128)(2,1)S(1)} %get-tuple-element.10), channel_id=1, source_target_pairs={{0,64},{16,80},{32,96},{48,112},{64,128},{80,144},{96,160},{112,17... | collective-permute-start | bytes 393224 | tf_op jit(solution)/shard_map/ppermute | solution.py:277
  34.7 12.7 %collective-permute-start.12 = (bf16[128,512]{1,0:T(8,128)(2,1)S(1)}, bf16[128,512]{1,0:T(8,128)(2,1)S(1)}, u32[]{:S(2)}, u32[]{:S(2)}) collective-permute-start(bf16[128,512]{1,0:T(8,128)(2,1)S(1)} %get-tuple-element.10), channel_id=1, source_target_pairs={{0,128},{16,144},{32,160},{48,176},{64,192},{80,208},{96,224},{112... | collective-permute-start | bytes 393224 | tf_op jit(solution)/shard_map/ppermute | solution.py:277
  37.3 10.0 %collective-permute-start.11 = (bf16[128,512]{1,0:T(8,128)(2,1)S(1)}, bf16[128,512]{1,0:T(8,128)(2,1)S(1)}, u32[]{:S(2)}, u32[]{:S(2)}) collective-permute-start(bf16[128,512]{1,0:T(8,128)(2,1)S(1)} %get-tuple-element.10), channel_id=1, source_target_pairs={{0,192},{16,208},{32,224},{48,240},{64,0},{80,16},{96,32},{112,48}... | collective-permute-start | bytes 393224 | tf_op jit(solution)/shard_map/ppermute | solution.py:277
  44.1 5.4 %collective-permute-start = (bf16[2,4096]{1,0:T(2,128)(2,1)S(1)}, bf16[2,4096]{1,0:T(2,128)(2,1)S(1)}, u32[]{:S(2)}, u32[]{:S(2)}) collective-permute-start(bf16[2,4096]{1,0:T(2,128)(2,1)S(1)} %convert_bitcast_fusion), channel_id=1, source_target_pairs={{0,2},{2,0},{4,6},{6,4},{8,10},{10,8},{12,14},{14,12},{1,3},{3,1},... | collective-permute-start | bytes 49160 | tf_op jit(solution)/shard_map/ppermute | solution.py:312
  45.2 23.8 %copy-start.2 = (bf16[4,128,512]{2,1,0:T(8,128)(2,1)}, bf16[4,128,512]{2,1,0:T(8,128)(2,1)S(1)}, u32[]{:S(2)}) copy-start(bf16[4,128,512]{2,1,0:T(8,128)(2,1)S(1)} %pad_maximum_fusion.refs_0_) | copy-start | bytes 1572868
  45.2 14.9 %collective-permute-start.7 = (bf16[4,128,512]{2,1,0:T(8,128)(2,1)S(1)}, bf16[4,128,512]{2,1,0:T(8,128)(2,1)S(1)}, u32[]{:S(2)}, u32[]{:S(2)}) collective-permute-start(bf16[4,128,512]{2,1,0:T(8,128)(2,1)S(1)} %pad_maximum_fusion.refs_0_), channel_id=1, source_target_pairs={{0,192},{16,208},{32,224},{48,240},{64,0},{80,16},{96,32},{112,48}... | collective-permute-start | bytes 1572872 | tf_op jit(solution)/shard_map/ppermute | solution.py:277
  46.1 13.9 %collective-permute-start.8 = (bf16[4,128,512]{2,1,0:T(8,128)(2,1)S(1)}, bf16[4,128,512]{2,1,0:T(8,128)(2,1)S(1)}, u32[]{:S(2)}, u32[]{:S(2)}) collective-permute-start(bf16[4,128,512]{2,1,0:T(8,128)(2,1)S(1)} %pad_maximum_fusion.refs_0_), channel_id=1, source_target_pairs={{0,64},{16,80},{32,96},{48,112},{64,128},{80,144},{96,160},{112,17... | collective-permute-start | bytes 1572872 | tf_op jit(solution)/shard_map/ppermute | solution.py:277
  47.4 21.7 %copy-start.3 = (bf16[4,128,512]{2,1,0:T(8,128)(2,1)}, bf16[4,128,512]{2,1,0:T(8,128)(2,1)S(1)}, u32[]{:S(2)}) copy-start(bf16[4,128,512]{2,1,0:T(8,128)(2,1)S(1)} %pad_maximum_fusion.1.refs_5_) | copy-start | bytes 1572868
  47.4 17.5 %collective-permute-start.14 = (bf16[4,128,512]{2,1,0:T(8,128)(2,1)S(1)}, bf16[4,128,512]{2,1,0:T(8,128)(2,1)S(1)}, u32[]{:S(2)}, u32[]{:S(2)}) collective-permute-start(bf16[4,128,512]{2,1,0:T(8,128)(2,1)S(1)} %pad_maximum_fusion.1.refs_5_), channel_id=1, source_target_pairs={{0,48},{16,0},{32,16},{48,32},{64,112},{80,64},{96,80},{112,96},{1... | collective-permute-start | bytes 1572872 | tf_op jit(solution)/shard_map/ppermute | solution.py:277
  48.4 15.7 %collective-permute-start.15 = (bf16[4,128,512]{2,1,0:T(8,128)(2,1)S(1)}, bf16[4,128,512]{2,1,0:T(8,128)(2,1)S(1)}, u32[]{:S(2)}, u32[]{:S(2)}) collective-permute-start(bf16[4,128,512]{2,1,0:T(8,128)(2,1)S(1)} %pad_maximum_fusion.1.refs_5_), channel_id=1, source_target_pairs={{0,16},{16,32},{32,48},{48,0},{64,80},{80,96},{96,112},{112,64},{1... | collective-permute-start | bytes 1572872 | tf_op jit(solution)/shard_map/ppermute | solution.py:277
  60.0 5.7 %copy-start.6 = (bf16[4,128,512]{2,1,0:T(8,128)(2,1)}, bf16[4,128,512]{2,1,0:T(8,128)(2,1)S(1)}, u32[]{:S(2)}) copy-start(bf16[4,128,512]{2,1,0:T(8,128)(2,1)S(1)} %collective-permute-done.8.refs_2_) | copy-start | bytes 1572868
  60.0 21.8 %collective-permute-start.9 = (bf16[2,128,512]{2,1,0:T(8,128)(2,1)S(1)}, bf16[2,128,512]{2,1,0:T(8,128)(2,1)}, u32[]{:S(2)}, u32[]{:S(2)}) collective-permute-start(bf16[2,128,512]{2,1,0:T(8,128)(2,1)S(1)} %slice.50), channel_id=1, source_target_pairs={{0,64},{16,80},{32,96},{48,112},{64,128},{80,144},{96,160},{112,17... | collective-permute-start | bytes 786440 | tf_op jit(solution)/shard_map/ppermute | solution.py:277
  60.1 8.9 %copy-start.5 = (bf16[4,128,512]{2,1,0:T(8,128)(2,1)}, bf16[4,128,512]{2,1,0:T(8,128)(2,1)S(1)}, u32[]{:S(2)}) copy-start(bf16[4,128,512]{2,1,0:T(8,128)(2,1)S(1)} %collective-permute-done.7.refs_1_) | copy-start | bytes 1572868
  61.0 20.8 %collective-permute-start.10 = (bf16[2,128,512]{2,1,0:T(8,128)(2,1)}, bf16[2,128,512]{2,1,0:T(8,128)(2,1)}, u32[]{:S(2)}, u32[]{:S(2)}) collective-permute-start(bf16[2,128,512]{2,1,0:T(8,128)(2,1)} %slice.51), channel_id=1, source_target_pairs={{0,192},{16,208},{32,224},{48,240},{64,0},{80,16},{96,32},{112,48}... | collective-permute-start | bytes 786440 | tf_op jit(solution)/shard_map/ppermute | solution.py:277
  64.1 1.5 %copy-start.8 = (bf16[4,128,512]{2,1,0:T(8,128)(2,1)}, bf16[4,128,512]{2,1,0:T(8,128)(2,1)S(1)}, u32[]{:S(2)}) copy-start(bf16[4,128,512]{2,1,0:T(8,128)(2,1)S(1)} %collective-permute-done.15.refs_7_) | copy-start | bytes 1572868
  64.9 16.9 %collective-permute-start.16 = (bf16[2,128,512]{2,1,0:T(8,128)(2,1)}, bf16[2,128,512]{2,1,0:T(8,128)(2,1)}, u32[]{:S(2)}, u32[]{:S(2)}) collective-permute-start(bf16[2,128,512]{2,1,0:T(8,128)(2,1)} %slice.53), channel_id=1, source_target_pairs={{0,16},{16,32},{32,48},{48,0},{64,80},{80,96},{96,112},{112,64},{1... | collective-permute-start | bytes 786440 | tf_op jit(solution)/shard_map/ppermute | solution.py:277
  64.9 0.9 copy-start.7
  65.8 16.0 %collective-permute-start.17 = (bf16[2,128,512]{2,1,0:T(8,128)(2,1)}, bf16[2,128,512]{2,1,0:T(8,128)(2,1)}, u32[]{:S(2)}, u32[]{:S(2)}) collective-permute-start(bf16[2,128,512]{2,1,0:T(8,128)(2,1)} %slice.54), channel_id=1, source_target_pairs={{0,48},{16,0},{32,16},{48,32},{64,112},{80,64},{96,80},{112,96},{1... | collective-permute-start | bytes 786440 | tf_op jit(solution)/shard_map/ppermute | solution.py:277
  69.0 3.7 %copy-start = (bf16[16,128,256]{2,1,0:T(8,128)(2,1)}, bf16[16,128,256]{2,1,0:T(8,128)(2,1)S(1)}, u32[]{:S(2)}) copy-start(bf16[16,128,256]{2,1,0:T(8,128)(2,1)S(1)} %all-to-all-done.2.y_ref) | copy-start | bytes 3145732
  69.1 22.1 %all-to-all-start = ((bf16[16,128,256]{2,1,0:T(8,128)(2,1)}), bf16[16,128,256]{2,1,0:T(8,128)(2,1)S(1)}, u32[]{:S(2)}, u32[]{:S(2)}) async-start(bf16[16,128,256]{2,1,0:T(8,128)(2,1)} %shard_map.59), calls=%async_computation | async-start | bytes 2097152 | tf_op jit(solution)/shard_map/all_to_all | solution.py:307
  91.0 19.5 %collective-permute-start.18 = (bf16[4,64,1024]{2,0,1:T(4,128)(2,1)S(1)}, bf16[4,64,1024]{2,0,1:T(4,128)(2,1)S(1)}, u32[]{:S(2)}, u32[]{:S(2)}) collective-permute-start(bf16[4,64,1024]{2,0,1:T(4,128)(2,1)S(1)} %bitcast.45), channel_id=1, source_target_pairs={{0,1},{1,0},{2,3},{3,2},{4,5},{5,4},{6,7},{7,6},{8,9},{9,8},{10,11... | collective-permute-start | bytes 1572872 | tf_op jit(solution)/shard_map/ppermute | solution.py:329
  91.1 1.0 copy-start.1
  98.6 33.1 %all-to-all-start.1 = ((bf16[128,16,128]{2,1,0:T(8,128)(2,1)}), bf16[128,16,128]{2,1,0:T(8,128)(2,1)S(1)}, u32[]{:S(2)}, u32[]{:S(2)}) async-start(bf16[128,16,128]{2,1,0:T(8,128)(2,1)} %shard_map.61), calls=%async_computation.1 | async-start | bytes 1048576 | tf_op jit(solution)/shard_map/all_to_all | solution.py:321
  111.3 17.2 %collective-permute-start.19 = (bf16[2,64,1024]{2,0,1:T(2,128)(2,1)S(1)}, bf16[2,64,1024]{2,0,1:T(2,128)(2,1)S(1)}, u32[]{:S(2)}, u32[]{:S(2)}) collective-permute-start(bf16[2,64,1024]{2,0,1:T(2,128)(2,1)S(1)} %slice.65), channel_id=1, source_target_pairs={{0,2},{2,0},{4,6},{6,4},{8,10},{10,8},{12,14},{14,12},{1,3},{3,1},... | collective-permute-start | bytes 786440 | tf_op jit(solution)/shard_map/ppermute | solution.py:330

commit v3 on v2

--- a/solution.py
+++ b/solution.py
@@ -9,16 +9,15 @@
 
 BF = jnp.bfloat16
 F32 = jnp.float32
-VMEM_LIMIT = 56 * 1024 * 1024
-SIDE = 4
+VMEM_LIMIT = 16 * 1024 * 1024
 
 
 def params():
     return pltpu.CompilerParams(vmem_limit_bytes=VMEM_LIMIT)
 
 
-def cost(flops, data):
-    return pl.CostEstimate(flops=flops, bytes_accessed=data, transcendentals=0)
+def cost(microseconds):
+    return pl.CostEstimate(flops=0, bytes_accessed=int(microseconds * 3.6e6), transcendentals=0)
 
 
 def turn_kernel(x_ref, y_ref):
@@ -39,7 +38,7 @@
         in_specs=[pl.BlockSpec((tokens, width // steps), lambda s: (0, s))],
         out_specs=pl.BlockSpec((n_chunk // steps, own, tokens), lambda s: (s, 0, 0)),
         compiler_params=params(),
-        cost_estimate=cost(0, 4 * tokens * width),
+        cost_estimate=cost(2.3),
     )(x)
 
 
@@ -49,7 +48,7 @@
     sub = cols // per
     x = x_ref[...]
     for k in range(count):
-        u = jnp.dot(x, w_ref[k], preferred_element_type=F32).T.astype(BF)
+        u = jnp.dot(x, w_ref[k], preferred_element_type=F32).astype(BF).T
         for c in range(per):
             y_ref[c, k * sub : (k + 1) * sub, :] = u[c * sub : (c + 1) * sub]
 
@@ -69,7 +68,7 @@
         ],
         out_specs=pl.BlockSpec((n_chunk // steps, rows, tokens), lambda s: (s, 0, 0)),
         compiler_params=params(),
-        cost_estimate=cost(2 * tokens * width * count * out_width, 2 * count * width * out_width),
+        cost_estimate=cost(7),
     )(x, w)
 
 
@@ -120,7 +119,7 @@
         functools.partial(out_table_kernel, block),
         out_shape=jax.ShapeDtypeStruct((count, length, block), BF),
         compiler_params=params(),
-        cost_estimate=cost(0, 2 * count * length * block),
+        cost_estimate=cost(3.6),
     )(f)
 
 
@@ -130,7 +129,7 @@
         functools.partial(feature_table_kernel, block),
         out_shape=jax.ShapeDtypeStruct((length, count * block // 2), BF),
         compiler_params=params(),
-        cost_estimate=cost(0, count * length * block),
+        cost_estimate=cost(5),
     )(f)
 
 
@@ -174,7 +173,7 @@
         out_shape=jax.ShapeDtypeStruct((n * parts, block // parts // 2, 2 * sub), BF),
         scratch_shapes=[pltpu.VMEM((count, block, n * block), BF)],
         compiler_params=params(),
-        cost_estimate=cost(2 * count * sub * (n * block) ** 2, 2 * count * n * block * block),
+        cost_estimate=cost(6.5),
     )(y, z)
 
 
@@ -210,78 +209,85 @@
         out_shape=jax.ShapeDtypeStruct((count * width, length // 2), BF),
         scratch_shapes=[pltpu.VMEM((block, length), BF)],
         compiler_params=params(),
-        cost_estimate=cost(count * width * length * length, 2 * length * cols),
+        cost_estimate=cost(9),
     )(y, z)
 
 
-def grad_kernel(place_ref, f_ref, *refs):
-    pieces, out_ref, grad_ref, sem = refs[:-3], refs[-3], refs[-2], refs[-1]
-    half_rows = grad_ref.shape[0] // (SIDE * SIDE)
-    half_cols = grad_ref.shape[1] // 2
-    y, x = place_ref[0], place_ref[1]
+def grad_kernel(steps, core_ref, f_hbm, g_hbm, rest_ref, mine_ref, f_ref, g_ref, acc_ref, sem):
+    count, own, _ = mine_ref.shape
+    rows, length = f_ref.shape
+    depth = length // steps
+    core = core_ref[0]
     copies = []
-    for side, group in enumerate((pieces[:5], pieces[5:])):
-        for far in range(SIDE):
-            for near in range(SIDE):
-                if far == 0:
-                    ref, index = group[0], near
-                elif far == 1:
-                    ref, index = group[1], near
-                elif far == SIDE - 1:
-                    ref, index = group[2], near
-                elif near < SIDE // 2:
-                    ref, index = group[3], near
-                else:
-                    ref, index = group[4], near - SIDE // 2
-                dy, dx = (far, near) if side == 0 else (near, far)
-                block = lax.rem(y + dy, SIDE) * SIDE + lax.rem(x + dx, SIDE)
-                rows = pl.ds(pl.multiple_of(block * half_rows, half_rows), half_rows)
-                copies.append(
-                    pltpu.make_async_copy(
-                        ref.at[index], grad_ref.at[rows, side * half_cols : (side + 1) * half_cols], sem.at[len(copies)]
-                    )
-                )
-    for copy in copies:
-        copy.start()
-    for copy in copies:
-        copy.wait()
-    count = out_ref.shape[0]
-    rows = f_ref.shape[0] // count
-    for k in range(count):
-        out_ref[k] = jnp.dot(f_ref[k * rows : (k + 1) * rows, :], grad_ref[...], preferred_element_type=F32).astype(BF)
-
-
-def grad(f, pieces, place, count, out_width):
+    for s in range(steps):
+        at = pl.ds(s * depth, depth)
+        copies.append(
+            (
+                pltpu.make_async_copy(f_hbm.at[:, at], f_ref.at[:, at], sem.at[2 * s]),
+                pltpu.make_async_copy(g_hbm.at[at, :], g_ref.at[at, :], sem.at[2 * s + 1]),
+            )
+        )
+    for group in copies:
+        for copy in group:
+            copy.start()
+    for s in range(steps):
+        for copy in copies[s]:
+            copy.wait()
+        at = slice(s * depth, (s + 1) * depth)
+        part = jnp.dot(f_ref[:, at], g_ref[at, :], preferred_element_type=F32)
+        if s:
+            part += acc_ref[...]
+        acc_ref[...] = part
+    for k in range(count):
+        for which, out_ref in ((1 - core, rest_ref), (core, mine_ref)):
+            start = pl.multiple_of((2 * k + which) * own, own)
+            out_ref[k] = acc_ref[pl.ds(start, own), :].astype(BF)
+
+
+def grad(f, g, core, count):
     rows, length = f.shape
-    return pl.pallas_call(
-        grad_kernel,
-        out_shape=jax.ShapeDtypeStruct((count, rows // count, out_width), BF),
-        in_specs=[pl.BlockSpec(memory_space=pltpu.SMEM), pl.BlockSpec(memory_space=pltpu.VMEM)]
-        + [pl.BlockSpec(memory_space=pl.ANY)] * len(pieces),
-        scratch_shapes=[pltpu.VMEM((length, out_width), BF), pltpu.SemaphoreType.DMA((2 * SIDE * SIDE,))],
-        compiler_params=params(),
-        cost_estimate=cost(2 * rows * length * out_width, 2 * length * out_width),
-    )(place, f, *pieces)
-
-
-def shift(axis, step):
-    pairs = []
-    for y in range(SIDE):
-        for x in range(SIDE):
-            to = ((y + step) % SIDE, x) if axis == "y" else (y, (x + step) % SIDE)
-            pairs.append((y * SIDE + x, to[0] * SIDE + to[1]))
-    return pairs
-
-
-def move(a, axis, step):
-    return lax.ppermute(a, "seq", shift(axis, step))
-
-
-def plane_gather(a, near, far):
-    ring = jnp.stack([a, move(a, near, -1), move(a, near, 2), move(a, near, 1)])
-    after, before = move(ring, far, -1), move(ring, far, 1)
-    h = SIDE // 2
-    return [ring, after, before, move(before[:h], far, 1), move(after[h:], far, -1)]
+    cols = g.shape[1]
+    steps = 4
+    shape = jax.ShapeDtypeStruct((count, rows // count // 2, cols), BF)
+    return pl.pallas_call(
+        functools.partial(grad_kernel, steps),
+        out_shape=(shape, shape),
+        in_specs=[pl.BlockSpec(memory_space=pltpu.SMEM)] + [pl.BlockSpec(memory_space=pl.ANY)] * 2,
+        scratch_shapes=[
+            pltpu.VMEM((rows, length), BF),
+            pltpu.VMEM((length, cols), BF),
+            pltpu.VMEM((rows, cols), F32),
+            pltpu.SemaphoreType.DMA((2 * steps,)),
+        ],
+        compiler_params=params(),
+        cost_estimate=cost(5),
+    )(core, f, g)
+
+
+def finish_kernel(p_ref, o_ref):
+    n, parts, half, lanes = p_ref.shape
+    sub = lanes // 2
+    for i in range(n // 2):
+        pair = []
+        for s in range(2):
+            total = p_ref[2 * i + s, 0].astype(F32)
+            for j in range(1, parts):
+                total += p_ref[2 * i + s, j].astype(F32)
+            pair.append(total)
+        low = jnp.concatenate([pair[0][:, :sub], pair[1][:, :sub]], axis=1)
+        high = jnp.concatenate([pair[0][:, sub:], pair[1][:, sub:]], axis=1)
+        o_ref[:half, i * lanes : (i + 1) * lanes] = low.astype(BF)
+        o_ref[half:, i * lanes : (i + 1) * lanes] = high.astype(BF)
+
+
+def finish(p, n, parts):
+    _, half, lanes = p.shape
+    return pl.pallas_call(
+        finish_kernel,
+        out_shape=jax.ShapeDtypeStruct((2 * half, n * lanes // 2), BF),
+        compiler_params=params(),
+        cost_estimate=cost(1.8),
+    )(p.reshape(n, parts, half, lanes))
 
 
 def shards(n_seq, n_filt, inputs, filters, weights, cotangent):
@@ -292,23 +298,19 @@
     sub = out_width // n_seq
     own = width // n_seq
     piece = tokens // n_filt
-    at_seq, at_filt, at_dp = lax.axis_index("seq"), lax.axis_index("filt"), lax.axis_index("dp")
+    at_filt, at_dp = lax.axis_index("filt"), lax.axis_index("dp")
     parity = at_filt % 2
 
-    c = cotangent[0]
+    xt, c, fb = lax.optimization_barrier((turn(x, n_seq), cotangent[0], filters.T.astype(BF)))
+    xs = lax.all_to_all(xt, "seq", 0, 0, tiled=True)
+
     quads = [c] + [
         lax.ppermute(c, "filt", [((i + step) % n_filt, i) for i in range(n_filt)]) for step in (2, 4, 6)
     ]
-    stack = jnp.stack(quads + quads)
-    half = lax.dynamic_slice_in_dim(stack, (n_filt // 2 - at_filt // 2) % (n_filt // 2), n_filt // 2, 0)
+    half = lax.dynamic_slice_in_dim(jnp.stack(quads + quads), (n_filt // 2 - at_filt // 2) % (n_filt // 2), n_filt // 2, 0)
     half = jnp.stack([half[0], half[2], half[1], half[3]]).reshape(tokens // 2, out_width)
-
-    xs = lax.all_to_all(turn(x, n_seq), "seq", 0, 0, tiled=True)
-    us = lax.all_to_all(project(x, weights, n_seq), "seq", 0, 0, tiled=True)
-
-    pieces = plane_gather(half[:, : out_width // 2], "x", "y") + plane_gather(half[:, out_width // 2 :], "y", "x")
-
-    fb = filters.T.astype(BF)
+    full_grad = lax.all_gather(half, "seq", axis=0, tiled=True)
+
     other = lax.ppermute(fb, "filt", [(i, i ^ 1) for i in range(n_filt)])
     pad = ((0, 0), (tokens, tokens))
     pair = jnp.pad(jnp.concatenate([fb, other]).astype(F32), pad)
@@ -316,19 +318,21 @@
     z_out = out_table(jnp.pad(fb.astype(F32), ((0, 0), (tokens, 0))), length, tokens)
     z_feature = feature_table(pair, length, tokens)
 
+    u = project(x, weights, n_seq)
+    xs, u, z_out, z_feature = lax.optimization_barrier((xs, u, z_out, z_feature))
+    us = lax.all_to_all(u, "seq", 0, 0, tiled=True)
     f = feature_conv(xs, z_feature)
-    p = out_conv(us, z_out, n_filt)
+
+    us, z_out, f = lax.optimization_barrier((us, z_out, f))
+    p, f = lax.optimization_barrier((out_conv(us, z_out, n_filt), f))
     p = lax.all_to_all(p, ("seq", "filt"), 0, 0, tiled=True)
-    p = p.reshape(n_seq, n_filt, piece // 2, 2, sub).astype(F32).sum(axis=1)
-    outputs = p.transpose(2, 1, 0, 3).reshape(1, piece, out_width).astype(BF)
-
-    place = jnp.stack([at_seq // SIDE, at_seq % SIDE]).astype(jnp.int32)
-    g = grad(f, pieces, place, 2 * count, out_width).reshape(2 * count, 2, own // 2, out_width)
-    mine = lax.dynamic_index_in_dim(g, at_dp, 1, keepdims=False)
-    rest = lax.dynamic_index_in_dim(g, 1 - at_dp, 1, keepdims=False)
+
+    rest, mine = grad(f, full_grad, at_dp.astype(jnp.int32)[None], 2 * count)
     total = mine.astype(F32) + lax.ppermute(rest, "dp", [(0, 1), (1, 0)]).astype(F32)
-    back = lax.ppermute(total[count:].astype(BF), "filt", [(i, i ^ 1) for i in range(n_filt)])
+    send, p = lax.optimization_barrier((total[count:].astype(BF), p))
+    back = lax.ppermute(send, "filt", [(i, i ^ 1) for i in range(n_filt)])
     weight_grad = (total[:count] + back.astype(F32)).astype(BF).transpose(1, 0, 2)
+    outputs = finish(p, n_seq, n_filt)[None]
     return outputs, weight_grad
 
 

time: 136 us -> 125 us (0.919)
  starting transfers between devices: 57.6 us -> 35 us
  Pallas kernels: 40.5 us -> 23.3 us
  between operations: 1.02 us -> 14.2 us
  local copies, waits for them, and re-layouts: 6.91 us -> 17.9 us
  waiting for transfers between devices: 23.3 us -> 31.5 us
  other arithmetic: 5.41 us -> 1.87 us
    ppermute x15 -> x1, starting transfers between devices: 24.5 us -> 1.45 us  [shards(): back = lax.ppermute(send, 'filt', [(i, i ^ 1) for i in range(n_filt)])]
    ppermute x15 -> x1, waiting for transfers between devices: 21.1 us -> 4.15 us  [shards(): back = lax.ppermute(send, 'filt', [(i, i ^ 1) for i in range(n_filt)])]
    unnamed x27 -> x24, local copies, waits for them, and re-layouts: 1.23 us -> 17.9 us
    all_to_all x2, waiting for transfers between devices: 0.01 us -> 9.46 us  [the longest x1 7.86 us: shards(): us = lax.all_to_all(u, 'seq', 0, 0, tiled=True)]
    all_to_all x1, waiting for transfers between devices: 2.13 us -> 10.9 us  [shards(): p = lax.all_to_all(p, ('seq', 'filt'), 0, 0, tiled=True)]
    ppermute x3, waiting for transfers between devices: 0.01 us -> 5.07 us  [shards(): lax.ppermute(c, 'filt', [((i + step) % n_filt, i) for i in range(n_filt)])]
    pallas_call x1, Pallas kernels: 9.05 us -> 5.15 us  [feature_conv(): pl.pallas_call(feature_kernel, out_shape=jax.ShapeDtypeStruct((count * wi...]
    pallas_call x1 -> x2, Pallas kernels: 7.52 us -> 4.01 us  [the longest x1 3.24 us: grad(): pl.pallas_call(functools.partial(grad_kernel, steps), out_shape=(shape, s...]
  transfers between devices with their start and end apart: 23 -> 10, of which waited for: 3 -> 7; matrix products, arithmetic and copies ran while one was open for 6% -> 1% of each run, Pallas kernels for 30% -> 18%
where the time goes in v3:
time: 125 us; the launch traced here: 124 us
  starting transfers between devices  35 us (28%)
  waiting for transfers between devices  31.5 us (25%)
  Pallas kernels  23.3 us (19%)
  local copies, waits for them, and re-layouts  17.9 us (14%)
  between operations  14.2 us (11%)
  other arithmetic  1.87 us (1%)
    unnamed x24, local copies, waits for them, and re-layouts  17.9 us
    all_to_all x1, waiting for transfers between devices, shards(): p = lax.all_to_all(p, ('seq', 'filt'), 0, 0, tiled=True)  10.9 us
    all_to_all x1, starting transfers between devices, shards(): p = lax.all_to_all(p, ('seq', 'filt'), 0, 0, tiled=True)  10.6 us
    ppermute x3, starting transfers between devices, shards(): lax.ppermute(c, 'filt', [((i + step) % n_filt, i) for i in range(n_filt)])  9.29 us
    all_to_all x1, waiting for transfers between devices, shards(): us = lax.all_to_all(u, 'seq', 0, 0, tiled=True)  7.86 us
    all_to_all x1, starting transfers between devices, shards(): xs = lax.all_to_all(xt, 'seq', 0, 0, tiled=True)  6.83 us
    all_to_all x1, starting transfers between devices, shards(): us = lax.all_to_all(u, 'seq', 0, 0, tiled=True)  5.6 us
    pallas_call x1, Pallas kernels, feature_conv(): pl.pallas_call(feature_kernel, out_shape=jax.ShapeDtypeStruct((count * wi...  5.15 us
  transfers between devices with their start and end apart: 10, of which 7 were waited for; matrix products, arithmetic and copies ran while one was open for 1% of the time, Pallas kernels for 18%

profile of v3, /device:TPU:32, one launch (start us, length us, event | category | flops | bytes accessed | tf_op | source)
XLA Modules:
  0.0 123.8 jit_solution(4550874938373872506)
XLA Ops:
  7.2 0.0 all-gather.2.cloned.1.call-start
  7.2 0.0 copy-start.5
  7.2 1.2 copy-done.5
  8.4 1.3 %shard_map.59 = bf16[16,128,256]{2,1,0:T(8,128)(2,1)} custom-call(bf16[256,2048]{1,0:T(8,128)(2,1)S(1)} %bitcast.22), custom_call_target="tpu_custom_call" | custom-call | bytes 8279999 | tf_op jit(solution)/shard_map/pallas_call | solution.py:34
  9.7 0.8 convert_bitcast_fusion
  10.5 5.5 %collective-permute-start.1 = (bf16[32,1024]{1,0:T(8,128)(2,1)}, bf16[32,1024]{1,0:T(8,128)(2,1)S(1)}, u32[]{:S(2)}, u32[]{:S(2)}) collective-permute-start(bf16[32,1024]{1,0:T(8,128)(2,1)} %bitcast.26), channel_id=1, source_target_pairs={{4,0},{6,2},{8,4},{10,6},{12,8},{14,10},{0,12},{2,14},{5,1},{7,3},... | collective-permute-start | bytes 196616 | tf_op jit(solution)/shard_map/ppermute | solution.py:308
  16.0 1.4 %collective-permute-start.2 = (bf16[32,1024]{1,0:T(8,128)(2,1)}, bf16[32,1024]{1,0:T(8,128)(2,1)S(1)}, u32[]{:S(2)}, u32[]{:S(2)}) collective-permute-start(bf16[32,1024]{1,0:T(8,128)(2,1)} %bitcast.27), channel_id=1, source_target_pairs={{8,0},{10,2},{12,4},{14,6},{0,8},{2,10},{4,12},{6,14},{9,1},{11,3}... | collective-permute-start | bytes 196616 | tf_op jit(solution)/shard_map/ppermute | solution.py:308
  17.4 2.4 %collective-permute-start.3 = (bf16[32,1024]{1,0:T(8,128)(2,1)}, bf16[32,1024]{1,0:T(8,128)(2,1)S(1)}, u32[]{:S(2)}, u32[]{:S(2)}) collective-permute-start(bf16[32,1024]{1,0:T(8,128)(2,1)} %bitcast.28), channel_id=1, source_target_pairs={{12,0},{14,2},{0,4},{2,6},{4,8},{6,10},{8,12},{10,14},{13,1},{15,3... | collective-permute-start | bytes 196616 | tf_op jit(solution)/shard_map/ppermute | solution.py:308
  19.8 0.9 bitcast_dynamic-update-slice_fusion.6
  20.7 0.0 collective-permute-done.1
  20.7 3.9 %collective-permute-done.2 = bf16[32,1024]{1,0:T(8,128)(2,1)S(1)} collective-permute-done((bf16[32,1024]{1,0:T(8,128)(2,1)}, bf16[32,1024]{1,0:T(8,128)(2,1)S(1)}, u32[]{:S(2)}, u32[]{:S(2)}) %collective-permute-start.2) | collective-permute-done | bytes 65568 | tf_op jit(solution)/shard_map/ppermute | solution.py:308
  24.6 1.1 collective-permute-done.3
  25.8 0.8 bitcast_dynamic-update-slice_fusion.7
  26.7 0.7 pad_maximum_fusion
  27.4 0.0 all-gather.2.cloned.1.call-update
  27.5 6.8 %all-to-all-start = ((bf16[16,128,256]{2,1,0:T(8,128)(2,1)}), bf16[16,128,256]{2,1,0:T(8,128)(2,1)S(1)}, u32[]{:S(2)}, u32[]{:S(2)}) async-start(bf16[16,128,256]{2,1,0:T(8,128)(2,1)} %shard_map.59), calls=%async_computation | async-start | bytes 2097152 | tf_op jit(solution)/shard_map/all_to_all | solution.py:305
  34.3 1.1 collective-permute-start
  35.4 0.0 copy-start.4
  35.4 3.4 %copy-done.4 = bf16[2,2048,1024]{2,1,0:T(8,128)(2,1)S(1)} copy-done((bf16[2,2048,1024]{2,1,0:T(8,128)(2,1)S(1)}, bf16[2,2048,1024]{2,1,0:T(8,128)(2,1)}, u32[]{:S(2)}) %copy-start.4) | copy-done | bytes 8388632
  38.8 5.0 %shard_map.60 = bf16[16,128,256]{2,1,0:T(8,128)(2,1)} custom-call(bf16[256,2048]{1,0:T(8,128)(2,1)S(1)} %bitcast.23, bf16[2,2048,1024]{2,1,0:T(8,128)(2,1)S(1)} %copy-done.4), custom_call_target="tpu_custom_call" | custom-call | bytes 25200000 | tf_op jit(solution)/shard_map/pallas_call | solution.py:61
  43.8 0.8 shard_map.61.z_ref
  44.6 2.0 %copy-done.2 = bf16[2,4096,256]{2,1,0:T(8,128)(2,1)} copy-done((bf16[2,4096,256]{2,1,0:T(8,128)(2,1)}, bf16[2,4096,256]{2,1,0:T(8,128)(2,1)S(1)}, u32[]{:S(2)}) %copy-start.2) | copy-done | bytes 4194328
  46.6 0.0 collective-permute-done
  46.6 0.1 fusion.7.f_ref
  46.7 2.0 %shard_map.62.z_ref = bf16[4096,512]{1,0:T(8,128)(2,1)S(1)} custom-call(f32[4,4352]{1,0:T(4,128)S(1)} %fusion.7.f_ref), custom_call_target="tpu_custom_call" | custom-call | bytes 18000000 | tf_op jit(solution)/shard_map/pallas_call | solution.py:128
  48.7 0.0 copy-start
  48.7 2.0 %copy-done = bf16[4096,512]{1,0:T(8,128)(2,1)} copy-done((bf16[4096,512]{1,0:T(8,128)(2,1)}, bf16[4096,512]{1,0:T(8,128)(2,1)S(1)}, u32[]{:S(2)}) %copy-start) | copy-done | bytes 4194328
  50.7 1.6 %all-to-all-done.y_ref = bf16[16,128,256]{2,1,0:T(8,128)(2,1)S(1)} async-done(((bf16[16,128,256]{2,1,0:T(8,128)(2,1)}), bf16[16,128,256]{2,1,0:T(8,128)(2,1)S(1)}, u32[]{:S(2)}, u32[]{:S(2)}) %all-to-all-start) | async-done | bytes 1048608 | tf_op jit(solution)/shard_map/all_to_all | solution.py:305
  52.3 5.6 %all-to-all-start.1 = ((bf16[16,128,256]{2,1,0:T(8,128)(2,1)}), bf16[16,128,256]{2,1,0:T(8,128)(2,1)}, u32[]{:S(2)}, u32[]{:S(2)}) async-start(bf16[16,128,256]{2,1,0:T(8,128)(2,1)} %shard_map.60), calls=%async_computation.1 | async-start | bytes 2097152 | tf_op jit(solution)/shard_map/all_to_all | solution.py:323
  57.9 2.2 %copy-done.1 = bf16[4096,512]{1,0:T(8,128)(2,1)S(1)} copy-done((bf16[4096,512]{1,0:T(8,128)(2,1)S(1)}, bf16[4096,512]{1,0:T(8,128)(2,1)}, u32[]{:S(2)}) %copy-start.1) | copy-done | bytes 4194328
  60.1 5.2 %shard_map.63.f_hbm = bf16[512,2048]{1,0:T(8,128)(2,1)S(1)} custom-call(bf16[16,128,256]{2,1,0:T(8,128)(2,1)S(1)} %all-to-all-done.y_ref, bf16[4096,512]{1,0:T(8,128)(2,1)S(1)} %copy-done.1), custom_call_target="tpu_custom_call" | custom-call | bytes 32400000 | tf_op jit(solution)/shard_map/pallas_call | solution.py:207
  65.2 7.9 %all-to-all-done.1.y_ref = bf16[16,128,256]{2,1,0:T(8,128)(2,1)} async-done(((bf16[16,128,256]{2,1,0:T(8,128)(2,1)}), bf16[16,128,256]{2,1,0:T(8,128)(2,1)}, u32[]{:S(2)}, u32[]{:S(2)}) %all-to-all-start.1) | async-done | bytes 1048608 | tf_op jit(solution)/shard_map/all_to_all | solution.py:323
  73.1 2.2 %copy-done.3 = bf16[2,4096,256]{2,1,0:T(8,128)(2,1)S(1)} copy-done((bf16[2,4096,256]{2,1,0:T(8,128)(2,1)S(1)}, bf16[2,4096,256]{2,1,0:T(8,128)(2,1)}, u32[]{:S(2)}) %copy-start.3) | copy-done | bytes 4194328
  75.3 5.1 %shard_map.64 = bf16[128,16,128]{2,1,0:T(8,128)(2,1)} custom-call(bf16[16,128,256]{2,1,0:T(8,128)(2,1)} %all-to-all-done.1.y_ref, bf16[2,4096,256]{2,1,0:T(8,128)(2,1)S(1)} %copy-done.3), custom_call_target="tpu_custom_call" | custom-call | bytes 23400000 | tf_op jit(solution)/shard_map/pallas_call | solution.py:171
  80.4 10.6 %all-to-all-start.2 = ((bf16[128,16,128]{2,1,0:T(8,128)(2,1)}), bf16[128,16,128]{2,1,0:T(8,128)(2,1)S(1)}, u32[]{:S(2)}, u32[]{:S(2)}) async-start(bf16[128,16,128]{2,1,0:T(8,128)(2,1)} %shard_map.64), calls=%async_computation.2 | async-start | bytes 1048576 | tf_op jit(solution)/shard_map/all_to_all | solution.py:328
  91.0 0.0 all-gather.2.cloned.1.call-done.g_hbm
  91.1 0.0 copy-start.7
  91.1 2.2 %copy-done.7 = bf16[2048,1024]{1,0:T(8,128)(2,1)S(1)} copy-done((bf16[2048,1024]{1,0:T(8,128)(2,1)S(1)}, bf16[2048,1024]{1,0:T(8,128)(2,1)}, u32[]{:S(2)}) %copy-start.7) | copy-done | bytes 4194328
  93.3 3.2 %shard_map.65 = (bf16[4,64,1024]{2,1,0:T(8,128)(2,1)S(1)}, bf16[4,64,1024]{2,1,0:T(8,128)(2,1)S(1)}) custom-call(s32[1]{0:T(128)} %bitcast.core_ref, bf16[512,2048]{1,0:T(8,128)(2,1)S(1)} %shard_map.63.f_hbm, bf16[2048,1024]{1,0:T(8,128)(2,1)S(1)} %copy-done.7), custom_call_target="tpu_custom_call" | custom-call | bytes 18000000 | tf_op jit(solution)/shard_map/pallas_call | solution.py:252
  96.5 0.1 collective-permute-start.4
  96.6 1.9 %collective-permute-done.4 = bf16[4,64,1024]{2,1,0:T(8,128)(2,1)S(1)} collective-permute-done((bf16[4,64,1024]{2,1,0:T(8,128)(2,1)S(1)}, bf16[4,64,1024]{2,1,0:T(8,128)(2,1)S(1)}, u32[]{:S(2)}, u32[]{:S(2)}) %collective-permute-start.4) | collective-permute-done | bytes 524320 | tf_op jit(solution)/shard_map/ppermute | solution.py:331
  98.5 0.2 convert_add_fusion
  98.7 10.9 %all-to-all-done.2 = bf16[128,16,128]{2,1,0:T(8,128)(2,1)S(1)} async-done(((bf16[128,16,128]{2,1,0:T(8,128)(2,1)}), bf16[128,16,128]{2,1,0:T(8,128)(2,1)S(1)}, u32[]{:S(2)}, u32[]{:S(2)}) %all-to-all-start.2) | async-done | bytes 524320 | tf_op jit(solution)/shard_map/all_to_all | solution.py:328
  109.6 1.5 %collective-permute-start.5 = (bf16[2,64,1024]{2,1,0:T(8,128)(2,1)S(1)}, bf16[2,64,1024]{2,1,0:T(8,128)(2,1)S(1)}, u32[]{:S(2)}, u32[]{:S(2)}) collective-permute-start(bf16[2,64,1024]{2,1,0:T(8,128)(2,1)S(1)} %slice.33), channel_id=1, source_target_pairs={{0,2},{2,0},{4,6},{6,4},{8,10},{10,8},{12,14},{14,12},{1,3},{3,1},... | collective-permute-start | bytes 786440 | tf_op jit(solution)/shard_map/ppermute | solution.py:333
  111.0 0.8 shard_map.66
  111.8 4.2 %collective-permute-done.5 = bf16[2,64,1024]{2,1,0:T(8,128)(2,1)S(1)} collective-permute-done((bf16[2,64,1024]{2,1,0:T(8,128)(2,1)S(1)}, bf16[2,64,1024]{2,1,0:T(8,128)(2,1)S(1)}, u32[]{:S(2)}, u32[]{:S(2)}) %collective-permute-start.5) | collective-permute-done | bytes 262176 | tf_op jit(solution)/shard_map/ppermute | solution.py:333
  116.0 0.1 fusion.1
  116.0 1.0 copy.6
  (14 shorter events, 0.1 us)
Async XLA Ops:
  7.2 83.9 %all-gather.2.cloned.1.call-start = ((), (), s32[]{:S(2)}) async-start(), calls=%async_computation.3 | async-start | bytes 4456448 | tf_op jit(solution)/shard_map/all_gather | solution.py:312
  7.2 1.2 copy-start.5
  8.4 27.0 %copy-start.6 = (bf16[1,256,2048]{2,1,0:T(8,128)(2,1)S(1)}, bf16[1,256,2048]{2,1,0:T(8,128)(2,1)}, u32[]{:S(2)}) copy-start(bf16[1,256,2048]{2,1,0:T(8,128)(2,1)} %param.4) | copy-start | bytes 3145732
  10.5 10.2 %collective-permute-start.1 = (bf16[32,1024]{1,0:T(8,128)(2,1)}, bf16[32,1024]{1,0:T(8,128)(2,1)S(1)}, u32[]{:S(2)}, u32[]{:S(2)}) collective-permute-start(bf16[32,1024]{1,0:T(8,128)(2,1)} %bitcast.26), channel_id=1, source_target_pairs={{4,0},{6,2},{8,4},{10,6},{12,8},{14,10},{0,12},{2,14},{5,1},{7,3},... | collective-permute-start | bytes 196616 | tf_op jit(solution)/shard_map/ppermute | solution.py:308
  16.0 8.7 %collective-permute-start.2 = (bf16[32,1024]{1,0:T(8,128)(2,1)}, bf16[32,1024]{1,0:T(8,128)(2,1)S(1)}, u32[]{:S(2)}, u32[]{:S(2)}) collective-permute-start(bf16[32,1024]{1,0:T(8,128)(2,1)} %bitcast.27), channel_id=1, source_target_pairs={{8,0},{10,2},{12,4},{14,6},{0,8},{2,10},{4,12},{6,14},{9,1},{11,3}... | collective-permute-start | bytes 196616 | tf_op jit(solution)/shard_map/ppermute | solution.py:308
  17.4 8.3 %collective-permute-start.3 = (bf16[32,1024]{1,0:T(8,128)(2,1)}, bf16[32,1024]{1,0:T(8,128)(2,1)S(1)}, u32[]{:S(2)}, u32[]{:S(2)}) collective-permute-start(bf16[32,1024]{1,0:T(8,128)(2,1)} %bitcast.28), channel_id=1, source_target_pairs={{12,0},{14,2},{0,4},{2,6},{4,8},{6,10},{8,12},{10,14},{13,1},{15,3... | collective-permute-start | bytes 196616 | tf_op jit(solution)/shard_map/ppermute | solution.py:308
  27.5 24.8 %all-to-all-start = ((bf16[16,128,256]{2,1,0:T(8,128)(2,1)}), bf16[16,128,256]{2,1,0:T(8,128)(2,1)S(1)}, u32[]{:S(2)}, u32[]{:S(2)}) async-start(bf16[16,128,256]{2,1,0:T(8,128)(2,1)} %shard_map.59), calls=%async_computation | async-start | bytes 2097152 | tf_op jit(solution)/shard_map/all_to_all | solution.py:305
  34.3 12.3 %collective-permute-start = (bf16[2,4096]{1,0:T(2,128)(2,1)S(1)}, bf16[2,4096]{1,0:T(2,128)(2,1)S(1)}, u32[]{:S(2)}, u32[]{:S(2)}) collective-permute-start(bf16[2,4096]{1,0:T(2,128)(2,1)S(1)} %convert_bitcast_fusion), channel_id=1, source_target_pairs={{0,2},{2,0},{4,6},{6,4},{8,10},{10,8},{12,14},{14,12},{1,3},{3,1},... | collective-permute-start | bytes 49160 | tf_op jit(solution)/shard_map/ppermute | solution.py:314
  35.4 3.4 %copy-start.4 = (bf16[2,2048,1024]{2,1,0:T(8,128)(2,1)S(1)}, bf16[2,2048,1024]{2,1,0:T(8,128)(2,1)}, u32[]{:S(2)}) copy-start(bf16[2,2048,1024]{2,1,0:T(8,128)(2,1)} %w_ref.1) | copy-start | bytes 25165828
  44.6 2.0 %copy-start.2 = (bf16[2,4096,256]{2,1,0:T(8,128)(2,1)}, bf16[2,4096,256]{2,1,0:T(8,128)(2,1)S(1)}, u32[]{:S(2)}) copy-start(bf16[2,4096,256]{2,1,0:T(8,128)(2,1)S(1)} %shard_map.61.z_ref) | copy-start | bytes 12582916
  48.7 2.0 %copy-start = (bf16[4096,512]{1,0:T(8,128)(2,1)}, bf16[4096,512]{1,0:T(8,128)(2,1)S(1)}, u32[]{:S(2)}) copy-start(bf16[4096,512]{1,0:T(8,128)(2,1)S(1)} %shard_map.62.z_ref) | copy-start | bytes 12582916
  52.3 20.8 %all-to-all-start.1 = ((bf16[16,128,256]{2,1,0:T(8,128)(2,1)}), bf16[16,128,256]{2,1,0:T(8,128)(2,1)}, u32[]{:S(2)}, u32[]{:S(2)}) async-start(bf16[16,128,256]{2,1,0:T(8,128)(2,1)} %shard_map.60), calls=%async_computation.1 | async-start | bytes 2097152 | tf_op jit(solution)/shard_map/all_to_all | solution.py:323
  57.9 2.2 %copy-start.1 = (bf16[4096,512]{1,0:T(8,128)(2,1)S(1)}, bf16[4096,512]{1,0:T(8,128)(2,1)}, u32[]{:S(2)}) copy-start(bf16[4096,512]{1,0:T(8,128)(2,1)} %copy-done) | copy-start | bytes 12582916
  73.1 2.2 %copy-start.3 = (bf16[2,4096,256]{2,1,0:T(8,128)(2,1)S(1)}, bf16[2,4096,256]{2,1,0:T(8,128)(2,1)}, u32[]{:S(2)}) copy-start(bf16[2,4096,256]{2,1,0:T(8,128)(2,1)} %copy-done.2) | copy-start | bytes 12582916
  80.4 29.2 %all-to-all-start.2 = ((bf16[128,16,128]{2,1,0:T(8,128)(2,1)}), bf16[128,16,128]{2,1,0:T(8,128)(2,1)S(1)}, u32[]{:S(2)}, u32[]{:S(2)}) async-start(bf16[128,16,128]{2,1,0:T(8,128)(2,1)} %shard_map.64), calls=%async_computation.2 | async-start | bytes 1048576 | tf_op jit(solution)/shard_map/all_to_all | solution.py:328
  91.1 2.2 %copy-start.7 = (bf16[2048,1024]{1,0:T(8,128)(2,1)S(1)}, bf16[2048,1024]{1,0:T(8,128)(2,1)}, u32[]{:S(2)}) copy-start(bf16[2048,1024]{1,0:T(8,128)(2,1)} %all-gather.2.cloned.1.call-done.g_hbm) | copy-start | bytes 12582916
  96.5 2.0 %collective-permute-start.4 = (bf16[4,64,1024]{2,1,0:T(8,128)(2,1)S(1)}, bf16[4,64,1024]{2,1,0:T(8,128)(2,1)S(1)}, u32[]{:S(2)}, u32[]{:S(2)}) collective-permute-start(bf16[4,64,1024]{2,1,0:T(8,128)(2,1)S(1)} %get-tuple-element.30), channel_id=1, source_target_pairs={{0,1},{1,0},{2,3},{3,2},{4,5},{5,4},{6,7},{7,6},{8,9},{9,8},{10,11... | collective-permute-start | bytes 1572872 | tf_op jit(solution)/shard_map/ppermute | solution.py:331
  109.6 6.4 %collective-permute-start.5 = (bf16[2,64,1024]{2,1,0:T(8,128)(2,1)S(1)}, bf16[2,64,1024]{2,1,0:T(8,128)(2,1)S(1)}, u32[]{:S(2)}, u32[]{:S(2)}) collective-permute-start(bf16[2,64,1024]{2,1,0:T(8,128)(2,1)S(1)} %slice.33), channel_id=1, source_target_pairs={{0,2},{2,0},{4,6},{6,4},{8,10},{10,8},{12,14},{14,12},{1,3},{3,1},... | collective-permute-start | bytes 786440 | tf_op jit(solution)/shard_map/ppermute | solution.py:333
Sparse Core Ops, SparseCore 0:
  27.6 60.9 all-gather.1

commit v4 on v3

--- a/solution.py
+++ b/solution.py
@@ -10,10 +10,14 @@
 BF = jnp.bfloat16
 F32 = jnp.float32
 VMEM_LIMIT = 16 * 1024 * 1024
-
-
-def params():
-    return pltpu.CompilerParams(vmem_limit_bytes=VMEM_LIMIT)
+GRAD_LIMIT = 57 * 1024 * 1024
+
+
+DONE = jax.ShapeDtypeStruct((8, 128), F32)
+
+
+def params(limit=None):
+    return pltpu.CompilerParams(vmem_limit_bytes=limit or VMEM_LIMIT)
 
 
 def cost(microseconds):
@@ -38,7 +42,7 @@
         in_specs=[pl.BlockSpec((tokens, width // steps), lambda s: (0, s))],
         out_specs=pl.BlockSpec((n_chunk // steps, own, tokens), lambda s: (s, 0, 0)),
         compiler_params=params(),
-        cost_estimate=cost(2.3),
+        cost_estimate=cost(1.3),
     )(x)
 
 
@@ -68,11 +72,11 @@
         ],
         out_specs=pl.BlockSpec((n_chunk // steps, rows, tokens), lambda s: (s, 0, 0)),
         compiler_params=params(),
-        cost_estimate=cost(7),
+        cost_estimate=cost(0.01),
     )(x, w)
 
 
-def out_table_kernel(block, f_ref, z_ref):
+def fill_out_table(block, f_ref, z_ref):
     count, length, _ = z_ref.shape
     n = length // block
     for k in range(count):
@@ -86,7 +90,8 @@
                 z_ref[k, c * block + 16 * g : c * block + 16 * g + 16, :] = rows[:, (n - c) * block : (n - c + 1) * block]
 
 
-def feature_table_kernel(block, f_ref, z_ref):
+def feature_table_kernel(block, f_ref, z_ref, done_ref):
+    done_ref[...] = jnp.zeros_like(done_ref)
     length, cols = z_ref.shape
     count = f_ref.shape[0]
     half = cols // count
@@ -113,27 +118,20 @@
                 z_ref[c * block + 16 * g : c * block + 16 * g + 16, k * half : (k + 1) * half] = both.astype(BF)
 
 
-def out_table(f, length, block):
-    count = f.shape[0]
-    return pl.pallas_call(
-        functools.partial(out_table_kernel, block),
-        out_shape=jax.ShapeDtypeStruct((count, length, block), BF),
-        compiler_params=params(),
-        cost_estimate=cost(3.6),
-    )(f)
-
-
 def feature_table(f, length, block):
     count = f.shape[0]
     return pl.pallas_call(
         functools.partial(feature_table_kernel, block),
-        out_shape=jax.ShapeDtypeStruct((length, count * block // 2), BF),
-        compiler_params=params(),
-        cost_estimate=cost(5),
+        out_shape=(jax.ShapeDtypeStruct((length, count * block // 2), BF), DONE),
+        compiler_params=params(),
+        cost_estimate=cost(0.01),
     )(f)
 
 
-def out_conv_kernel(parts, y_ref, z_ref, p_ref, u_ref):
+def out_conv_kernel(parts, y_ref, f_ref, *refs):
+    p_ref, done_ref, u_ref, z_ref = refs[-4:]
+    fill_out_table(y_ref.shape[2], f_ref, z_ref)
+    done_ref[...] = jnp.zeros_like(done_ref)
     n, rows, block = y_ref.shape
     count = z_ref.shape[0]
     sub = rows // count
@@ -164,20 +162,22 @@
                 p_ref[i * parts + j] = jnp.concatenate([low, high], axis=1).astype(BF)
 
 
-def out_conv(y, z, parts):
+def out_conv(y, f, parts, after):
     n, rows, block = y.shape
-    count = z.shape[0]
+    count = f.shape[0]
     sub = rows // count
     return pl.pallas_call(
         functools.partial(out_conv_kernel, parts),
-        out_shape=jax.ShapeDtypeStruct((n * parts, block // parts // 2, 2 * sub), BF),
-        scratch_shapes=[pltpu.VMEM((count, block, n * block), BF)],
-        compiler_params=params(),
-        cost_estimate=cost(6.5),
-    )(y, z)
-
-
-def feature_kernel(y_ref, z_ref, f_ref, x_ref):
+        out_shape=(jax.ShapeDtypeStruct((n * parts, block // parts // 2, 2 * sub), BF), DONE),
+        in_specs=[pl.BlockSpec(memory_space=pltpu.VMEM)] * 2 + [pl.BlockSpec(memory_space=pl.ANY)] * len(after),
+        scratch_shapes=[pltpu.VMEM((count, block, n * block), BF), pltpu.VMEM((count, n * block, block), BF)],
+        compiler_params=params(),
+        cost_estimate=cost(5.0),
+    )(y, f, *after)
+
+
+def feature_kernel(y_ref, z_ref, f_ref, done_ref, x_ref):
+    done_ref[...] = jnp.zeros_like(done_ref)
     n, width, block = y_ref.shape
     length, cols = z_ref.shape
     half = block // 2
@@ -206,62 +206,65 @@
     count = cols // (block // 2)
     return pl.pallas_call(
         feature_kernel,
-        out_shape=jax.ShapeDtypeStruct((count * width, length // 2), BF),
+        out_shape=(jax.ShapeDtypeStruct((count * width, length // 2), BF), DONE),
         scratch_shapes=[pltpu.VMEM((block, length), BF)],
         compiler_params=params(),
-        cost_estimate=cost(9),
+        cost_estimate=cost(5.0),
     )(y, z)
 
 
-def grad_kernel(steps, core_ref, f_hbm, g_hbm, rest_ref, mine_ref, f_ref, g_ref, acc_ref, sem):
+def grad_kernel(steps, place_ref, f_hbm, g_hbm, _, rest_ref, mine_ref, f_ref, g_ref, acc_ref, sem):
     count, own, _ = mine_ref.shape
     rows, length = f_ref.shape
+    blocks, quarters, piece, width = g_ref.shape
     depth = length // steps
-    core = core_ref[0]
+    per = blocks // steps
+    core, first = place_ref[0], place_ref[1]
     copies = []
     for s in range(steps):
-        at = pl.ds(s * depth, depth)
-        copies.append(
-            (
-                pltpu.make_async_copy(f_hbm.at[:, at], f_ref.at[:, at], sem.at[2 * s]),
-                pltpu.make_async_copy(g_hbm.at[at, :], g_ref.at[at, :], sem.at[2 * s + 1]),
-            )
-        )
-    for group in copies:
-        for copy in group:
-            copy.start()
+        at = pl.ds(s * per, per)
+        group = [pltpu.make_async_copy(f_hbm.at[:, pl.ds(s * depth, depth)], f_ref.at[:, pl.ds(s * depth, depth)], sem.at[s, quarters])]
+        for r in range(quarters):
+            quarter = lax.rem(first + r, quarters)
+            to = lax.rem(quarter, 2) * 2 + quarter // 2
+            group.append(pltpu.make_async_copy(g_hbm.at[at, r], g_ref.at[at, to], sem.at[s, r]))
+        copies.append(group)
+    for copy in copies[0] + copies[1]:
+        copy.start()
     for s in range(steps):
         for copy in copies[s]:
             copy.wait()
+        if s + 2 < steps:
+            for copy in copies[s + 2]:
+                copy.start()
         at = slice(s * depth, (s + 1) * depth)
-        part = jnp.dot(f_ref[:, at], g_ref[at, :], preferred_element_type=F32)
-        if s:
-            part += acc_ref[...]
-        acc_ref[...] = part
-    for k in range(count):
-        for which, out_ref in ((1 - core, rest_ref), (core, mine_ref)):
-            start = pl.multiple_of((2 * k + which) * own, own)
-            out_ref[k] = acc_ref[pl.ds(start, own), :].astype(BF)
-
-
-def grad(f, g, core, count):
+        g = g_ref[s * per : (s + 1) * per].reshape(depth, width)
+        part = jnp.dot(f_ref[:, at], g, preferred_element_type=F32)
+        acc_ref[...] = part if s == 0 else acc_ref[...] + part
+    for k in range(count):
+        low, high = acc_ref[2 * k * own : (2 * k + 1) * own], acc_ref[(2 * k + 1) * own : (2 * k + 2) * own]
+        mine_ref[k] = jnp.where(core == 0, low, high).astype(BF)
+        rest_ref[k] = jnp.where(core == 0, high, low).astype(BF)
+
+
+def grad(f, g, place, count, after):
     rows, length = f.shape
-    cols = g.shape[1]
+    width = g.shape[-1]
     steps = 4
-    shape = jax.ShapeDtypeStruct((count, rows // count // 2, cols), BF)
+    shape = jax.ShapeDtypeStruct((count, rows // count // 2, width), BF)
     return pl.pallas_call(
         functools.partial(grad_kernel, steps),
         out_shape=(shape, shape),
-        in_specs=[pl.BlockSpec(memory_space=pltpu.SMEM)] + [pl.BlockSpec(memory_space=pl.ANY)] * 2,
+        in_specs=[pl.BlockSpec(memory_space=pltpu.SMEM)] + [pl.BlockSpec(memory_space=pl.ANY)] * 3,
         scratch_shapes=[
             pltpu.VMEM((rows, length), BF),
-            pltpu.VMEM((length, cols), BF),
-            pltpu.VMEM((rows, cols), F32),
-            pltpu.SemaphoreType.DMA((2 * steps,)),
+            pltpu.VMEM(g.shape, BF),
+            pltpu.VMEM((rows, width), F32),
+            pltpu.SemaphoreType.DMA((steps, g.shape[1] + 1)),
         ],
-        compiler_params=params(),
-        cost_estimate=cost(5),
-    )(core, f, g)
+        compiler_params=params(GRAD_LIMIT),
+        cost_estimate=cost(5.0),
+    )(place, f, g, after)
 
 
 def finish_kernel(p_ref, o_ref):
@@ -286,7 +289,7 @@
         finish_kernel,
         out_shape=jax.ShapeDtypeStruct((2 * half, n * lanes // 2), BF),
         compiler_params=params(),
-        cost_estimate=cost(1.8),
+        cost_estimate=cost(0.8),
     )(p.reshape(n, parts, half, lanes))
 
 
@@ -301,33 +304,34 @@
     at_filt, at_dp = lax.axis_index("filt"), lax.axis_index("dp")
     parity = at_filt % 2
 
-    xt, c, fb = lax.optimization_barrier((turn(x, n_seq), cotangent[0], filters.T.astype(BF)))
+    quads = [cotangent[0]] + [
+        lax.ppermute(cotangent[0], "filt", [((i + step) % n_filt, i) for i in range(n_filt)]) for step in (2, 4, 6)
+    ]
+
+    fb = filters.T.astype(BF)
+    xt, quads = lax.optimization_barrier((turn(x, n_seq), quads))
+    full_grad = lax.all_gather(jnp.concatenate(quads), "seq", axis=0, tiled=True)
+    full_grad = full_grad.reshape(n_seq, n_filt // 2, piece, out_width)
     xs = lax.all_to_all(xt, "seq", 0, 0, tiled=True)
-
-    quads = [c] + [
-        lax.ppermute(c, "filt", [((i + step) % n_filt, i) for i in range(n_filt)]) for step in (2, 4, 6)
-    ]
-    half = lax.dynamic_slice_in_dim(jnp.stack(quads + quads), (n_filt // 2 - at_filt // 2) % (n_filt // 2), n_filt // 2, 0)
-    half = jnp.stack([half[0], half[2], half[1], half[3]]).reshape(tokens // 2, out_width)
-    full_grad = lax.all_gather(half, "seq", axis=0, tiled=True)
 
     other = lax.ppermute(fb, "filt", [(i, i ^ 1) for i in range(n_filt)])
     pad = ((0, 0), (tokens, tokens))
     pair = jnp.pad(jnp.concatenate([fb, other]).astype(F32), pad)
     pair = lax.dynamic_slice_in_dim(pair, piece * parity, length + tokens, 1)
-    z_out = out_table(jnp.pad(fb.astype(F32), ((0, 0), (tokens, 0))), length, tokens)
-    z_feature = feature_table(pair, length, tokens)
+    alone = jnp.pad(fb.astype(F32), ((0, 0), (tokens, 0)))
+    z_feature, done_feature = feature_table(pair, length, tokens)
 
     u = project(x, weights, n_seq)
-    xs, u, z_out, z_feature = lax.optimization_barrier((xs, u, z_out, z_feature))
+    xs, u, *after = lax.optimization_barrier((xs, u, done_feature))
     us = lax.all_to_all(u, "seq", 0, 0, tiled=True)
-    f = feature_conv(xs, z_feature)
-
-    us, z_out, f = lax.optimization_barrier((us, z_out, f))
-    p, f = lax.optimization_barrier((out_conv(us, z_out, n_filt), f))
+    f, done_f = feature_conv(xs, z_feature)
+
+    us, *late = lax.optimization_barrier((us, done_f))
+    p, done_p = out_conv(us, alone, n_filt, after + late)
+    place = jnp.stack([at_dp, at_filt // 2]).astype(jnp.int32)
     p = lax.all_to_all(p, ("seq", "filt"), 0, 0, tiled=True)
 
-    rest, mine = grad(f, full_grad, at_dp.astype(jnp.int32)[None], 2 * count)
+    rest, mine = grad(f, full_grad, place, 2 * count, done_p)
     total = mine.astype(F32) + lax.ppermute(rest, "dp", [(0, 1), (1, 0)]).astype(F32)
     send, p = lax.optimization_barrier((total[count:].astype(BF), p))
     back = lax.ppermute(send, "filt", [(i, i ^ 1) for i in range(n_filt)])

time: 125 us -> 118 us (0.944)
  local copies, waits for them, and re-layouts: 17.9 us -> 11.2 us
  other arithmetic: 1.87 us -> 3.59 us
  waiting for transfers between devices: 31.5 us -> 29.8 us
  Pallas kernels: 23.3 us -> 24.8 us
    unnamed x24 -> x17, local copies, waits for them, and re-layouts: 17.9 us -> 11.1 us
    pallas_call x1, Pallas kernels: 3.24 us -> 5.98 us  [grad(): pl.pallas_call(functools.partial(grad_kernel, steps), out_shape=(shape, s...]
    all_to_all x1, waiting for transfers between devices: 1.6 us -> 4.3 us  [shards(): xs = lax.all_to_all(xt, 'seq', 0, 0, tiled=True)]
    all_to_all x1, starting transfers between devices: 5.6 us -> 3.65 us  [shards(): us = lax.all_to_all(u, 'seq', 0, 0, tiled=True)]
    all_to_all x1, waiting for transfers between devices: 7.86 us -> 5.95 us  [shards(): us = lax.all_to_all(u, 'seq', 0, 0, tiled=True)]
    ppermute x3, waiting for transfers between devices: 5.07 us -> 3.42 us  [shards(): lax.ppermute(cotangent[0], 'filt', [((i + step) % n_filt, i) for i in ran...]
    concatenate x0 -> x1, other arithmetic: none -> 1.56 us  [shards(): jnp.concatenate(quads)]
    all_to_all x1, waiting for transfers between devices: 10.9 us -> 9.55 us  [shards(): p = lax.all_to_all(p, ('seq', 'filt'), 0, 0, tiled=True)]
  transfers between devices with their start and end apart: 10 -> 10, of which waited for: 7 -> 8; matrix products, arithmetic and copies ran while one was open for 1% -> 2% of each run, Pallas kernels for 18% -> 21%
where the time goes in v4:
time: 118 us
  starting transfers between devices  34.2 us (29%)
  waiting for transfers between devices  29.8 us (25%)
  Pallas kernels  24.8 us (21%)
  between operations  14.2 us (12%)
  local copies, waits for them, and re-layouts  11.2 us (9%)
  other arithmetic  3.59 us (3%)
    all_to_all x1, starting transfers between devices, shards(): p = lax.all_to_all(p, ('seq', 'filt'), 0, 0, tiled=True)  11.8 us
    unnamed x17, local copies, waits for them, and re-layouts  11.1 us
    all_to_all x1, waiting for transfers between devices, shards(): p = lax.all_to_all(p, ('seq', 'filt'), 0, 0, tiled=True)  9.55 us
    ppermute x3, starting transfers between devices, shards(): lax.ppermute(cotangent[0], 'filt', [((i + step) % n_filt, i) for i in ran...  9.29 us
    all_to_all x1, starting transfers between devices, shards(): xs = lax.all_to_all(xt, 'seq', 0, 0, tiled=True)  6.83 us
    pallas_call x1, Pallas kernels, grad(): pl.pallas_call(functools.partial(grad_kernel, steps), out_shape=(shape, s...  5.98 us
    all_to_all x1, waiting for transfers between devices, shards(): us = lax.all_to_all(u, 'seq', 0, 0, tiled=True)  5.95 us
    pallas_call x1, Pallas kernels, feature_conv(): pl.pallas_call(feature_kernel, out_shape=(jax.ShapeDtypeStruct((count * w...  5.15 us
  transfers between devices with their start and end apart: 10, of which 8 were waited for; matrix products, arithmetic and copies ran while one was open for 2% of the time, Pallas kernels for 21%

profile of v4, /device:TPU:32, one launch (start us, length us, event | category | flops | bytes accessed | tf_op | source)
XLA Modules:
  0.0 117.7 jit_solution(7600674624235669586)
XLA Ops:
  7.2 0.0 all-gather.2.cloned.1.call-start
  7.2 5.5 %collective-permute-start = (bf16[32,1024]{1,0:T(8,128)(2,1)}, bf16[32,1024]{1,0:T(8,128)(2,1)S(1)}, u32[]{:S(2)}, u32[]{:S(2)}) collective-permute-start(bf16[32,1024]{1,0:T(8,128)(2,1)} %bitcast.16), channel_id=1, source_target_pairs={{4,0},{6,2},{8,4},{10,6},{12,8},{14,10},{0,12},{2,14},{5,1},{7,3},... | collective-permute-start | bytes 196616 | tf_op jit(solution)/shard_map/ppermute | solution.py:308
  12.7 1.4 %collective-permute-start.1 = (bf16[32,1024]{1,0:T(8,128)(2,1)}, bf16[32,1024]{1,0:T(8,128)(2,1)S(1)}, u32[]{:S(2)}, u32[]{:S(2)}) collective-permute-start(bf16[32,1024]{1,0:T(8,128)(2,1)} %bitcast.17), channel_id=1, source_target_pairs={{8,0},{10,2},{12,4},{14,6},{0,8},{2,10},{4,12},{6,14},{9,1},{11,3}... | collective-permute-start | bytes 196616 | tf_op jit(solution)/shard_map/ppermute | solution.py:308
  14.1 2.4 %collective-permute-start.2 = (bf16[32,1024]{1,0:T(8,128)(2,1)}, bf16[32,1024]{1,0:T(8,128)(2,1)S(1)}, u32[]{:S(2)}, u32[]{:S(2)}) collective-permute-start(bf16[32,1024]{1,0:T(8,128)(2,1)} %bitcast.18), channel_id=1, source_target_pairs={{12,0},{14,2},{0,4},{2,6},{4,8},{6,10},{8,12},{10,14},{13,1},{15,3... | collective-permute-start | bytes 196616 | tf_op jit(solution)/shard_map/ppermute | solution.py:308
  16.5 0.0 copy-start.3
  16.5 1.2 %copy-done.3 = bf16[1,256,2048]{2,1,0:T(8,128)(2,1)S(1)} copy-done((bf16[1,256,2048]{2,1,0:T(8,128)(2,1)S(1)}, bf16[1,256,2048]{2,1,0:T(8,128)(2,1)}, u32[]{:S(2)}) %copy-start.3) | copy-done | bytes 1048600
  17.7 0.0 copy-start.4
  17.7 1.3 %shard_map.59 = bf16[16,128,256]{2,1,0:T(8,128)(2,1)} custom-call(bf16[256,2048]{1,0:T(8,128)(2,1)S(1)} %bitcast.11), custom_call_target="tpu_custom_call" | custom-call | bytes 4680000 | tf_op jit(solution)/shard_map/pallas_call | solution.py:38
  19.0 0.0 collective-permute-done
  19.1 2.3 %collective-permute-done.1 = bf16[32,1024]{1,0:T(8,128)(2,1)S(1)} collective-permute-done((bf16[32,1024]{1,0:T(8,128)(2,1)}, bf16[32,1024]{1,0:T(8,128)(2,1)S(1)}, u32[]{:S(2)}, u32[]{:S(2)}) %collective-permute-start.1) | collective-permute-done | bytes 65568 | tf_op jit(solution)/shard_map/ppermute | solution.py:308
  21.3 1.1 collective-permute-done.2
  22.5 1.6 %pad_maximum_fusion = bf16[128,1024]{1,0:T(8,128)(2,1)} fusion(bf16[32,1024]{1,0:T(8,128)(2,1)S(1)} %collective-permute-done.2, bf16[32,1024]{1,0:T(8,128)(2,1)S(1)} %collective-permute-done.1, bf16[32,1024]{1,0:T(8,128)(2,1)S(1)} %collective-permute-done, bf16[32,1024]{1,0:T(8,128)(2,1)} %bitcast.19), kind=kLoop, calls=%fused_computation.5 | loop fusion | flops 1048576 | bytes 524288 | tf_op jit(solution)/shard_map/concatenate | solution.py:313
  24.0 0.0 all-gather.2.cloned.1.call-update
  24.0 6.8 %all-to-all-start = ((bf16[16,128,256]{2,1,0:T(8,128)(2,1)}), bf16[16,128,256]{2,1,0:T(8,128)(2,1)S(1)}, u32[]{:S(2)}, u32[]{:S(2)}) async-start(bf16[16,128,256]{2,1,0:T(8,128)(2,1)} %shard_map.59), calls=%async_computation | async-start | bytes 2097152 | tf_op jit(solution)/shard_map/all_to_all | solution.py:315
  30.9 0.0 copy-done.7
  30.9 1.0 collective-permute-start.3
  32.0 0.0 copy-done.4
  32.0 0.0 copy-start
  32.0 3.4 %copy-done = bf16[2,2048,1024]{2,1,0:T(8,128)(2,1)S(1)} copy-done((bf16[2,2048,1024]{2,1,0:T(8,128)(2,1)S(1)}, bf16[2,2048,1024]{2,1,0:T(8,128)(2,1)}, u32[]{:S(2)}) %copy-start) | copy-done | bytes 8388632
  35.4 5.0 %shard_map.60 = bf16[16,128,256]{2,1,0:T(8,128)(2,1)} custom-call(bf16[256,2048]{1,0:T(8,128)(2,1)S(1)} %bitcast.12, bf16[2,2048,1024]{2,1,0:T(8,128)(2,1)S(1)} %copy-done), custom_call_target="tpu_custom_call" | custom-call | bytes 36000 | tf_op jit(solution)/shard_map/pallas_call | solution.py:65
  40.3 0.0 collective-permute-done.3
  40.3 0.1 fusion.7.f_ref
  40.5 2.0 %shard_map.61 = (bf16[4096,512]{1,0:T(8,128)(2,1)S(1)}, f32[8,128]{1,0:T(8,128)S(1)}) custom-call(f32[4,4352]{1,0:T(4,128)S(1)} %fusion.7.f_ref), custom_call_target="tpu_custom_call" | custom-call | bytes 36000 | tf_op jit(solution)/shard_map/pallas_call | solution.py:123
  42.4 0.0 copy-start.1
  42.5 2.0 %copy-done.1 = bf16[4096,512]{1,0:T(8,128)(2,1)} copy-done((bf16[4096,512]{1,0:T(8,128)(2,1)}, bf16[4096,512]{1,0:T(8,128)(2,1)S(1)}, u32[]{:S(2)}) %copy-start.1) | copy-done | bytes 4194328
  44.5 4.3 %all-to-all-done.y_ref = bf16[16,128,256]{2,1,0:T(8,128)(2,1)S(1)} async-done(((bf16[16,128,256]{2,1,0:T(8,128)(2,1)}), bf16[16,128,256]{2,1,0:T(8,128)(2,1)S(1)}, u32[]{:S(2)}, u32[]{:S(2)}) %all-to-all-start) | async-done | bytes 1048608 | tf_op jit(solution)/shard_map/all_to_all | solution.py:315
  48.8 3.7 %all-to-all-start.1 = ((bf16[16,128,256]{2,1,0:T(8,128)(2,1)}), bf16[16,128,256]{2,1,0:T(8,128)(2,1)S(1)}, u32[]{:S(2)}, u32[]{:S(2)}) async-start(bf16[16,128,256]{2,1,0:T(8,128)(2,1)} %shard_map.60), calls=%async_computation.1 | async-start | bytes 2097152 | tf_op jit(solution)/shard_map/all_to_all | solution.py:326
  52.4 0.0 copy-start.2
  52.5 2.2 %copy-done.2 = bf16[4096,512]{1,0:T(8,128)(2,1)S(1)} copy-done((bf16[4096,512]{1,0:T(8,128)(2,1)S(1)}, bf16[4096,512]{1,0:T(8,128)(2,1)}, u32[]{:S(2)}) %copy-start.2) | copy-done | bytes 4194328
  54.6 5.2 %shard_map.62 = (bf16[512,2048]{1,0:T(8,128)(2,1)S(1)}, f32[8,128]{1,0:T(8,128)S(1)}) custom-call(bf16[16,128,256]{2,1,0:T(8,128)(2,1)S(1)} %all-to-all-done.y_ref, bf16[4096,512]{1,0:T(8,128)(2,1)S(1)} %copy-done.2), custom_call_target="tpu_custom_call" | custom-call | bytes 18000000 | tf_op jit(solution)/shard_map/pallas_call | solution.py:207
  59.8 0.0 copy-start.5
  59.8 1.4 %copy-done.5 = bf16[512,2048]{1,0:T(8,128)(2,1)} copy-done((bf16[512,2048]{1,0:T(8,128)(2,1)}, bf16[512,2048]{1,0:T(8,128)(2,1)S(1)}, u32[]{:S(2)}) %copy-start.5) | copy-done | bytes 2097176
  61.2 6.0 %all-to-all-done.1.y_ref = bf16[16,128,256]{2,1,0:T(8,128)(2,1)S(1)} async-done(((bf16[16,128,256]{2,1,0:T(8,128)(2,1)}), bf16[16,128,256]{2,1,0:T(8,128)(2,1)S(1)}, u32[]{:S(2)}, u32[]{:S(2)}) %all-to-all-start.1) | async-done | bytes 1048608 | tf_op jit(solution)/shard_map/all_to_all | solution.py:326
  67.1 4.6 %shard_map.63 = (bf16[128,16,128]{2,1,0:T(8,128)(2,1)}, f32[8,128]{1,0:T(8,128)S(1)}) custom-call(bf16[16,128,256]{2,1,0:T(8,128)(2,1)S(1)} %all-to-all-done.1.y_ref, f32[2,4352]{1,0:T(2,128)S(1)} %pad_convert_fusion.f_ref, f32[8,128]{1,0:T(8,128)S(1)} %get-tuple-element.34.refs_0_, f32[8,128]{1,0:T(8,128)S(1)} %get-tuple-element.35.refs_1_), custom_call_target="tpu_custom_call" | custom-call | bytes 18000000 | tf_op jit(solution)/shard_map/pallas_call | solution.py:169
  71.7 11.8 %all-to-all-start.2 = ((bf16[128,16,128]{2,1,0:T(8,128)(2,1)}), bf16[128,16,128]{2,1,0:T(8,128)(2,1)S(1)}, u32[]{:S(2)}, u32[]{:S(2)}) async-start(bf16[128,16,128]{2,1,0:T(8,128)(2,1)} %get-tuple-element.39), calls=%async_computation.2 | async-start | bytes 1048576 | tf_op jit(solution)/shard_map/all_to_all | solution.py:332
  83.5 0.6 pad_add_fusion.place_ref
  84.1 0.4 all-gather.2.cloned.1.call-done
  84.5 0.0 copy-done.6
  84.5 6.0 %shard_map.64 = (bf16[4,64,1024]{2,1,0:T(8,128)(2,1)}, bf16[4,64,1024]{2,1,0:T(8,128)(2,1)}) custom-call(s32[2]{0:T(128)} %pad_add_fusion.place_ref, bf16[512,2048]{1,0:T(8,128)(2,1)} %copy-done.5, bf16[16,4,32,1024]{3,2,1,0:T(8,128)(2,1)} %bitcast.14, f32[8,128]{1,0:T(8,128)} %copy-done.6), custom_call_target="tpu_custom_call" | custom-call | bytes 18000000 | tf_op jit(solution)/shard_map/pallas_call | solution.py:255
  90.5 0.1 collective-permute-start.4
  90.6 2.1 %collective-permute-done.4 = bf16[4,64,1024]{2,1,0:T(8,128)(2,1)S(1)} collective-permute-done((bf16[4,64,1024]{2,1,0:T(8,128)(2,1)}, bf16[4,64,1024]{2,1,0:T(8,128)(2,1)S(1)}, u32[]{:S(2)}, u32[]{:S(2)}) %collective-permute-start.4) | collective-permute-done | bytes 524320 | tf_op jit(solution)/shard_map/ppermute | solution.py:335
  92.7 1.2 %convert_add_fusion = f32[4,64,1024]{2,1,0:T(8,128)S(1)} fusion(bf16[4,64,1024]{2,1,0:T(8,128)(2,1)S(1)} %collective-permute-done.4, bf16[4,64,1024]{2,1,0:T(8,128)(2,1)} %get-tuple-element.37), kind=kLoop, calls=%fused_computation | loop fusion | flops 786432 | bytes 2097152 | tf_op jit(solution)/shard_map/add | solution.py:335
  93.9 9.5 %all-to-all-done.2 = bf16[128,16,128]{2,1,0:T(8,128)(2,1)S(1)} async-done(((bf16[128,16,128]{2,1,0:T(8,128)(2,1)}), bf16[128,16,128]{2,1,0:T(8,128)(2,1)S(1)}, u32[]{:S(2)}, u32[]{:S(2)}) %all-to-all-start.2) | async-done | bytes 524320 | tf_op jit(solution)/shard_map/all_to_all | solution.py:332
  103.5 1.5 %collective-permute-start.5 = (bf16[2,64,1024]{2,1,0:T(8,128)(2,1)S(1)}, bf16[2,64,1024]{2,1,0:T(8,128)(2,1)S(1)}, u32[]{:S(2)}, u32[]{:S(2)}) collective-permute-start(bf16[2,64,1024]{2,1,0:T(8,128)(2,1)S(1)} %slice.17), channel_id=1, source_target_pairs={{0,2},{2,0},{4,6},{6,4},{8,10},{10,8},{12,14},{14,12},{1,3},{3,1},... | collective-permute-start | bytes 786440 | tf_op jit(solution)/shard_map/ppermute | solution.py:337
  104.9 0.8 shard_map.65
  105.7 4.1 %collective-permute-done.5 = bf16[2,64,1024]{2,1,0:T(8,128)(2,1)S(1)} collective-permute-done((bf16[2,64,1024]{2,1,0:T(8,128)(2,1)S(1)}, bf16[2,64,1024]{2,1,0:T(8,128)(2,1)S(1)}, u32[]{:S(2)}, u32[]{:S(2)}) %collective-permute-start.5) | collective-permute-done | bytes 262176 | tf_op jit(solution)/shard_map/ppermute | solution.py:337
  109.9 0.1 fusion.1
  109.9 1.0 copy.6
  (5 shorter events, 0.1 us)
Async XLA Ops:
  7.2 77.3 %all-gather.2.cloned.1.call-start = ((), (), s32[]{:S(2)}) async-start(), calls=%async_computation.3 | async-start | bytes 4456448 | tf_op jit(solution)/shard_map/all_gather | solution.py:313
  7.2 11.8 %collective-permute-start = (bf16[32,1024]{1,0:T(8,128)(2,1)}, bf16[32,1024]{1,0:T(8,128)(2,1)S(1)}, u32[]{:S(2)}, u32[]{:S(2)}) collective-permute-start(bf16[32,1024]{1,0:T(8,128)(2,1)} %bitcast.16), channel_id=1, source_target_pairs={{4,0},{6,2},{8,4},{10,6},{12,8},{14,10},{0,12},{2,14},{5,1},{7,3},... | collective-permute-start | bytes 196616 | tf_op jit(solution)/shard_map/ppermute | solution.py:308
  12.7 8.7 %collective-permute-start.1 = (bf16[32,1024]{1,0:T(8,128)(2,1)}, bf16[32,1024]{1,0:T(8,128)(2,1)S(1)}, u32[]{:S(2)}, u32[]{:S(2)}) collective-permute-start(bf16[32,1024]{1,0:T(8,128)(2,1)} %bitcast.17), channel_id=1, source_target_pairs={{8,0},{10,2},{12,4},{14,6},{0,8},{2,10},{4,12},{6,14},{9,1},{11,3}... | collective-permute-start | bytes 196616 | tf_op jit(solution)/shard_map/ppermute | solution.py:308
  14.1 8.3 %collective-permute-start.2 = (bf16[32,1024]{1,0:T(8,128)(2,1)}, bf16[32,1024]{1,0:T(8,128)(2,1)S(1)}, u32[]{:S(2)}, u32[]{:S(2)}) collective-permute-start(bf16[32,1024]{1,0:T(8,128)(2,1)} %bitcast.18), channel_id=1, source_target_pairs={{12,0},{14,2},{0,4},{2,6},{4,8},{6,10},{8,12},{10,14},{13,1},{15,3... | collective-permute-start | bytes 196616 | tf_op jit(solution)/shard_map/ppermute | solution.py:308
  16.5 1.2 %copy-start.3 = (bf16[1,256,2048]{2,1,0:T(8,128)(2,1)S(1)}, bf16[1,256,2048]{2,1,0:T(8,128)(2,1)}, u32[]{:S(2)}) copy-start(bf16[1,256,2048]{2,1,0:T(8,128)(2,1)} %param.4) | copy-start | bytes 3145732
  17.7 13.2 %copy-start.7 = (f32[4096,2]{0,1:T(2,128)S(1)}, f32[4096,2]{0,1:T(2,128)}, u32[]{:S(2)}) copy-start(f32[4096,2]{0,1:T(2,128)} %param.5) | copy-start | bytes 98308
  17.7 14.2 %copy-start.4 = (bf16[1,256,2048]{2,1,0:T(8,128)(2,1)S(1)}, bf16[1,256,2048]{2,1,0:T(8,128)(2,1)}, u32[]{:S(2)}) copy-start(bf16[1,256,2048]{2,1,0:T(8,128)(2,1)} %param.4) | copy-start | bytes 3145732
  24.0 24.7 %all-to-all-start = ((bf16[16,128,256]{2,1,0:T(8,128)(2,1)}), bf16[16,128,256]{2,1,0:T(8,128)(2,1)S(1)}, u32[]{:S(2)}, u32[]{:S(2)}) async-start(bf16[16,128,256]{2,1,0:T(8,128)(2,1)} %shard_map.59), calls=%async_computation | async-start | bytes 2097152 | tf_op jit(solution)/shard_map/all_to_all | solution.py:315
  30.9 9.4 %collective-permute-start.3 = (bf16[2,4096]{1,0:T(2,128)(2,1)S(1)}, bf16[2,4096]{1,0:T(2,128)(2,1)S(1)}, u32[]{:S(2)}, u32[]{:S(2)}) collective-permute-start(bf16[2,4096]{1,0:T(2,128)(2,1)S(1)} %convert_bitcast_fusion), channel_id=1, source_target_pairs={{0,2},{2,0},{4,6},{6,4},{8,10},{10,8},{12,14},{14,12},{1,3},{3,1},... | collective-permute-start | bytes 49160 | tf_op jit(solution)/shard_map/ppermute | solution.py:317
  32.0 3.4 %copy-start = (bf16[2,2048,1024]{2,1,0:T(8,128)(2,1)S(1)}, bf16[2,2048,1024]{2,1,0:T(8,128)(2,1)}, u32[]{:S(2)}) copy-start(bf16[2,2048,1024]{2,1,0:T(8,128)(2,1)} %w_ref.1) | copy-start | bytes 25165828
  42.4 2.0 %copy-start.1 = (bf16[4096,512]{1,0:T(8,128)(2,1)}, bf16[4096,512]{1,0:T(8,128)(2,1)S(1)}, u32[]{:S(2)}) copy-start(bf16[4096,512]{1,0:T(8,128)(2,1)S(1)} %get-tuple-element.25.z_ref) | copy-start | bytes 12582916
  48.8 18.4 %all-to-all-start.1 = ((bf16[16,128,256]{2,1,0:T(8,128)(2,1)}), bf16[16,128,256]{2,1,0:T(8,128)(2,1)S(1)}, u32[]{:S(2)}, u32[]{:S(2)}) async-start(bf16[16,128,256]{2,1,0:T(8,128)(2,1)} %shard_map.60), calls=%async_computation.1 | async-start | bytes 2097152 | tf_op jit(solution)/shard_map/all_to_all | solution.py:326
  52.4 2.2 %copy-start.2 = (bf16[4096,512]{1,0:T(8,128)(2,1)S(1)}, bf16[4096,512]{1,0:T(8,128)(2,1)}, u32[]{:S(2)}) copy-start(bf16[4096,512]{1,0:T(8,128)(2,1)} %copy-done.1) | copy-start | bytes 12582916
  59.8 1.4 %copy-start.5 = (bf16[512,2048]{1,0:T(8,128)(2,1)}, bf16[512,2048]{1,0:T(8,128)(2,1)S(1)}, u32[]{:S(2)}) copy-start(bf16[512,2048]{1,0:T(8,128)(2,1)S(1)} %get-tuple-element.26.f_hbm) | copy-start | bytes 6291460
  71.7 12.8 %copy-start.6 = (f32[8,128]{1,0:T(8,128)}, f32[8,128]{1,0:T(8,128)S(1)}, u32[]{:S(2)}) copy-start(f32[8,128]{1,0:T(8,128)S(1)} %get-tuple-element.36._) | copy-start | bytes 12292
  71.7 31.8 %all-to-all-start.2 = ((bf16[128,16,128]{2,1,0:T(8,128)(2,1)}), bf16[128,16,128]{2,1,0:T(8,128)(2,1)S(1)}, u32[]{:S(2)}, u32[]{:S(2)}) async-start(bf16[128,16,128]{2,1,0:T(8,128)(2,1)} %get-tuple-element.39), calls=%async_computation.2 | async-start | bytes 1048576 | tf_op jit(solution)/shard_map/all_to_all | solution.py:332
  90.5 2.2 %collective-permute-start.4 = (bf16[4,64,1024]{2,1,0:T(8,128)(2,1)}, bf16[4,64,1024]{2,1,0:T(8,128)(2,1)S(1)}, u32[]{:S(2)}, u32[]{:S(2)}) collective-permute-start(bf16[4,64,1024]{2,1,0:T(8,128)(2,1)} %get-tuple-element.38), channel_id=1, source_target_pairs={{0,1},{1,0},{2,3},{3,2},{4,5},{5,4},{6,7},{7,6},{8,9},{9,8},{10,11... | collective-permute-start | bytes 1572872 | tf_op jit(solution)/shard_map/ppermute | solution.py:335
  103.5 6.4 %collective-permute-start.5 = (bf16[2,64,1024]{2,1,0:T(8,128)(2,1)S(1)}, bf16[2,64,1024]{2,1,0:T(8,128)(2,1)S(1)}, u32[]{:S(2)}, u32[]{:S(2)}) collective-permute-start(bf16[2,64,1024]{2,1,0:T(8,128)(2,1)S(1)} %slice.17), channel_id=1, source_target_pairs={{0,2},{2,0},{4,6},{6,4},{8,10},{10,8},{12,14},{14,12},{1,3},{3,1},... | collective-permute-start | bytes 786440 | tf_op jit(solution)/shard_map/ppermute | solution.py:337
Sparse Core Ops, SparseCore 0:
  24.2 60.2 all-gather.1

commit v5 on v4

--- a/solution.py
+++ b/solution.py
@@ -10,7 +10,8 @@
 BF = jnp.bfloat16
 F32 = jnp.float32
 VMEM_LIMIT = 16 * 1024 * 1024
-GRAD_LIMIT = 57 * 1024 * 1024
+WIDE_LIMIT = 56 * 1024 * 1024
+SIDE = 4
 
 
 DONE = jax.ShapeDtypeStruct((8, 128), F32)
@@ -71,8 +72,8 @@
             pl.BlockSpec((count, width, out_width // steps), lambda s: (0, 0, s)),
         ],
         out_specs=pl.BlockSpec((n_chunk // steps, rows, tokens), lambda s: (s, 0, 0)),
-        compiler_params=params(),
-        cost_estimate=cost(0.01),
+        compiler_params=params(WIDE_LIMIT),
+        cost_estimate=cost(7),
     )(x, w)
 
 
@@ -90,8 +91,7 @@
                 z_ref[k, c * block + 16 * g : c * block + 16 * g + 16, :] = rows[:, (n - c) * block : (n - c + 1) * block]
 
 
-def feature_table_kernel(block, f_ref, z_ref, done_ref):
-    done_ref[...] = jnp.zeros_like(done_ref)
+def fill_feature_table(block, f_ref, z_ref):
     length, cols = z_ref.shape
     count = f_ref.shape[0]
     half = cols // count
@@ -116,16 +116,6 @@
                 start = (n - c) * block
                 both = jnp.where(first, a[:, start : start + half], b[:, start + half : start + 2 * half])
                 z_ref[c * block + 16 * g : c * block + 16 * g + 16, k * half : (k + 1) * half] = both.astype(BF)
-
-
-def feature_table(f, length, block):
-    count = f.shape[0]
-    return pl.pallas_call(
-        functools.partial(feature_table_kernel, block),
-        out_shape=(jax.ShapeDtypeStruct((length, count * block // 2), BF), DONE),
-        compiler_params=params(),
-        cost_estimate=cost(0.01),
-    )(f)
 
 
 def out_conv_kernel(parts, y_ref, f_ref, *refs):
@@ -176,9 +166,10 @@
     )(y, f, *after)
 
 
-def feature_kernel(y_ref, z_ref, f_ref, done_ref, x_ref):
+def feature_kernel(y_ref, taps_ref, f_ref, done_ref, x_ref, z_ref):
     done_ref[...] = jnp.zeros_like(done_ref)
     n, width, block = y_ref.shape
+    fill_feature_table(block, taps_ref, z_ref)
     length, cols = z_ref.shape
     half = block // 2
     count = cols // half
@@ -200,71 +191,82 @@
                 ]
 
 
-def feature_conv(y, z):
+def feature_conv(y, taps):
     n, width, block = y.shape
-    length, cols = z.shape
-    count = cols // (block // 2)
+    length = n * block
+    count = taps.shape[0]
     return pl.pallas_call(
         feature_kernel,
         out_shape=(jax.ShapeDtypeStruct((count * width, length // 2), BF), DONE),
-        scratch_shapes=[pltpu.VMEM((block, length), BF)],
+        scratch_shapes=[pltpu.VMEM((block, length), BF), pltpu.VMEM((length, count * block // 2), BF)],
         compiler_params=params(),
         cost_estimate=cost(5.0),
-    )(y, z)
-
-
-def grad_kernel(steps, place_ref, f_hbm, g_hbm, _, rest_ref, mine_ref, f_ref, g_ref, acc_ref, sem):
+    )(y, taps)
+
+
+def grad_kernel(place_ref, f_ref, *refs):
+    pieces, (rest_ref, mine_ref, grad_ref, sem) = refs[: 2 * SIDE], refs[-4:]
     count, own, _ = mine_ref.shape
-    rows, length = f_ref.shape
-    blocks, quarters, piece, width = g_ref.shape
-    depth = length // steps
-    per = blocks // steps
-    core, first = place_ref[0], place_ref[1]
+    half_rows = grad_ref.shape[1] // (SIDE * SIDE)
+    cols = grad_ref.shape[2]
+    y, x, core = place_ref[0], place_ref[1], place_ref[2]
     copies = []
-    for s in range(steps):
-        at = pl.ds(s * per, per)
-        group = [pltpu.make_async_copy(f_hbm.at[:, pl.ds(s * depth, depth)], f_ref.at[:, pl.ds(s * depth, depth)], sem.at[s, quarters])]
-        for r in range(quarters):
-            quarter = lax.rem(first + r, quarters)
-            to = lax.rem(quarter, 2) * 2 + quarter // 2
-            group.append(pltpu.make_async_copy(g_hbm.at[at, r], g_ref.at[at, to], sem.at[s, r]))
-        copies.append(group)
-    for copy in copies[0] + copies[1]:
+    for side in range(2):
+        for far in range(SIDE):
+            for near in range(SIDE):
+                dy, dx = (far, near) if side == 0 else (near, far)
+                block = lax.rem(y + SIDE - dy, SIDE) * SIDE + lax.rem(x + SIDE - dx, SIDE)
+                rows = pl.ds(pl.multiple_of(block * half_rows, half_rows), half_rows)
+                copies.append(
+                    pltpu.make_async_copy(
+                        pieces[side * SIDE + far].at[near], grad_ref.at[side, rows, :], sem.at[len(copies)]
+                    )
+                )
+    for copy in copies:
         copy.start()
-    for s in range(steps):
-        for copy in copies[s]:
+    for side in range(2):
+        for copy in copies[side * SIDE * SIDE : (side + 1) * SIDE * SIDE]:
             copy.wait()
-        if s + 2 < steps:
-            for copy in copies[s + 2]:
-                copy.start()
-        at = slice(s * depth, (s + 1) * depth)
-        g = g_ref[s * per : (s + 1) * per].reshape(depth, width)
-        part = jnp.dot(f_ref[:, at], g, preferred_element_type=F32)
-        acc_ref[...] = part if s == 0 else acc_ref[...] + part
-    for k in range(count):
-        low, high = acc_ref[2 * k * own : (2 * k + 1) * own], acc_ref[(2 * k + 1) * own : (2 * k + 2) * own]
-        mine_ref[k] = jnp.where(core == 0, low, high).astype(BF)
-        rest_ref[k] = jnp.where(core == 0, high, low).astype(BF)
-
-
-def grad(f, g, place, count, after):
+        part = jnp.dot(f_ref[...], grad_ref[side], preferred_element_type=F32).astype(BF)
+        at = slice(side * cols, (side + 1) * cols)
+        for k in range(count):
+            low, high = part[2 * k * own : (2 * k + 1) * own], part[(2 * k + 1) * own : (2 * k + 2) * own]
+            mine_ref[k, :, at] = jnp.where(core == 0, low, high)
+            rest_ref[k, :, at] = jnp.where(core == 0, high, low)
+
+
+def grad(f, pieces, place, count, out_width, after):
     rows, length = f.shape
-    width = g.shape[-1]
-    steps = 4
-    shape = jax.ShapeDtypeStruct((count, rows // count // 2, width), BF)
-    return pl.pallas_call(
-        functools.partial(grad_kernel, steps),
+    shape = jax.ShapeDtypeStruct((count, rows // count // 2, out_width), BF)
+    return pl.pallas_call(
+        grad_kernel,
         out_shape=(shape, shape),
-        in_specs=[pl.BlockSpec(memory_space=pltpu.SMEM)] + [pl.BlockSpec(memory_space=pl.ANY)] * 3,
+        in_specs=[pl.BlockSpec(memory_space=pltpu.SMEM), pl.BlockSpec(memory_space=pltpu.VMEM)]
+        + [pl.BlockSpec(memory_space=pl.ANY)] * (len(pieces) + 1),
         scratch_shapes=[
-            pltpu.VMEM((rows, length), BF),
-            pltpu.VMEM(g.shape, BF),
-            pltpu.VMEM((rows, width), F32),
-            pltpu.SemaphoreType.DMA((steps, g.shape[1] + 1)),
+            pltpu.VMEM((2, length, out_width // 2), BF),
+            pltpu.SemaphoreType.DMA((2 * SIDE * SIDE,)),
         ],
-        compiler_params=params(GRAD_LIMIT),
-        cost_estimate=cost(5.0),
-    )(place, f, g, after)
+        compiler_params=params(),
+        cost_estimate=cost(5),
+    )(place, f, *pieces, after)
+
+
+def shift(axis, step):
+    pairs = []
+    for y in range(SIDE):
+        for x in range(SIDE):
+            to = ((y + step) % SIDE, x) if axis == "y" else (y, (x + step) % SIDE)
+            pairs.append((y * SIDE + x, to[0] * SIDE + to[1]))
+    return pairs
+
+
+def step(a, axis, d):
+    return lax.ppermute(a, "seq", shift(axis, d))
+
+
+def ring(a, axis):
+    return [a] + [step(a, axis, d) for d in range(1, SIDE)]
 
 
 def finish_kernel(p_ref, o_ref):
@@ -301,7 +303,7 @@
     sub = out_width // n_seq
     own = width // n_seq
     piece = tokens // n_filt
-    at_filt, at_dp = lax.axis_index("filt"), lax.axis_index("dp")
+    at_seq, at_filt, at_dp = lax.axis_index("seq"), lax.axis_index("filt"), lax.axis_index("dp")
     parity = at_filt % 2
 
     quads = [cotangent[0]] + [
@@ -309,29 +311,37 @@
     ]
 
     fb = filters.T.astype(BF)
-    xt, quads = lax.optimization_barrier((turn(x, n_seq), quads))
-    full_grad = lax.all_gather(jnp.concatenate(quads), "seq", axis=0, tiled=True)
-    full_grad = full_grad.reshape(n_seq, n_filt // 2, piece, out_width)
-    xs = lax.all_to_all(xt, "seq", 0, 0, tiled=True)
-
+    xs = lax.all_to_all(turn(x, n_seq), "seq", 0, 0, tiled=True)
     other = lax.ppermute(fb, "filt", [(i, i ^ 1) for i in range(n_filt)])
+    u, quads, other = lax.optimization_barrier((project(x, weights, n_seq), quads, other))
+    half = lax.dynamic_slice_in_dim(jnp.stack(quads + quads), (n_filt // 2 - at_filt // 2) % (n_filt // 2), n_filt // 2, 0)
+    half = jnp.stack([half[0], half[2], half[1], half[3]]).reshape(tokens // 2, out_width)
+    left = ring(half[:, : out_width // 2], "x")
+    half = half[:, out_width // 2 :]
+    right = [half, step(half, "y", 1), step(half, "y", 3)]
+
     pad = ((0, 0), (tokens, tokens))
     pair = jnp.pad(jnp.concatenate([fb, other]).astype(F32), pad)
     pair = lax.dynamic_slice_in_dim(pair, piece * parity, length + tokens, 1)
     alone = jnp.pad(fb.astype(F32), ((0, 0), (tokens, 0)))
-    z_feature, done_feature = feature_table(pair, length, tokens)
-
-    u = project(x, weights, n_seq)
-    xs, u, *after = lax.optimization_barrier((xs, u, done_feature))
+
+    xs, u = lax.optimization_barrier((xs, u))
     us = lax.all_to_all(u, "seq", 0, 0, tiled=True)
-    f, done_f = feature_conv(xs, z_feature)
-
-    us, *late = lax.optimization_barrier((us, done_f))
-    p, done_p = out_conv(us, alone, n_filt, after + late)
-    place = jnp.stack([at_dp, at_filt // 2]).astype(jnp.int32)
+    f, done_f = feature_conv(xs, pair)
+
+    left, half, done_f = lax.optimization_barrier((left, half, done_f))
+    left = jnp.stack(left)
+    pieces = [left] + [step(left, "y", d) for d in range(1, SIDE)]
+    right.insert(2, step(half, "y", 2))
+
+    p, done_p = out_conv(us, alone, n_filt, [done_f])
+    right, done_p = lax.optimization_barrier((right, done_p))
+    right = jnp.stack(right)
+    pieces += [right] + [step(right, "x", d) for d in range(1, SIDE)]
     p = lax.all_to_all(p, ("seq", "filt"), 0, 0, tiled=True)
 
-    rest, mine = grad(f, full_grad, place, 2 * count, done_p)
+    place = jnp.stack([at_seq // SIDE, at_seq % SIDE, at_dp]).astype(jnp.int32)
+    rest, mine = grad(f, pieces, place, 2 * count, out_width, done_p)
     total = mine.astype(F32) + lax.ppermute(rest, "dp", [(0, 1), (1, 0)]).astype(F32)
     send, p = lax.optimization_barrier((total[count:].astype(BF), p))
     back = lax.ppermute(send, "filt", [(i, i ^ 1) for i in range(n_filt)])

time: 118 us -> 114 us (0.966); the launches traced: 118 us -> 112 us
  starting transfers between devices: 34.2 us -> 51.4 us
  between operations: 14.2 us -> 0.96 us
  local copies, waits for them, and re-layouts: 11.2 us -> 5.28 us
  waiting for transfers between devices: 29.8 us -> 26.1 us
  Pallas kernels: 24.8 us -> 26.3 us
  other arithmetic: 3.59 us -> 2.29 us
    ppermute x0 -> x12, starting transfers between devices: none -> 18.4 us  [step(): return lax.ppermute(a, 'seq', shift(axis, d))]
    ppermute x0 -> x12, waiting for transfers between devices: none -> 14.5 us  [step(): return lax.ppermute(a, 'seq', shift(axis, d))]
    all_to_all x1, waiting for transfers between devices: 9.55 us -> 0.01 us  [shards(): p = lax.all_to_all(p, ('seq', 'filt'), 0, 0, tiled=True)]
    unnamed x17 -> x18, local copies, waits for them, and re-layouts: 11.1 us -> 5.19 us
    all_to_all x1, waiting for transfers between devices: 5.95 us -> 1.34 us  [shards(): us = lax.all_to_all(u, 'seq', 0, 0, tiled=True)]
    all_to_all x1, starting transfers between devices: 11.8 us -> 8.25 us  [shards(): p = lax.all_to_all(p, ('seq', 'filt'), 0, 0, tiled=True)]
    ppermute x3, waiting for transfers between devices: 3.42 us -> 0.01 us  [shards(): lax.ppermute(cotangent[0], 'filt', [((i + step) % n_filt, i) for i in ran...]
    all_to_all x1, waiting for transfers between devices: 4.3 us -> 1.78 us  [shards(): xs = lax.all_to_all(turn(x, n_seq), 'seq', 0, 0, tiled=True)]
  transfers between devices with their start and end apart: 10 -> 21, of which waited for: 8 -> 8; matrix products, arithmetic and copies ran while one was open for 2% -> 2% of each run, Pallas kernels for 21% -> 23%
where the time goes in v5:
time: 114 us; the launch traced here: 112 us
  starting transfers between devices  51.4 us (45%)
  Pallas kernels  26.3 us (23%)
  waiting for transfers between devices  26.1 us (23%)
  local copies, waits for them, and re-layouts  5.28 us (5%)
  other arithmetic  2.29 us (2%)
    ppermute x12, starting transfers between devices, step(): return lax.ppermute(a, 'seq', shift(axis, d))  18.4 us
    ppermute x12, waiting for transfers between devices, step(): return lax.ppermute(a, 'seq', shift(axis, d))  14.5 us
    ppermute x3, starting transfers between devices, shards(): lax.ppermute(cotangent[0], 'filt', [((i + step) % n_filt, i) for i in ran...  10.5 us
    all_to_all x1, starting transfers between devices, shards(): p = lax.all_to_all(p, ('seq', 'filt'), 0, 0, tiled=True)  8.25 us
    pallas_call x1, Pallas kernels, grad(): pl.pallas_call(grad_kernel, out_shape=(shape, shape), in_specs=[pl.BlockS...  7.36 us
    all_to_all x1, starting transfers between devices, shards(): xs = lax.all_to_all(turn(x, n_seq), 'seq', 0, 0, tiled=True)  7.03 us
    pallas_call x1, Pallas kernels, project(): pl.pallas_call(project_kernel, grid=(steps,), out_shape=jax.ShapeDtypeStr...  6.8 us
    ppermute x1, waiting for transfers between devices, shards(): back = lax.ppermute(send, 'filt', [(i, i ^ 1) for i in range(n_filt)])  6.63 us
  transfers between devices with their start and end apart: 21, of which 8 were waited for; matrix products, arithmetic and copies ran while one was open for 2% of the time, Pallas kernels for 23%

profile of v5, /device:TPU:32, one launch (start us, length us, event | category | flops | bytes accessed | tf_op | source)
XLA Modules:
  0.0 112.4 jit_solution(964977741526812420)
XLA Ops:
  0.6 3.3 %collective-permute-start.2 = (bf16[32,1024]{1,0:T(8,128)(2,1)}, bf16[32,1024]{1,0:T(8,128)(2,1)S(1)}, u32[]{:S(2)}, u32[]{:S(2)}) collective-permute-start(bf16[32,1024]{1,0:T(8,128)(2,1)} %bitcast.38), channel_id=1, source_target_pairs={{12,0},{14,2},{0,4},{2,6},{4,8},{6,10},{8,12},{10,14},{13,1},{15,3... | collective-permute-start | bytes 196616 | tf_op jit(solution)/shard_map/ppermute | solution.py:310
  4.0 4.5 %collective-permute-start.1 = (bf16[32,1024]{1,0:T(8,128)(2,1)}, bf16[32,1024]{1,0:T(8,128)(2,1)S(1)}, u32[]{:S(2)}, u32[]{:S(2)}) collective-permute-start(bf16[32,1024]{1,0:T(8,128)(2,1)} %bitcast.39), channel_id=1, source_target_pairs={{8,0},{10,2},{12,4},{14,6},{0,8},{2,10},{4,12},{6,14},{9,1},{11,3}... | collective-permute-start | bytes 196616 | tf_op jit(solution)/shard_map/ppermute | solution.py:310
  8.5 2.7 %collective-permute-start = (bf16[32,1024]{1,0:T(8,128)(2,1)}, bf16[32,1024]{1,0:T(8,128)(2,1)S(1)}, u32[]{:S(2)}, u32[]{:S(2)}) collective-permute-start(bf16[32,1024]{1,0:T(8,128)(2,1)} %bitcast.40), channel_id=1, source_target_pairs={{4,0},{6,2},{8,4},{10,6},{12,8},{14,10},{0,12},{2,14},{5,1},{7,3},... | collective-permute-start | bytes 196616 | tf_op jit(solution)/shard_map/ppermute | solution.py:310
  11.1 0.8 convert_bitcast_fusion
  11.9 1.1 collective-permute-start.3
  13.0 1.2 %copy-done = bf16[1,256,2048]{2,1,0:T(8,128)(2,1)S(1)} copy-done((bf16[1,256,2048]{2,1,0:T(8,128)(2,1)S(1)}, bf16[1,256,2048]{2,1,0:T(8,128)(2,1)}, u32[]{:S(2)}) %copy-start) | copy-done | bytes 1048600
  14.2 1.3 %shard_map.59 = bf16[16,128,256]{2,1,0:T(8,128)(2,1)} custom-call(bf16[256,2048]{1,0:T(8,128)(2,1)S(1)} %bitcast.33), custom_call_target="tpu_custom_call" | custom-call | bytes 4680000 | tf_op jit(solution)/shard_map/pallas_call | solution.py:39
  15.5 7.0 %all-to-all-start = ((bf16[16,128,256]{2,1,0:T(8,128)(2,1)}), bf16[16,128,256]{2,1,0:T(8,128)(2,1)S(1)}, u32[]{:S(2)}, u32[]{:S(2)}) async-start(bf16[16,128,256]{2,1,0:T(8,128)(2,1)} %shard_map.59), calls=%async_computation | async-start | bytes 2097152 | tf_op jit(solution)/shard_map/all_to_all | solution.py:314
  22.6 6.8 %shard_map.60 = bf16[16,128,256]{2,1,0:T(8,128)(2,1)} custom-call(bf16[256,2048]{1,0:T(8,128)(2,1)} %bitcast.32, bf16[2,2048,1024]{2,1,0:T(8,128)(2,1)} %w_ref.1), custom_call_target="tpu_custom_call" | custom-call | bytes 25200000 | tf_op jit(solution)/shard_map/pallas_call | solution.py:66
  29.4 0.0 collective-permute-done.3
  29.4 0.0 collective-permute-done.1
  29.7 3.2 %collective-permute-start.12 = (bf16[128,512]{1,0:T(8,128)(2,1)S(1)}, bf16[128,512]{1,0:T(8,128)(2,1)S(1)}, u32[]{:S(2)}, u32[]{:S(2)}) collective-permute-start(bf16[128,512]{1,0:T(8,128)(2,1)S(1)} %get-tuple-element.46), channel_id=1, source_target_pairs={{0,192},{16,208},{32,224},{48,240},{64,0},{80,16},{96,32},{112,48}... | collective-permute-start | bytes 393224 | tf_op jit(solution)/shard_map/ppermute | solution.py:265
  32.8 0.0 collective-permute-start.10
  32.9 2.7 %collective-permute-start.6 = (bf16[128,512]{1,0:T(8,128)(2,1)S(1)}, bf16[128,512]{1,0:T(8,128)(2,1)S(1)}, u32[]{:S(2)}, u32[]{:S(2)}) collective-permute-start(bf16[128,512]{1,0:T(8,128)(2,1)S(1)} %get-tuple-element.38), channel_id=1, source_target_pairs={{0,48},{16,0},{32,16},{48,32},{64,112},{80,64},{96,80},{112,96},{1... | collective-permute-start | bytes 393224 | tf_op jit(solution)/shard_map/ppermute | solution.py:265
  35.5 0.9 collective-permute-start.5
  36.4 0.9 collective-permute-start.4
  37.2 1.8 %all-to-all-done.y_ref = bf16[16,128,256]{2,1,0:T(8,128)(2,1)S(1)} async-done(((bf16[16,128,256]{2,1,0:T(8,128)(2,1)}), bf16[16,128,256]{2,1,0:T(8,128)(2,1)S(1)}, u32[]{:S(2)}, u32[]{:S(2)}) %all-to-all-start) | async-done | bytes 1048608 | tf_op jit(solution)/shard_map/all_to_all | solution.py:314
  39.0 5.0 %all-to-all-start.1 = ((bf16[16,128,256]{2,1,0:T(8,128)(2,1)}), bf16[16,128,256]{2,1,0:T(8,128)(2,1)S(1)}, u32[]{:S(2)}, u32[]{:S(2)}) async-start(bf16[16,128,256]{2,1,0:T(8,128)(2,1)} %shard_map.60), calls=%async_computation.1 | async-start | bytes 2097152 | tf_op jit(solution)/shard_map/all_to_all | solution.py:329
  44.1 0.1 fusion.7.taps_ref
  44.2 6.2 %shard_map.61 = (bf16[512,2048]{1,0:T(8,128)(2,1)S(1)}, f32[8,128]{1,0:T(8,128)S(1)}) custom-call(bf16[16,128,256]{2,1,0:T(8,128)(2,1)S(1)} %all-to-all-done.y_ref, f32[4,4352]{1,0:T(4,128)S(1)} %fusion.7.taps_ref), custom_call_target="tpu_custom_call" | custom-call | bytes 18000000 | tf_op jit(solution)/shard_map/pallas_call | solution.py:198
  50.4 1.3 %copy-done.1 = bf16[512,2048]{1,0:T(8,128)(2,1)} copy-done((bf16[512,2048]{1,0:T(8,128)(2,1)}, bf16[512,2048]{1,0:T(8,128)(2,1)S(1)}, u32[]{:S(2)}) %copy-start.1) | copy-done | bytes 2097176
  51.8 3.5 %collective-permute-start.11 = (bf16[128,512]{1,0:T(8,128)(2,1)S(1)}, bf16[128,512]{1,0:T(8,128)(2,1)}, u32[]{:S(2)}, u32[]{:S(2)}) collective-permute-start(bf16[128,512]{1,0:T(8,128)(2,1)S(1)} %get-tuple-element.46), channel_id=1, source_target_pairs={{0,128},{16,144},{32,160},{48,176},{64,192},{80,208},{96,224},{112... | collective-permute-start | bytes 393224 | tf_op jit(solution)/shard_map/ppermute | solution.py:265
  55.3 0.1 pad_maximum_fusion.refs_0_
  55.4 1.2 %collective-permute-start.9 = (bf16[4,128,512]{2,1,0:T(8,128)(2,1)S(1)}, bf16[4,128,512]{2,1,0:T(8,128)(2,1)S(1)}, u32[]{:S(2)}, u32[]{:S(2)}) collective-permute-start(bf16[4,128,512]{2,1,0:T(8,128)(2,1)S(1)} %pad_maximum_fusion.refs_0_), channel_id=1, source_target_pairs={{0,192},{16,208},{32,224},{48,240},{64,0},{80,16},{96,32},{112,48}... | collective-permute-start | bytes 1572872 | tf_op jit(solution)/shard_map/ppermute | solution.py:265
  56.6 1.6 %collective-permute-start.8 = (bf16[4,128,512]{2,1,0:T(8,128)(2,1)S(1)}, bf16[4,128,512]{2,1,0:T(8,128)(2,1)S(1)}, u32[]{:S(2)}, u32[]{:S(2)}) collective-permute-start(bf16[4,128,512]{2,1,0:T(8,128)(2,1)S(1)} %pad_maximum_fusion.refs_0_), channel_id=1, source_target_pairs={{0,128},{16,144},{32,160},{48,176},{64,192},{80,208},{96,224},{112... | collective-permute-start | bytes 1572872 | tf_op jit(solution)/shard_map/ppermute | solution.py:265
  58.2 1.3 %all-to-all-done.1.y_ref = bf16[16,128,256]{2,1,0:T(8,128)(2,1)S(1)} async-done(((bf16[16,128,256]{2,1,0:T(8,128)(2,1)}), bf16[16,128,256]{2,1,0:T(8,128)(2,1)S(1)}, u32[]{:S(2)}, u32[]{:S(2)}) %all-to-all-start.1) | async-done | bytes 1048608 | tf_op jit(solution)/shard_map/all_to_all | solution.py:329
  59.5 3.8 %shard_map.62 = (bf16[128,16,128]{2,1,0:T(8,128)(2,1)S(1)}, f32[8,128]{1,0:T(8,128)S(1)}) custom-call(bf16[16,128,256]{2,1,0:T(8,128)(2,1)S(1)} %all-to-all-done.1.y_ref, f32[2,4352]{1,0:T(2,128)S(1)} %pad_convert_fusion.f_ref, f32[8,128]{1,0:T(8,128)S(1)} %get-tuple-element.44.refs_0_), custom_call_target="tpu_custom_call" | custom-call | bytes 18000000 | tf_op jit(solution)/shard_map/pallas_call | solution.py:159
  63.4 1.0 collective-permute-start.7
  64.3 1.0 pad_maximum_fusion.1.refs_4_
  65.3 0.6 collective-permute-start.15
  65.9 1.5 %collective-permute-start.14 = (bf16[4,128,512]{2,1,0:T(8,128)(2,1)S(1)}, bf16[4,128,512]{2,1,0:T(8,128)(2,1)}, u32[]{:S(2)}, u32[]{:S(2)}) collective-permute-start(bf16[4,128,512]{2,1,0:T(8,128)(2,1)S(1)} %pad_maximum_fusion.1.refs_4_), channel_id=1, source_target_pairs={{0,32},{16,48},{32,0},{48,16},{64,96},{80,112},{96,64},{112,80},{1... | collective-permute-start | bytes 1572872 | tf_op jit(solution)/shard_map/ppermute | solution.py:265
  67.4 4.1 %collective-permute-done.9.refs_3_ = bf16[4,128,512]{2,1,0:T(8,128)(2,1)S(1)} collective-permute-done((bf16[4,128,512]{2,1,0:T(8,128)(2,1)S(1)}, bf16[4,128,512]{2,1,0:T(8,128)(2,1)S(1)}, u32[]{:S(2)}, u32[]{:S(2)}) %collective-permute-start.9) | collective-permute-done | bytes 524320 | tf_op jit(solution)/shard_map/ppermute | solution.py:265
  71.5 1.5 %collective-permute-start.13 = (bf16[4,128,512]{2,1,0:T(8,128)(2,1)S(1)}, bf16[4,128,512]{2,1,0:T(8,128)(2,1)}, u32[]{:S(2)}, u32[]{:S(2)}) collective-permute-start(bf16[4,128,512]{2,1,0:T(8,128)(2,1)S(1)} %pad_maximum_fusion.1.refs_4_), channel_id=1, source_target_pairs={{0,16},{16,32},{32,48},{48,0},{64,80},{80,96},{96,112},{112,64},{1... | collective-permute-start | bytes 1572872 | tf_op jit(solution)/shard_map/ppermute | solution.py:265
  73.0 8.3 %all-to-all-start.2 = ((bf16[128,16,128]{2,1,0:T(8,128)(2,1)}), bf16[128,16,128]{2,1,0:T(8,128)(2,1)S(1)}, u32[]{:S(2)}, u32[]{:S(2)}) async-start(bf16[128,16,128]{2,1,0:T(8,128)(2,1)} %copy-done.3), calls=%async_computation.2 | async-start | bytes 1048576 | tf_op jit(solution)/shard_map/all_to_all | solution.py:341
  81.3 0.1 pad_add_fusion.place_ref
  81.4 0.9 collective-permute-done.7.refs_1_
  82.2 5.2 %collective-permute-done.15.refs_7_ = bf16[4,128,512]{2,1,0:T(8,128)(2,1)} collective-permute-done((bf16[4,128,512]{2,1,0:T(8,128)(2,1)S(1)}, bf16[4,128,512]{2,1,0:T(8,128)(2,1)}, u32[]{:S(2)}, u32[]{:S(2)}) %collective-permute-start.15) | collective-permute-done | bytes 524320 | tf_op jit(solution)/shard_map/ppermute | solution.py:265
  87.4 4.3 %collective-permute-done.13.refs_5_ = bf16[4,128,512]{2,1,0:T(8,128)(2,1)} collective-permute-done((bf16[4,128,512]{2,1,0:T(8,128)(2,1)S(1)}, bf16[4,128,512]{2,1,0:T(8,128)(2,1)}, u32[]{:S(2)}, u32[]{:S(2)}) %collective-permute-start.13) | collective-permute-done | bytes 524320 | tf_op jit(solution)/shard_map/ppermute | solution.py:265
  91.7 1.6 %copy-done.2 = bf16[512,2048]{1,0:T(8,128)(2,1)S(1)} copy-done((bf16[512,2048]{1,0:T(8,128)(2,1)S(1)}, bf16[512,2048]{1,0:T(8,128)(2,1)}, u32[]{:S(2)}) %copy-start.2) | copy-done | bytes 2097176
  93.3 7.4 %shard_map.63 = (bf16[4,64,1024]{2,1,0:T(8,128)(2,1)S(1)}, bf16[4,64,1024]{2,1,0:T(8,128)(2,1)S(1)}) custom-call(s32[3]{0:T(128)S(1)} %pad_add_fusion.place_ref, bf16[512,2048]{1,0:T(8,128)(2,1)S(1)} %copy-done.2, bf16[4,128,512]{2,1,0:T(8,128)(2,1)S(1)} %pad_maximum_fusion.refs_0_, bf16[4,128,512]{2,1,0:T(8,128)(2,1)S(1)} %collective-permute-done.7.refs_1_, ...), custom_call_target="tpu_custom_call" | custom-call | bytes 18000000 | tf_op jit(solution)/shard_map/pallas_call | solution.py:241
  100.7 0.1 collective-permute-start.16
  100.8 1.9 %collective-permute-done.16 = bf16[4,64,1024]{2,1,0:T(8,128)(2,1)S(1)} collective-permute-done((bf16[4,64,1024]{2,1,0:T(8,128)(2,1)S(1)}, bf16[4,64,1024]{2,1,0:T(8,128)(2,1)S(1)}, u32[]{:S(2)}, u32[]{:S(2)}) %collective-permute-start.16) | collective-permute-done | bytes 524320 | tf_op jit(solution)/shard_map/ppermute | solution.py:345
  102.7 0.2 convert_add_fusion
  102.9 1.0 collective-permute-start.17
  103.9 0.8 shard_map.64
  104.7 6.6 %collective-permute-done.17 = bf16[2,64,1024]{2,1,0:T(8,128)(2,1)S(1)} collective-permute-done((bf16[2,64,1024]{2,1,0:T(8,128)(2,1)S(1)}, bf16[2,64,1024]{2,1,0:T(8,128)(2,1)S(1)}, u32[]{:S(2)}, u32[]{:S(2)}) %collective-permute-start.17) | collective-permute-done | bytes 262176 | tf_op jit(solution)/shard_map/ppermute | solution.py:347
  111.3 0.1 fusion.1
  111.4 1.0 copy.6
  (31 shorter events, 0.2 us)
Async XLA Ops:
  0.6 28.8 %collective-permute-start.2 = (bf16[32,1024]{1,0:T(8,128)(2,1)}, bf16[32,1024]{1,0:T(8,128)(2,1)S(1)}, u32[]{:S(2)}, u32[]{:S(2)}) collective-permute-start(bf16[32,1024]{1,0:T(8,128)(2,1)} %bitcast.38), channel_id=1, source_target_pairs={{12,0},{14,2},{0,4},{2,6},{4,8},{6,10},{8,12},{10,14},{13,1},{15,3... | collective-permute-start | bytes 196616 | tf_op jit(solution)/shard_map/ppermute | solution.py:310
  4.0 25.4 %collective-permute-start.1 = (bf16[32,1024]{1,0:T(8,128)(2,1)}, bf16[32,1024]{1,0:T(8,128)(2,1)S(1)}, u32[]{:S(2)}, u32[]{:S(2)}) collective-permute-start(bf16[32,1024]{1,0:T(8,128)(2,1)} %bitcast.39), channel_id=1, source_target_pairs={{8,0},{10,2},{12,4},{14,6},{0,8},{2,10},{4,12},{6,14},{9,1},{11,3}... | collective-permute-start | bytes 196616 | tf_op jit(solution)/shard_map/ppermute | solution.py:310
  8.5 21.0 %collective-permute-start = (bf16[32,1024]{1,0:T(8,128)(2,1)}, bf16[32,1024]{1,0:T(8,128)(2,1)S(1)}, u32[]{:S(2)}, u32[]{:S(2)}) collective-permute-start(bf16[32,1024]{1,0:T(8,128)(2,1)} %bitcast.40), channel_id=1, source_target_pairs={{4,0},{6,2},{8,4},{10,6},{12,8},{14,10},{0,12},{2,14},{5,1},{7,3},... | collective-permute-start | bytes 196616 | tf_op jit(solution)/shard_map/ppermute | solution.py:310
  11.9 17.5 %collective-permute-start.3 = (bf16[2,4096]{1,0:T(2,128)(2,1)S(1)}, bf16[2,4096]{1,0:T(2,128)(2,1)S(1)}, u32[]{:S(2)}, u32[]{:S(2)}) collective-permute-start(bf16[2,4096]{1,0:T(2,128)(2,1)S(1)} %convert_bitcast_fusion), channel_id=1, source_target_pairs={{0,2},{2,0},{4,6},{6,4},{8,10},{10,8},{12,14},{14,12},{1,3},{3,1},... | collective-permute-start | bytes 49160 | tf_op jit(solution)/shard_map/ppermute | solution.py:315
  13.0 1.2 %copy-start = (bf16[1,256,2048]{2,1,0:T(8,128)(2,1)S(1)}, bf16[1,256,2048]{2,1,0:T(8,128)(2,1)}, u32[]{:S(2)}) copy-start(bf16[1,256,2048]{2,1,0:T(8,128)(2,1)} %param.4) | copy-start | bytes 3145732
  14.2 15.2 %copy-start.4 = (bf16[1,32,1024]{2,1,0:T(8,128)(2,1)S(1)}, bf16[1,32,1024]{2,1,0:T(8,128)(2,1)}, u32[]{:S(2)}) copy-start(bf16[1,32,1024]{2,1,0:T(8,128)(2,1)} %param.7) | copy-start | bytes 196612
  15.5 23.5 %all-to-all-start = ((bf16[16,128,256]{2,1,0:T(8,128)(2,1)}), bf16[16,128,256]{2,1,0:T(8,128)(2,1)S(1)}, u32[]{:S(2)}, u32[]{:S(2)}) async-start(bf16[16,128,256]{2,1,0:T(8,128)(2,1)} %shard_map.59), calls=%async_computation | async-start | bytes 2097152 | tf_op jit(solution)/shard_map/all_to_all | solution.py:314
  29.7 33.7 %collective-permute-start.12 = (bf16[128,512]{1,0:T(8,128)(2,1)S(1)}, bf16[128,512]{1,0:T(8,128)(2,1)S(1)}, u32[]{:S(2)}, u32[]{:S(2)}) collective-permute-start(bf16[128,512]{1,0:T(8,128)(2,1)S(1)} %get-tuple-element.46), channel_id=1, source_target_pairs={{0,192},{16,208},{32,224},{48,240},{64,0},{80,16},{96,32},{112,48}... | collective-permute-start | bytes 393224 | tf_op jit(solution)/shard_map/ppermute | solution.py:265
  32.8 31.5 %collective-permute-start.10 = (bf16[128,512]{1,0:T(8,128)(2,1)S(1)}, bf16[128,512]{1,0:T(8,128)(2,1)S(1)}, u32[]{:S(2)}, u32[]{:S(2)}) collective-permute-start(bf16[128,512]{1,0:T(8,128)(2,1)S(1)} %get-tuple-element.46), channel_id=1, source_target_pairs={{0,64},{16,80},{32,96},{48,112},{64,128},{80,144},{96,160},{112,17... | collective-permute-start | bytes 393224 | tf_op jit(solution)/shard_map/ppermute | solution.py:265
  32.9 18.9 %collective-permute-start.6 = (bf16[128,512]{1,0:T(8,128)(2,1)S(1)}, bf16[128,512]{1,0:T(8,128)(2,1)S(1)}, u32[]{:S(2)}, u32[]{:S(2)}) collective-permute-start(bf16[128,512]{1,0:T(8,128)(2,1)S(1)} %get-tuple-element.38), channel_id=1, source_target_pairs={{0,48},{16,0},{32,16},{48,32},{64,112},{80,64},{96,80},{112,96},{1... | collective-permute-start | bytes 393224 | tf_op jit(solution)/shard_map/ppermute | solution.py:265
  35.5 16.3 %collective-permute-start.5 = (bf16[128,512]{1,0:T(8,128)(2,1)S(1)}, bf16[128,512]{1,0:T(8,128)(2,1)S(1)}, u32[]{:S(2)}, u32[]{:S(2)}) collective-permute-start(bf16[128,512]{1,0:T(8,128)(2,1)S(1)} %get-tuple-element.38), channel_id=1, source_target_pairs={{0,32},{16,48},{32,0},{48,16},{64,96},{80,112},{96,64},{112,80},{1... | collective-permute-start | bytes 393224 | tf_op jit(solution)/shard_map/ppermute | solution.py:265
  36.4 15.4 %collective-permute-start.4 = (bf16[128,512]{1,0:T(8,128)(2,1)S(1)}, bf16[128,512]{1,0:T(8,128)(2,1)S(1)}, u32[]{:S(2)}, u32[]{:S(2)}) collective-permute-start(bf16[128,512]{1,0:T(8,128)(2,1)S(1)} %get-tuple-element.38), channel_id=1, source_target_pairs={{0,16},{16,32},{32,48},{48,0},{64,80},{80,96},{96,112},{112,64},{1... | collective-permute-start | bytes 393224 | tf_op jit(solution)/shard_map/ppermute | solution.py:265
  39.0 20.5 %all-to-all-start.1 = ((bf16[16,128,256]{2,1,0:T(8,128)(2,1)}), bf16[16,128,256]{2,1,0:T(8,128)(2,1)S(1)}, u32[]{:S(2)}, u32[]{:S(2)}) async-start(bf16[16,128,256]{2,1,0:T(8,128)(2,1)} %shard_map.60), calls=%async_computation.1 | async-start | bytes 2097152 | tf_op jit(solution)/shard_map/all_to_all | solution.py:329
  50.4 1.4 %copy-start.1 = (bf16[512,2048]{1,0:T(8,128)(2,1)}, bf16[512,2048]{1,0:T(8,128)(2,1)S(1)}, u32[]{:S(2)}) copy-start(bf16[512,2048]{1,0:T(8,128)(2,1)S(1)} %get-tuple-element.32.f_ref) | copy-start | bytes 6291460
  51.8 12.5 %collective-permute-start.11 = (bf16[128,512]{1,0:T(8,128)(2,1)S(1)}, bf16[128,512]{1,0:T(8,128)(2,1)}, u32[]{:S(2)}, u32[]{:S(2)}) collective-permute-start(bf16[128,512]{1,0:T(8,128)(2,1)S(1)} %get-tuple-element.46), channel_id=1, source_target_pairs={{0,128},{16,144},{32,160},{48,176},{64,192},{80,208},{96,224},{112... | collective-permute-start | bytes 393224 | tf_op jit(solution)/shard_map/ppermute | solution.py:265
  55.4 16.1 %collective-permute-start.9 = (bf16[4,128,512]{2,1,0:T(8,128)(2,1)S(1)}, bf16[4,128,512]{2,1,0:T(8,128)(2,1)S(1)}, u32[]{:S(2)}, u32[]{:S(2)}) collective-permute-start(bf16[4,128,512]{2,1,0:T(8,128)(2,1)S(1)} %pad_maximum_fusion.refs_0_), channel_id=1, source_target_pairs={{0,192},{16,208},{32,224},{48,240},{64,0},{80,16},{96,32},{112,48}... | collective-permute-start | bytes 1572872 | tf_op jit(solution)/shard_map/ppermute | solution.py:265
  56.6 24.7 %collective-permute-start.8 = (bf16[4,128,512]{2,1,0:T(8,128)(2,1)S(1)}, bf16[4,128,512]{2,1,0:T(8,128)(2,1)S(1)}, u32[]{:S(2)}, u32[]{:S(2)}) collective-permute-start(bf16[4,128,512]{2,1,0:T(8,128)(2,1)S(1)} %pad_maximum_fusion.refs_0_), channel_id=1, source_target_pairs={{0,128},{16,144},{32,160},{48,176},{64,192},{80,208},{96,224},{112... | collective-permute-start | bytes 1572872 | tf_op jit(solution)/shard_map/ppermute | solution.py:265
  63.4 9.6 %copy-start.3 = (bf16[128,16,128]{2,1,0:T(8,128)(2,1)}, bf16[128,16,128]{2,1,0:T(8,128)(2,1)S(1)}, u32[]{:S(2)}) copy-start(bf16[128,16,128]{2,1,0:T(8,128)(2,1)S(1)} %get-tuple-element.53) | copy-start | bytes 1572868
  63.4 18.9 %collective-permute-start.7 = (bf16[4,128,512]{2,1,0:T(8,128)(2,1)S(1)}, bf16[4,128,512]{2,1,0:T(8,128)(2,1)S(1)}, u32[]{:S(2)}, u32[]{:S(2)}) collective-permute-start(bf16[4,128,512]{2,1,0:T(8,128)(2,1)S(1)} %pad_maximum_fusion.refs_0_), channel_id=1, source_target_pairs={{0,64},{16,80},{32,96},{48,112},{64,128},{80,144},{96,160},{112,17... | collective-permute-start | bytes 1572872 | tf_op jit(solution)/shard_map/ppermute | solution.py:265
  65.3 22.1 %collective-permute-start.15 = (bf16[4,128,512]{2,1,0:T(8,128)(2,1)S(1)}, bf16[4,128,512]{2,1,0:T(8,128)(2,1)}, u32[]{:S(2)}, u32[]{:S(2)}) collective-permute-start(bf16[4,128,512]{2,1,0:T(8,128)(2,1)S(1)} %pad_maximum_fusion.1.refs_4_), channel_id=1, source_target_pairs={{0,48},{16,0},{32,16},{48,32},{64,112},{80,64},{96,80},{112,96},{1... | collective-permute-start | bytes 1572872 | tf_op jit(solution)/shard_map/ppermute | solution.py:265
  65.9 21.5 %collective-permute-start.14 = (bf16[4,128,512]{2,1,0:T(8,128)(2,1)S(1)}, bf16[4,128,512]{2,1,0:T(8,128)(2,1)}, u32[]{:S(2)}, u32[]{:S(2)}) collective-permute-start(bf16[4,128,512]{2,1,0:T(8,128)(2,1)S(1)} %pad_maximum_fusion.1.refs_4_), channel_id=1, source_target_pairs={{0,32},{16,48},{32,0},{48,16},{64,96},{80,112},{96,64},{112,80},{1... | collective-permute-start | bytes 1572872 | tf_op jit(solution)/shard_map/ppermute | solution.py:265
  71.5 20.2 %collective-permute-start.13 = (bf16[4,128,512]{2,1,0:T(8,128)(2,1)S(1)}, bf16[4,128,512]{2,1,0:T(8,128)(2,1)}, u32[]{:S(2)}, u32[]{:S(2)}) collective-permute-start(bf16[4,128,512]{2,1,0:T(8,128)(2,1)S(1)} %pad_maximum_fusion.1.refs_4_), channel_id=1, source_target_pairs={{0,16},{16,32},{32,48},{48,0},{64,80},{80,96},{96,112},{112,64},{1... | collective-permute-start | bytes 1572872 | tf_op jit(solution)/shard_map/ppermute | solution.py:265
  73.0 29.9 %all-to-all-start.2 = ((bf16[128,16,128]{2,1,0:T(8,128)(2,1)}), bf16[128,16,128]{2,1,0:T(8,128)(2,1)S(1)}, u32[]{:S(2)}, u32[]{:S(2)}) async-start(bf16[128,16,128]{2,1,0:T(8,128)(2,1)} %copy-done.3), calls=%async_computation.2 | async-start | bytes 1048576 | tf_op jit(solution)/shard_map/all_to_all | solution.py:341
  91.7 1.6 %copy-start.2 = (bf16[512,2048]{1,0:T(8,128)(2,1)S(1)}, bf16[512,2048]{1,0:T(8,128)(2,1)}, u32[]{:S(2)}) copy-start(bf16[512,2048]{1,0:T(8,128)(2,1)} %copy-done.1) | copy-start | bytes 6291460
  100.7 2.0 %collective-permute-start.16 = (bf16[4,64,1024]{2,1,0:T(8,128)(2,1)S(1)}, bf16[4,64,1024]{2,1,0:T(8,128)(2,1)S(1)}, u32[]{:S(2)}, u32[]{:S(2)}) collective-permute-start(bf16[4,64,1024]{2,1,0:T(8,128)(2,1)S(1)} %get-tuple-element.52), channel_id=1, source_target_pairs={{0,1},{1,0},{2,3},{3,2},{4,5},{5,4},{6,7},{7,6},{8,9},{9,8},{10,11... | collective-permute-start | bytes 1572872 | tf_op jit(solution)/shard_map/ppermute | solution.py:345
  102.9 8.4 %collective-permute-start.17 = (bf16[2,64,1024]{2,1,0:T(8,128)(2,1)S(1)}, bf16[2,64,1024]{2,1,0:T(8,128)(2,1)S(1)}, u32[]{:S(2)}, u32[]{:S(2)}) collective-permute-start(bf16[2,64,1024]{2,1,0:T(8,128)(2,1)S(1)} %slice.43), channel_id=1, source_target_pairs={{0,2},{2,0},{4,6},{6,4},{8,10},{10,8},{12,14},{14,12},{1,3},{3,1},... | collective-permute-start | bytes 786440 | tf_op jit(solution)/shard_map/ppermute | solution.py:347

commit v6 on v5

--- a/solution.py
+++ b/solution.py
@@ -222,11 +222,14 @@
                         pieces[side * SIDE + far].at[near], grad_ref.at[side, rows, :], sem.at[len(copies)]
                     )
                 )
-    for copy in copies:
+    for copy in copies[: SIDE * SIDE]:
         copy.start()
     for side in range(2):
         for copy in copies[side * SIDE * SIDE : (side + 1) * SIDE * SIDE]:
             copy.wait()
+        if side == 0:
+            for copy in copies[SIDE * SIDE :]:
+                copy.start()
         part = jnp.dot(f_ref[...], grad_ref[side], preferred_element_type=F32).astype(BF)
         at = slice(side * cols, (side + 1) * cols)
         for k in range(count):

time: 114 us -> 114 us (level)
  no operation moved by 1% of the time
where the time goes in v6:
time: 114 us; the launch traced here: 112 us
  starting transfers between devices  51.4 us (45%)
  Pallas kernels  26.3 us (23%)
  waiting for transfers between devices  26.1 us (23%)
  local copies, waits for them, and re-layouts  5.28 us (5%)
  other arithmetic  2.29 us (2%)
    ppermute x12, starting transfers between devices, step(): return lax.ppermute(a, 'seq', shift(axis, d))  18.4 us
    ppermute x12, waiting for transfers between devices, step(): return lax.ppermute(a, 'seq', shift(axis, d))  14.5 us
    ppermute x3, starting transfers between devices, shards(): lax.ppermute(cotangent[0], 'filt', [((i + step) % n_filt, i) for i in ran...  10.5 us
    all_to_all x1, starting transfers between devices, shards(): p = lax.all_to_all(p, ('seq', 'filt'), 0, 0, tiled=True)  8.25 us
    pallas_call x1, Pallas kernels, grad(): pl.pallas_call(grad_kernel, out_shape=(shape, shape), in_specs=[pl.BlockS...  7.38 us
    all_to_all x1, starting transfers between devices, shards(): xs = lax.all_to_all(turn(x, n_seq), 'seq', 0, 0, tiled=True)  7.03 us
    pallas_call x1, Pallas kernels, project(): pl.pallas_call(project_kernel, grid=(steps,), out_shape=jax.ShapeDtypeStr...  6.8 us
    ppermute x1, waiting for transfers between devices, shards(): back = lax.ppermute(send, 'filt', [(i, i ^ 1) for i in range(n_filt)])  6.63 us
  transfers between devices with their start and end apart: 21, of which 8 were waited for; matrix products, arithmetic and copies ran while one was open for 2% of the time, Pallas kernels for 23%

profile of v6, /device:TPU:32, one launch (start us, length us, event | category | flops | bytes accessed | tf_op | source)
XLA Modules:
  0.0 112.4 jit_solution(5120191822308464367)
XLA Ops:
  0.6 3.3 %collective-permute-start.2 = (bf16[32,1024]{1,0:T(8,128)(2,1)}, bf16[32,1024]{1,0:T(8,128)(2,1)S(1)}, u32[]{:S(2)}, u32[]{:S(2)}) collective-permute-start(bf16[32,1024]{1,0:T(8,128)(2,1)} %bitcast.38), channel_id=1, source_target_pairs={{12,0},{14,2},{0,4},{2,6},{4,8},{6,10},{8,12},{10,14},{13,1},{15,3... | collective-permute-start | bytes 196616 | tf_op jit(solution)/shard_map/ppermute | solution.py:313
  4.0 4.5 %collective-permute-start.1 = (bf16[32,1024]{1,0:T(8,128)(2,1)}, bf16[32,1024]{1,0:T(8,128)(2,1)S(1)}, u32[]{:S(2)}, u32[]{:S(2)}) collective-permute-start(bf16[32,1024]{1,0:T(8,128)(2,1)} %bitcast.39), channel_id=1, source_target_pairs={{8,0},{10,2},{12,4},{14,6},{0,8},{2,10},{4,12},{6,14},{9,1},{11,3}... | collective-permute-start | bytes 196616 | tf_op jit(solution)/shard_map/ppermute | solution.py:313
  8.5 2.7 %collective-permute-start = (bf16[32,1024]{1,0:T(8,128)(2,1)}, bf16[32,1024]{1,0:T(8,128)(2,1)S(1)}, u32[]{:S(2)}, u32[]{:S(2)}) collective-permute-start(bf16[32,1024]{1,0:T(8,128)(2,1)} %bitcast.40), channel_id=1, source_target_pairs={{4,0},{6,2},{8,4},{10,6},{12,8},{14,10},{0,12},{2,14},{5,1},{7,3},... | collective-permute-start | bytes 196616 | tf_op jit(solution)/shard_map/ppermute | solution.py:313
  11.1 0.8 convert_bitcast_fusion
  11.9 1.1 collective-permute-start.3
  13.0 1.2 %copy-done = bf16[1,256,2048]{2,1,0:T(8,128)(2,1)S(1)} copy-done((bf16[1,256,2048]{2,1,0:T(8,128)(2,1)S(1)}, bf16[1,256,2048]{2,1,0:T(8,128)(2,1)}, u32[]{:S(2)}) %copy-start) | copy-done | bytes 1048600
  14.2 1.3 %shard_map.59 = bf16[16,128,256]{2,1,0:T(8,128)(2,1)} custom-call(bf16[256,2048]{1,0:T(8,128)(2,1)S(1)} %bitcast.33), custom_call_target="tpu_custom_call" | custom-call | bytes 4680000 | tf_op jit(solution)/shard_map/pallas_call | solution.py:39
  15.5 7.0 %all-to-all-start = ((bf16[16,128,256]{2,1,0:T(8,128)(2,1)}), bf16[16,128,256]{2,1,0:T(8,128)(2,1)S(1)}, u32[]{:S(2)}, u32[]{:S(2)}) async-start(bf16[16,128,256]{2,1,0:T(8,128)(2,1)} %shard_map.59), calls=%async_computation | async-start | bytes 2097152 | tf_op jit(solution)/shard_map/all_to_all | solution.py:317
  22.6 6.8 %shard_map.60 = bf16[16,128,256]{2,1,0:T(8,128)(2,1)} custom-call(bf16[256,2048]{1,0:T(8,128)(2,1)} %bitcast.32, bf16[2,2048,1024]{2,1,0:T(8,128)(2,1)} %w_ref.1), custom_call_target="tpu_custom_call" | custom-call | bytes 25200000 | tf_op jit(solution)/shard_map/pallas_call | solution.py:66
  29.4 0.0 collective-permute-done.3
  29.4 0.0 collective-permute-done.1
  29.7 3.2 %collective-permute-start.12 = (bf16[128,512]{1,0:T(8,128)(2,1)S(1)}, bf16[128,512]{1,0:T(8,128)(2,1)S(1)}, u32[]{:S(2)}, u32[]{:S(2)}) collective-permute-start(bf16[128,512]{1,0:T(8,128)(2,1)S(1)} %get-tuple-element.46), channel_id=1, source_target_pairs={{0,192},{16,208},{32,224},{48,240},{64,0},{80,16},{96,32},{112,48}... | collective-permute-start | bytes 393224 | tf_op jit(solution)/shard_map/ppermute | solution.py:268
  32.8 0.0 collective-permute-start.10
  32.9 2.7 %collective-permute-start.6 = (bf16[128,512]{1,0:T(8,128)(2,1)S(1)}, bf16[128,512]{1,0:T(8,128)(2,1)S(1)}, u32[]{:S(2)}, u32[]{:S(2)}) collective-permute-start(bf16[128,512]{1,0:T(8,128)(2,1)S(1)} %get-tuple-element.38), channel_id=1, source_target_pairs={{0,48},{16,0},{32,16},{48,32},{64,112},{80,64},{96,80},{112,96},{1... | collective-permute-start | bytes 393224 | tf_op jit(solution)/shard_map/ppermute | solution.py:268
  35.5 0.9 collective-permute-start.5
  36.4 0.9 collective-permute-start.4
  37.2 1.8 %all-to-all-done.y_ref = bf16[16,128,256]{2,1,0:T(8,128)(2,1)S(1)} async-done(((bf16[16,128,256]{2,1,0:T(8,128)(2,1)}), bf16[16,128,256]{2,1,0:T(8,128)(2,1)S(1)}, u32[]{:S(2)}, u32[]{:S(2)}) %all-to-all-start) | async-done | bytes 1048608 | tf_op jit(solution)/shard_map/all_to_all | solution.py:317
  39.0 5.0 %all-to-all-start.1 = ((bf16[16,128,256]{2,1,0:T(8,128)(2,1)}), bf16[16,128,256]{2,1,0:T(8,128)(2,1)S(1)}, u32[]{:S(2)}, u32[]{:S(2)}) async-start(bf16[16,128,256]{2,1,0:T(8,128)(2,1)} %shard_map.60), calls=%async_computation.1 | async-start | bytes 2097152 | tf_op jit(solution)/shard_map/all_to_all | solution.py:332
  44.1 0.1 fusion.7.taps_ref
  44.2 6.2 %shard_map.61 = (bf16[512,2048]{1,0:T(8,128)(2,1)S(1)}, f32[8,128]{1,0:T(8,128)S(1)}) custom-call(bf16[16,128,256]{2,1,0:T(8,128)(2,1)S(1)} %all-to-all-done.y_ref, f32[4,4352]{1,0:T(4,128)S(1)} %fusion.7.taps_ref), custom_call_target="tpu_custom_call" | custom-call | bytes 18000000 | tf_op jit(solution)/shard_map/pallas_call | solution.py:198
  50.4 1.3 %copy-done.1 = bf16[512,2048]{1,0:T(8,128)(2,1)} copy-done((bf16[512,2048]{1,0:T(8,128)(2,1)}, bf16[512,2048]{1,0:T(8,128)(2,1)S(1)}, u32[]{:S(2)}) %copy-start.1) | copy-done | bytes 2097176
  51.8 3.5 %collective-permute-start.11 = (bf16[128,512]{1,0:T(8,128)(2,1)S(1)}, bf16[128,512]{1,0:T(8,128)(2,1)}, u32[]{:S(2)}, u32[]{:S(2)}) collective-permute-start(bf16[128,512]{1,0:T(8,128)(2,1)S(1)} %get-tuple-element.46), channel_id=1, source_target_pairs={{0,128},{16,144},{32,160},{48,176},{64,192},{80,208},{96,224},{112... | collective-permute-start | bytes 393224 | tf_op jit(solution)/shard_map/ppermute | solution.py:268
  55.3 0.1 pad_maximum_fusion.refs_0_
  55.4 1.2 %collective-permute-start.9 = (bf16[4,128,512]{2,1,0:T(8,128)(2,1)S(1)}, bf16[4,128,512]{2,1,0:T(8,128)(2,1)S(1)}, u32[]{:S(2)}, u32[]{:S(2)}) collective-permute-start(bf16[4,128,512]{2,1,0:T(8,128)(2,1)S(1)} %pad_maximum_fusion.refs_0_), channel_id=1, source_target_pairs={{0,192},{16,208},{32,224},{48,240},{64,0},{80,16},{96,32},{112,48}... | collective-permute-start | bytes 1572872 | tf_op jit(solution)/shard_map/ppermute | solution.py:268
  56.6 1.6 %collective-permute-start.8 = (bf16[4,128,512]{2,1,0:T(8,128)(2,1)S(1)}, bf16[4,128,512]{2,1,0:T(8,128)(2,1)S(1)}, u32[]{:S(2)}, u32[]{:S(2)}) collective-permute-start(bf16[4,128,512]{2,1,0:T(8,128)(2,1)S(1)} %pad_maximum_fusion.refs_0_), channel_id=1, source_target_pairs={{0,128},{16,144},{32,160},{48,176},{64,192},{80,208},{96,224},{112... | collective-permute-start | bytes 1572872 | tf_op jit(solution)/shard_map/ppermute | solution.py:268
  58.2 1.3 %all-to-all-done.1.y_ref = bf16[16,128,256]{2,1,0:T(8,128)(2,1)S(1)} async-done(((bf16[16,128,256]{2,1,0:T(8,128)(2,1)}), bf16[16,128,256]{2,1,0:T(8,128)(2,1)S(1)}, u32[]{:S(2)}, u32[]{:S(2)}) %all-to-all-start.1) | async-done | bytes 1048608 | tf_op jit(solution)/shard_map/all_to_all | solution.py:332
  59.5 3.8 %shard_map.62 = (bf16[128,16,128]{2,1,0:T(8,128)(2,1)S(1)}, f32[8,128]{1,0:T(8,128)S(1)}) custom-call(bf16[16,128,256]{2,1,0:T(8,128)(2,1)S(1)} %all-to-all-done.1.y_ref, f32[2,4352]{1,0:T(2,128)S(1)} %pad_convert_fusion.f_ref, f32[8,128]{1,0:T(8,128)S(1)} %get-tuple-element.44.refs_0_), custom_call_target="tpu_custom_call" | custom-call | bytes 18000000 | tf_op jit(solution)/shard_map/pallas_call | solution.py:159
  63.4 1.0 collective-permute-start.7
  64.3 1.0 pad_maximum_fusion.1.refs_4_
  65.3 0.6 collective-permute-start.15
  65.9 1.5 %collective-permute-start.14 = (bf16[4,128,512]{2,1,0:T(8,128)(2,1)S(1)}, bf16[4,128,512]{2,1,0:T(8,128)(2,1)}, u32[]{:S(2)}, u32[]{:S(2)}) collective-permute-start(bf16[4,128,512]{2,1,0:T(8,128)(2,1)S(1)} %pad_maximum_fusion.1.refs_4_), channel_id=1, source_target_pairs={{0,32},{16,48},{32,0},{48,16},{64,96},{80,112},{96,64},{112,80},{1... | collective-permute-start | bytes 1572872 | tf_op jit(solution)/shard_map/ppermute | solution.py:268
  67.4 4.1 %collective-permute-done.9.refs_3_ = bf16[4,128,512]{2,1,0:T(8,128)(2,1)S(1)} collective-permute-done((bf16[4,128,512]{2,1,0:T(8,128)(2,1)S(1)}, bf16[4,128,512]{2,1,0:T(8,128)(2,1)S(1)}, u32[]{:S(2)}, u32[]{:S(2)}) %collective-permute-start.9) | collective-permute-done | bytes 524320 | tf_op jit(solution)/shard_map/ppermute | solution.py:268
  71.5 1.5 %collective-permute-start.13 = (bf16[4,128,512]{2,1,0:T(8,128)(2,1)S(1)}, bf16[4,128,512]{2,1,0:T(8,128)(2,1)}, u32[]{:S(2)}, u32[]{:S(2)}) collective-permute-start(bf16[4,128,512]{2,1,0:T(8,128)(2,1)S(1)} %pad_maximum_fusion.1.refs_4_), channel_id=1, source_target_pairs={{0,16},{16,32},{32,48},{48,0},{64,80},{80,96},{96,112},{112,64},{1... | collective-permute-start | bytes 1572872 | tf_op jit(solution)/shard_map/ppermute | solution.py:268
  73.0 8.3 %all-to-all-start.2 = ((bf16[128,16,128]{2,1,0:T(8,128)(2,1)}), bf16[128,16,128]{2,1,0:T(8,128)(2,1)S(1)}, u32[]{:S(2)}, u32[]{:S(2)}) async-start(bf16[128,16,128]{2,1,0:T(8,128)(2,1)} %copy-done.3), calls=%async_computation.2 | async-start | bytes 1048576 | tf_op jit(solution)/shard_map/all_to_all | solution.py:344
  81.3 0.1 pad_add_fusion.place_ref
  81.4 0.9 collective-permute-done.7.refs_1_
  82.2 5.2 %collective-permute-done.15.refs_7_ = bf16[4,128,512]{2,1,0:T(8,128)(2,1)} collective-permute-done((bf16[4,128,512]{2,1,0:T(8,128)(2,1)S(1)}, bf16[4,128,512]{2,1,0:T(8,128)(2,1)}, u32[]{:S(2)}, u32[]{:S(2)}) %collective-permute-start.15) | collective-permute-done | bytes 524320 | tf_op jit(solution)/shard_map/ppermute | solution.py:268
  87.4 4.3 %collective-permute-done.13.refs_5_ = bf16[4,128,512]{2,1,0:T(8,128)(2,1)} collective-permute-done((bf16[4,128,512]{2,1,0:T(8,128)(2,1)S(1)}, bf16[4,128,512]{2,1,0:T(8,128)(2,1)}, u32[]{:S(2)}, u32[]{:S(2)}) %collective-permute-start.13) | collective-permute-done | bytes 524320 | tf_op jit(solution)/shard_map/ppermute | solution.py:268
  91.7 1.6 %copy-done.2 = bf16[512,2048]{1,0:T(8,128)(2,1)S(1)} copy-done((bf16[512,2048]{1,0:T(8,128)(2,1)S(1)}, bf16[512,2048]{1,0:T(8,128)(2,1)}, u32[]{:S(2)}) %copy-start.2) | copy-done | bytes 2097176
  93.3 7.4 %shard_map.63 = (bf16[4,64,1024]{2,1,0:T(8,128)(2,1)S(1)}, bf16[4,64,1024]{2,1,0:T(8,128)(2,1)S(1)}) custom-call(s32[3]{0:T(128)S(1)} %pad_add_fusion.place_ref, bf16[512,2048]{1,0:T(8,128)(2,1)S(1)} %copy-done.2, bf16[4,128,512]{2,1,0:T(8,128)(2,1)S(1)} %pad_maximum_fusion.refs_0_, bf16[4,128,512]{2,1,0:T(8,128)(2,1)S(1)} %collective-permute-done.7.refs_1_, ...), custom_call_target="tpu_custom_call" | custom-call | bytes 18000000 | tf_op jit(solution)/shard_map/pallas_call | solution.py:244
  100.7 0.1 collective-permute-start.16
  100.8 1.9 %collective-permute-done.16 = bf16[4,64,1024]{2,1,0:T(8,128)(2,1)S(1)} collective-permute-done((bf16[4,64,1024]{2,1,0:T(8,128)(2,1)S(1)}, bf16[4,64,1024]{2,1,0:T(8,128)(2,1)S(1)}, u32[]{:S(2)}, u32[]{:S(2)}) %collective-permute-start.16) | collective-permute-done | bytes 524320 | tf_op jit(solution)/shard_map/ppermute | solution.py:348
  102.7 0.2 convert_add_fusion
  102.9 1.0 collective-permute-start.17
  104.0 0.8 shard_map.64
  104.7 6.6 %collective-permute-done.17 = bf16[2,64,1024]{2,1,0:T(8,128)(2,1)S(1)} collective-permute-done((bf16[2,64,1024]{2,1,0:T(8,128)(2,1)S(1)}, bf16[2,64,1024]{2,1,0:T(8,128)(2,1)S(1)}, u32[]{:S(2)}, u32[]{:S(2)}) %collective-permute-start.17) | collective-permute-done | bytes 262176 | tf_op jit(solution)/shard_map/ppermute | solution.py:350
  111.4 0.1 fusion.1
  111.4 1.0 copy.6
  (31 shorter events, 0.2 us)
Async XLA Ops:
  0.6 28.8 %collective-permute-start.2 = (bf16[32,1024]{1,0:T(8,128)(2,1)}, bf16[32,1024]{1,0:T(8,128)(2,1)S(1)}, u32[]{:S(2)}, u32[]{:S(2)}) collective-permute-start(bf16[32,1024]{1,0:T(8,128)(2,1)} %bitcast.38), channel_id=1, source_target_pairs={{12,0},{14,2},{0,4},{2,6},{4,8},{6,10},{8,12},{10,14},{13,1},{15,3... | collective-permute-start | bytes 196616 | tf_op jit(solution)/shard_map/ppermute | solution.py:313
  4.0 25.4 %collective-permute-start.1 = (bf16[32,1024]{1,0:T(8,128)(2,1)}, bf16[32,1024]{1,0:T(8,128)(2,1)S(1)}, u32[]{:S(2)}, u32[]{:S(2)}) collective-permute-start(bf16[32,1024]{1,0:T(8,128)(2,1)} %bitcast.39), channel_id=1, source_target_pairs={{8,0},{10,2},{12,4},{14,6},{0,8},{2,10},{4,12},{6,14},{9,1},{11,3}... | collective-permute-start | bytes 196616 | tf_op jit(solution)/shard_map/ppermute | solution.py:313
  8.5 21.0 %collective-permute-start = (bf16[32,1024]{1,0:T(8,128)(2,1)}, bf16[32,1024]{1,0:T(8,128)(2,1)S(1)}, u32[]{:S(2)}, u32[]{:S(2)}) collective-permute-start(bf16[32,1024]{1,0:T(8,128)(2,1)} %bitcast.40), channel_id=1, source_target_pairs={{4,0},{6,2},{8,4},{10,6},{12,8},{14,10},{0,12},{2,14},{5,1},{7,3},... | collective-permute-start | bytes 196616 | tf_op jit(solution)/shard_map/ppermute | solution.py:313
  11.9 17.5 %collective-permute-start.3 = (bf16[2,4096]{1,0:T(2,128)(2,1)S(1)}, bf16[2,4096]{1,0:T(2,128)(2,1)S(1)}, u32[]{:S(2)}, u32[]{:S(2)}) collective-permute-start(bf16[2,4096]{1,0:T(2,128)(2,1)S(1)} %convert_bitcast_fusion), channel_id=1, source_target_pairs={{0,2},{2,0},{4,6},{6,4},{8,10},{10,8},{12,14},{14,12},{1,3},{3,1},... | collective-permute-start | bytes 49160 | tf_op jit(solution)/shard_map/ppermute | solution.py:318
  13.0 1.2 %copy-start = (bf16[1,256,2048]{2,1,0:T(8,128)(2,1)S(1)}, bf16[1,256,2048]{2,1,0:T(8,128)(2,1)}, u32[]{:S(2)}) copy-start(bf16[1,256,2048]{2,1,0:T(8,128)(2,1)} %param.4) | copy-start | bytes 3145732
  14.2 15.2 %copy-start.4 = (bf16[1,32,1024]{2,1,0:T(8,128)(2,1)S(1)}, bf16[1,32,1024]{2,1,0:T(8,128)(2,1)}, u32[]{:S(2)}) copy-start(bf16[1,32,1024]{2,1,0:T(8,128)(2,1)} %param.7) | copy-start | bytes 196612
  15.5 23.5 %all-to-all-start = ((bf16[16,128,256]{2,1,0:T(8,128)(2,1)}), bf16[16,128,256]{2,1,0:T(8,128)(2,1)S(1)}, u32[]{:S(2)}, u32[]{:S(2)}) async-start(bf16[16,128,256]{2,1,0:T(8,128)(2,1)} %shard_map.59), calls=%async_computation | async-start | bytes 2097152 | tf_op jit(solution)/shard_map/all_to_all | solution.py:317
  29.7 33.7 %collective-permute-start.12 = (bf16[128,512]{1,0:T(8,128)(2,1)S(1)}, bf16[128,512]{1,0:T(8,128)(2,1)S(1)}, u32[]{:S(2)}, u32[]{:S(2)}) collective-permute-start(bf16[128,512]{1,0:T(8,128)(2,1)S(1)} %get-tuple-element.46), channel_id=1, source_target_pairs={{0,192},{16,208},{32,224},{48,240},{64,0},{80,16},{96,32},{112,48}... | collective-permute-start | bytes 393224 | tf_op jit(solution)/shard_map/ppermute | solution.py:268
  32.8 31.5 %collective-permute-start.10 = (bf16[128,512]{1,0:T(8,128)(2,1)S(1)}, bf16[128,512]{1,0:T(8,128)(2,1)S(1)}, u32[]{:S(2)}, u32[]{:S(2)}) collective-permute-start(bf16[128,512]{1,0:T(8,128)(2,1)S(1)} %get-tuple-element.46), channel_id=1, source_target_pairs={{0,64},{16,80},{32,96},{48,112},{64,128},{80,144},{96,160},{112,17... | collective-permute-start | bytes 393224 | tf_op jit(solution)/shard_map/ppermute | solution.py:268
  32.9 18.9 %collective-permute-start.6 = (bf16[128,512]{1,0:T(8,128)(2,1)S(1)}, bf16[128,512]{1,0:T(8,128)(2,1)S(1)}, u32[]{:S(2)}, u32[]{:S(2)}) collective-permute-start(bf16[128,512]{1,0:T(8,128)(2,1)S(1)} %get-tuple-element.38), channel_id=1, source_target_pairs={{0,48},{16,0},{32,16},{48,32},{64,112},{80,64},{96,80},{112,96},{1... | collective-permute-start | bytes 393224 | tf_op jit(solution)/shard_map/ppermute | solution.py:268
  35.5 16.3 %collective-permute-start.5 = (bf16[128,512]{1,0:T(8,128)(2,1)S(1)}, bf16[128,512]{1,0:T(8,128)(2,1)S(1)}, u32[]{:S(2)}, u32[]{:S(2)}) collective-permute-start(bf16[128,512]{1,0:T(8,128)(2,1)S(1)} %get-tuple-element.38), channel_id=1, source_target_pairs={{0,32},{16,48},{32,0},{48,16},{64,96},{80,112},{96,64},{112,80},{1... | collective-permute-start | bytes 393224 | tf_op jit(solution)/shard_map/ppermute | solution.py:268
  36.4 15.4 %collective-permute-start.4 = (bf16[128,512]{1,0:T(8,128)(2,1)S(1)}, bf16[128,512]{1,0:T(8,128)(2,1)S(1)}, u32[]{:S(2)}, u32[]{:S(2)}) collective-permute-start(bf16[128,512]{1,0:T(8,128)(2,1)S(1)} %get-tuple-element.38), channel_id=1, source_target_pairs={{0,16},{16,32},{32,48},{48,0},{64,80},{80,96},{96,112},{112,64},{1... | collective-permute-start | bytes 393224 | tf_op jit(solution)/shard_map/ppermute | solution.py:268
  39.0 20.5 %all-to-all-start.1 = ((bf16[16,128,256]{2,1,0:T(8,128)(2,1)}), bf16[16,128,256]{2,1,0:T(8,128)(2,1)S(1)}, u32[]{:S(2)}, u32[]{:S(2)}) async-start(bf16[16,128,256]{2,1,0:T(8,128)(2,1)} %shard_map.60), calls=%async_computation.1 | async-start | bytes 2097152 | tf_op jit(solution)/shard_map/all_to_all | solution.py:332
  50.4 1.4 %copy-start.1 = (bf16[512,2048]{1,0:T(8,128)(2,1)}, bf16[512,2048]{1,0:T(8,128)(2,1)S(1)}, u32[]{:S(2)}) copy-start(bf16[512,2048]{1,0:T(8,128)(2,1)S(1)} %get-tuple-element.32.f_ref) | copy-start | bytes 6291460
  51.8 12.5 %collective-permute-start.11 = (bf16[128,512]{1,0:T(8,128)(2,1)S(1)}, bf16[128,512]{1,0:T(8,128)(2,1)}, u32[]{:S(2)}, u32[]{:S(2)}) collective-permute-start(bf16[128,512]{1,0:T(8,128)(2,1)S(1)} %get-tuple-element.46), channel_id=1, source_target_pairs={{0,128},{16,144},{32,160},{48,176},{64,192},{80,208},{96,224},{112... | collective-permute-start | bytes 393224 | tf_op jit(solution)/shard_map/ppermute | solution.py:268
  55.4 16.1 %collective-permute-start.9 = (bf16[4,128,512]{2,1,0:T(8,128)(2,1)S(1)}, bf16[4,128,512]{2,1,0:T(8,128)(2,1)S(1)}, u32[]{:S(2)}, u32[]{:S(2)}) collective-permute-start(bf16[4,128,512]{2,1,0:T(8,128)(2,1)S(1)} %pad_maximum_fusion.refs_0_), channel_id=1, source_target_pairs={{0,192},{16,208},{32,224},{48,240},{64,0},{80,16},{96,32},{112,48}... | collective-permute-start | bytes 1572872 | tf_op jit(solution)/shard_map/ppermute | solution.py:268
  56.6 24.7 %collective-permute-start.8 = (bf16[4,128,512]{2,1,0:T(8,128)(2,1)S(1)}, bf16[4,128,512]{2,1,0:T(8,128)(2,1)S(1)}, u32[]{:S(2)}, u32[]{:S(2)}) collective-permute-start(bf16[4,128,512]{2,1,0:T(8,128)(2,1)S(1)} %pad_maximum_fusion.refs_0_), channel_id=1, source_target_pairs={{0,128},{16,144},{32,160},{48,176},{64,192},{80,208},{96,224},{112... | collective-permute-start | bytes 1572872 | tf_op jit(solution)/shard_map/ppermute | solution.py:268
  63.4 9.6 %copy-start.3 = (bf16[128,16,128]{2,1,0:T(8,128)(2,1)}, bf16[128,16,128]{2,1,0:T(8,128)(2,1)S(1)}, u32[]{:S(2)}) copy-start(bf16[128,16,128]{2,1,0:T(8,128)(2,1)S(1)} %get-tuple-element.53) | copy-start | bytes 1572868
  63.4 18.9 %collective-permute-start.7 = (bf16[4,128,512]{2,1,0:T(8,128)(2,1)S(1)}, bf16[4,128,512]{2,1,0:T(8,128)(2,1)S(1)}, u32[]{:S(2)}, u32[]{:S(2)}) collective-permute-start(bf16[4,128,512]{2,1,0:T(8,128)(2,1)S(1)} %pad_maximum_fusion.refs_0_), channel_id=1, source_target_pairs={{0,64},{16,80},{32,96},{48,112},{64,128},{80,144},{96,160},{112,17... | collective-permute-start | bytes 1572872 | tf_op jit(solution)/shard_map/ppermute | solution.py:268
  65.3 22.1 %collective-permute-start.15 = (bf16[4,128,512]{2,1,0:T(8,128)(2,1)S(1)}, bf16[4,128,512]{2,1,0:T(8,128)(2,1)}, u32[]{:S(2)}, u32[]{:S(2)}) collective-permute-start(bf16[4,128,512]{2,1,0:T(8,128)(2,1)S(1)} %pad_maximum_fusion.1.refs_4_), channel_id=1, source_target_pairs={{0,48},{16,0},{32,16},{48,32},{64,112},{80,64},{96,80},{112,96},{1... | collective-permute-start | bytes 1572872 | tf_op jit(solution)/shard_map/ppermute | solution.py:268
  65.9 21.5 %collective-permute-start.14 = (bf16[4,128,512]{2,1,0:T(8,128)(2,1)S(1)}, bf16[4,128,512]{2,1,0:T(8,128)(2,1)}, u32[]{:S(2)}, u32[]{:S(2)}) collective-permute-start(bf16[4,128,512]{2,1,0:T(8,128)(2,1)S(1)} %pad_maximum_fusion.1.refs_4_), channel_id=1, source_target_pairs={{0,32},{16,48},{32,0},{48,16},{64,96},{80,112},{96,64},{112,80},{1... | collective-permute-start | bytes 1572872 | tf_op jit(solution)/shard_map/ppermute | solution.py:268
  71.5 20.2 %collective-permute-start.13 = (bf16[4,128,512]{2,1,0:T(8,128)(2,1)S(1)}, bf16[4,128,512]{2,1,0:T(8,128)(2,1)}, u32[]{:S(2)}, u32[]{:S(2)}) collective-permute-start(bf16[4,128,512]{2,1,0:T(8,128)(2,1)S(1)} %pad_maximum_fusion.1.refs_4_), channel_id=1, source_target_pairs={{0,16},{16,32},{32,48},{48,0},{64,80},{80,96},{96,112},{112,64},{1... | collective-permute-start | bytes 1572872 | tf_op jit(solution)/shard_map/ppermute | solution.py:268
  73.0 29.9 %all-to-all-start.2 = ((bf16[128,16,128]{2,1,0:T(8,128)(2,1)}), bf16[128,16,128]{2,1,0:T(8,128)(2,1)S(1)}, u32[]{:S(2)}, u32[]{:S(2)}) async-start(bf16[128,16,128]{2,1,0:T(8,128)(2,1)} %copy-done.3), calls=%async_computation.2 | async-start | bytes 1048576 | tf_op jit(solution)/shard_map/all_to_all | solution.py:344
  91.7 1.6 %copy-start.2 = (bf16[512,2048]{1,0:T(8,128)(2,1)S(1)}, bf16[512,2048]{1,0:T(8,128)(2,1)}, u32[]{:S(2)}) copy-start(bf16[512,2048]{1,0:T(8,128)(2,1)} %copy-done.1) | copy-start | bytes 6291460
  100.7 2.0 %collective-permute-start.16 = (bf16[4,64,1024]{2,1,0:T(8,128)(2,1)S(1)}, bf16[4,64,1024]{2,1,0:T(8,128)(2,1)S(1)}, u32[]{:S(2)}, u32[]{:S(2)}) collective-permute-start(bf16[4,64,1024]{2,1,0:T(8,128)(2,1)S(1)} %get-tuple-element.52), channel_id=1, source_target_pairs={{0,1},{1,0},{2,3},{3,2},{4,5},{5,4},{6,7},{7,6},{8,9},{9,8},{10,11... | collective-permute-start | bytes 1572872 | tf_op jit(solution)/shard_map/ppermute | solution.py:348
  102.9 8.4 %collective-permute-start.17 = (bf16[2,64,1024]{2,1,0:T(8,128)(2,1)S(1)}, bf16[2,64,1024]{2,1,0:T(8,128)(2,1)S(1)}, u32[]{:S(2)}, u32[]{:S(2)}) collective-permute-start(bf16[2,64,1024]{2,1,0:T(8,128)(2,1)S(1)} %slice.43), channel_id=1, source_target_pairs={{0,2},{2,0},{4,6},{6,4},{8,10},{10,8},{12,14},{14,12},{1,3},{3,1},... | collective-permute-start | bytes 786440 | tf_op jit(solution)/shard_map/ppermute | solution.py:350
